TPU v7x, 256 devices: a whole 4x4x8 slice. The times are simulated.
256 devices in a mesh: query: 16 (over x_lo, z), head: 16 (over y, x_hi, core).
Axes of the slice: x: 4 (x_hi: 2, x_lo: 2; x = x_hi * 2 + x_lo), y: 4, z: 8, core: 2. Of those that a mesh axis runs over, the one named last changes fastest.
Arguments:
- queries: bfloat16 [16384, 4096], P('query', 'head'), may hold values from -12 to 12
- mem_keys: bfloat16 [2048, 4096], P('head'), may hold values from -6 to 6
- mem_values: bfloat16 [2048, 4096], P('head'), may hold values from -6 to 6
- grad_out: bfloat16 [16384, 4096], P('query', 'head'), may hold values from -3 to 3
Outputs:
- attended: bfloat16 [16384, 4096], P('query', 'head')
- query_gradients: bfloat16 [16384, 4096], P('query', 'head')
- grad_keys: bfloat16 [2048, 4096], P(('query', 'head'))
- grad_values: bfloat16 [2048, 4096], P(('query', 'head'))
All inputs are finite; a program needn't handle non-finite values.
Results may differ from a plain program's by a relative error of at most 0.025.
Values may be sent and summed in bfloat16 or wider, within the bound.
No kernel may reach another device: no remote copies, remote signals or barrier semaphores. Data moves between devices by JAX's collectives and lax.ppermute only.
A program may use at most 64 MiB of HBM per device.

v0:
```python
import jax
import jax.numpy as jnp
from jax import lax
from jax.sharding import PartitionSpec as P

HEAD_DIM = 256


def per_device(queries, mem_keys, mem_values, grad_out):
    head_group = lax.axis_size("head")
    query_group = lax.axis_size("query")
    mem_rows, full_width = mem_keys.shape
    query_row_count, local_width = queries.shape
    local_heads = local_width // HEAD_DIM
    score_scale = HEAD_DIM ** (-0.5)
    split_keys = mem_keys.reshape(mem_rows, head_group, local_width)
    split_values = mem_values.reshape(mem_rows, head_group, local_width)
    local_key_block, local_value_block = (
        lax.all_to_all(split_keys, "head", split_axis=1, concat_axis=0, tiled=True),
        lax.all_to_all(split_values, "head", split_axis=1, concat_axis=0, tiled=True),
    )
    total_memory = mem_rows * head_group
    block_rows = 512
    block_count = query_row_count // block_rows
    query_blocks = queries.reshape(block_count, block_rows, local_heads, HEAD_DIM)
    cotan_blocks = grad_out.reshape(block_count, block_rows, local_heads, HEAD_DIM)

    def step(totals, pieces):
        key_total, value_total = totals
        query_tile, output_gradient_block = pieces
        scores = (
            jnp.einsum(
                "jlv,elv->lje", query_tile, local_key_block, preferred_element_type=jnp.float32
            )
            * score_scale
        )
        row_top = jnp.max(scores, axis=-1, keepdims=True)
        weights = jnp.exp(scores - row_top)
        attention_probabilities = (weights / jnp.sum(weights, axis=-1, keepdims=True)).astype(
            jnp.bfloat16
        )
        attended = jnp.einsum(
            "ijt,tia->jia",
            attention_probabilities,
            local_value_block,
            preferred_element_type=jnp.float32,
        ).astype(jnp.bfloat16)
        dprobs = jnp.einsum(
            "jlv,elv->lje",
            output_gradient_block,
            local_value_block,
            preferred_element_type=jnp.float32,
        )
        row_delta = jnp.sum(
            attention_probabilities.astype(jnp.float32) * dprobs, axis=-1, keepdims=True
        )
        score_gradients = (
            attention_probabilities.astype(jnp.float32) * (dprobs - row_delta) * score_scale
        ).astype(jnp.bfloat16)
        grad_query = jnp.einsum(
            "ijt,tia->jia", score_gradients, local_key_block, preferred_element_type=jnp.float32
        ).astype(jnp.bfloat16)
        key_total = key_total + jnp.einsum(
            "gqv,qgw->vgw", score_gradients, query_tile, preferred_element_type=jnp.float32
        )
        value_total = value_total + jnp.einsum(
            "gqv,qgw->vgw",
            attention_probabilities,
            output_gradient_block,
            preferred_element_type=jnp.float32,
        )
        return ((key_total, value_total), (attended, grad_query))

    empty = jnp.zeros((total_memory, local_heads, HEAD_DIM), jnp.float32)
    (key_total, value_total), (attended, query_gradients) = lax.scan(
        step, (empty, empty), (query_blocks, cotan_blocks)
    )
    attended = attended.reshape(query_row_count, local_width)
    query_gradients = query_gradients.reshape(query_row_count, local_width)
    share_rows = total_memory // (query_group * head_group)
    key_parts = key_total.reshape(query_group, head_group, share_rows, local_width)
    value_parts = value_total.reshape(query_group, head_group, share_rows, local_width)
    key_moved, value_moved = (
        lax.all_to_all(
            key_parts.astype(jnp.bfloat16), "head", split_axis=1, concat_axis=3, tiled=True
        ).astype(key_parts.dtype),
        lax.all_to_all(
            value_parts.astype(jnp.bfloat16), "head", split_axis=1, concat_axis=3, tiled=True
        ).astype(value_parts.dtype),
    )
    key_sum, value_sum = (
        lax.psum_scatter(
            key_moved.astype(jnp.bfloat16), "query", scatter_dimension=0, tiled=True
        ).astype(jnp.float32),
        lax.psum_scatter(
            value_moved.astype(jnp.bfloat16), "query", scatter_dimension=0, tiled=True
        ).astype(jnp.float32),
    )
    grad_keys = key_sum.astype(jnp.bfloat16)
    grad_values = value_sum.astype(jnp.bfloat16)
    grad_keys = grad_keys.reshape(share_rows, full_width)
    grad_values = grad_values.reshape(share_rows, full_width)
    return (attended, query_gradients, grad_keys, grad_values)


def solution(mesh):
    in_specs = (P("query", "head"), P("head", None), P("head", None), P("query", "head"))
    out_specs = (
        P("query", "head"),
        P("query", "head"),
        P(("query", "head"), None),
        P(("query", "head"), None),
    )
    return jax.shard_map(
        per_device, mesh=mesh, in_specs=in_specs, out_specs=out_specs, check_vma=False
    )
```

profile of v0, /device:TPU:32, one launch (start us, length us, event | category | flops | bytes accessed | tf_op | source)
XLA Modules:
  0.0 258.5 jit_solution(97790399324316005)
XLA Ops:
  7.2 2.4 copy.36
  9.5 7.0 %all-to-all-start.1 = ((bf16[128,16,256]{0,2,1:T(8,128)(2,1)}), bf16[128,16,256]{0,2,1:T(8,128)(2,1)S(1)}, u32[]{:S(2)}, u32[]{:S(2)}) async-start(bf16[128,16,256]{0,2,1:T(8,128)(2,1)} %bitcast.8), calls=%async_computation.1 | async-start | bytes 2097152 | tf_op jit(solution)/shard_map/all_to_all | solution.py:20
  16.6 1.3 copy.34
  17.9 16.7 %all-to-all-done.1 = bf16[128,16,256]{0,2,1:T(8,128)(2,1)S(1)} async-done(((bf16[128,16,256]{0,2,1:T(8,128)(2,1)}), bf16[128,16,256]{0,2,1:T(8,128)(2,1)S(1)}, u32[]{:S(2)}, u32[]{:S(2)}) %all-to-all-start.1) | async-done | bytes 1048608 | tf_op jit(solution)/shard_map/all_to_all | solution.py:20
  34.6 3.7 %all-to-all-start = ((bf16[128,16,256]{0,2,1:T(8,128)(2,1)}), bf16[128,16,256]{0,2,1:T(8,128)(2,1)S(1)}, u32[]{:S(2)}, u32[]{:S(2)}) async-start(bf16[128,16,256]{0,2,1:T(8,128)(2,1)} %bitcast.2), calls=%async_computation | async-start | bytes 2097152 | tf_op jit(solution)/shard_map/all_to_all | solution.py:19
  38.3 1.3 copy.37
  39.7 16.6 %all-to-all-done = bf16[128,16,256]{0,2,1:T(8,128)(2,1)S(1)} async-done(((bf16[128,16,256]{0,2,1:T(8,128)(2,1)}), bf16[128,16,256]{0,2,1:T(8,128)(2,1)S(1)}, u32[]{:S(2)}, u32[]{:S(2)}) %all-to-all-start) | async-done | bytes 1048608 | tf_op jit(solution)/shard_map/all_to_all | solution.py:19
  56.8 33.1 %while.17 = (s32[]{:T(128)}, f32[2048,1,256]{0,2,1:T(8,128)}, f32[2048,1,256]{0,2,1:T(8,128)}, bf16[2,512,1,256]{3,1,2,0:T(8,128)(2,1)}, bf16[2,512,1,256]{3,1,2...) while((s32[]{:T(128)}, f32[2048,1,256]{0,2,1:T(8,128)}, ...), condition=%wide.region_4.5_spmd.clone, body=%wide.region_0.4_spmd.clone.sunk | while | flops 3241409024 | bytes 74989384 | solution.py:75
  56.8 1.8 multiply_reduce_fusion.2
  58.6 0.8 fusion.55
  60.0 1.7 fusion.56
  61.7 2.0 fusion.57
  63.8 3.9 %fusion.58 = f32[2048,1,256]{0,2,1:T(8,128)} fusion(bf16[512,2048]{1,0:T(8,128)(2,1)} %fusion.57, f32[2048,1,256]{0,2,1:T(8,128)} %get-tuple-element.224, pred[]{:T(512)S(6)} %compare.3, bf16[2,512,1,256]{3,1,2,0:T(8,128)(2,1)} %get-tuple-element.239, s32[]{:T(128)} %get-tuple-element.223), kind=kOutput, calls=%fused_computation.11.clone.1 | convolution fusion | flops 537919488 | bytes 6554113 | tf_op jit(solution)/shard_map/while/body/eval_jaxpr/gqv,qgw->vgw/dot_general | solution.py:63
  67.7 0.7 fusion.61
  68.7 2.1 fusion.59
  70.8 1.4 fusion.60
  72.2 1.8 multiply_reduce_fusion.2
  74.0 0.8 fusion.55
  75.4 1.7 fusion.56
  77.1 2.0 fusion.57
  79.1 4.5 %fusion.58 = f32[2048,1,256]{0,2,1:T(8,128)} fusion(bf16[512,2048]{1,0:T(8,128)(2,1)} %fusion.57, f32[2048,1,256]{0,2,1:T(8,128)} %get-tuple-element.224, pred[]{:T(512)S(6)} %compare.3, bf16[2,512,1,256]{3,1,2,0:T(8,128)(2,1)} %get-tuple-element.239, s32[]{:T(128)} %get-tuple-element.223), kind=kOutput, calls=%fused_computation.11.clone.1 | convolution fusion | flops 537919488 | bytes 6554113 | tf_op jit(solution)/shard_map/while/body/eval_jaxpr/gqv,qgw->vgw/dot_general | solution.py:63
  83.7 0.7 fusion.61
  84.7 3.7 %fusion.59 = f32[2048,1,256]{0,2,1:T(8,128)} fusion(bf16[512,2048]{1,0:T(8,128)(2,1)S(1)} %get-tuple-element.209, f32[2048,1,256]{0,2,1:T(8,128)} %get-tuple-element.225, pred[]{:T(512)S(6)} %compare.3, bf16[2,512,1,256]{3,1,2,0:T(8,128)(2,1)S(1)} %copy-done.2, s32[]{:T(128)} %get-tuple-element.223), kind=kOutput, calls=%fused_computation.12.clone.1 | convolution fusion | flops 537919488 | bytes 6553605 | tf_op jit(solution)/shard_map/while/body/eval_jaxpr/gqv,qgw->vgw/dot_general | solution.py:66
  88.5 1.4 fusion.60
  89.9 1.8 copy.40
  91.8 20.6 %all_to_all.72 = bf16[16,16,8,256]{3,2,0,1:T(8,128)(2,1)S(1)} all-to-all(bf16[16,16,8,256]{3,2,0,1:T(8,128)(2,1)S(1)} %copy.41), channel_id=1, replica_groups=mesh['query'=16,'head'=16] {'head'}, dimensions={1} | all-to-all | bytes 2097152 | tf_op jit(solution)/shard_map/all_to_all | solution.py:84
  112.4 1.1 copy.46
  113.5 1.8 copy.43
  115.4 20.6 %all_to_all.73 = bf16[16,16,8,256]{3,2,0,1:T(8,128)(2,1)S(1)} all-to-all(bf16[16,16,8,256]{3,2,0,1:T(8,128)(2,1)S(1)} %copy.44), channel_id=1, replica_groups=mesh['query'=16,'head'=16] {'head'}, dimensions={1} | all-to-all | bytes 2097152 | tf_op jit(solution)/shard_map/all_to_all | solution.py:87
  136.0 1.1 copy.47
  137.2 43.6 %reduce-scatter.3.cloned.1.call-done = bf16[1,1,8,4096]{3,2,0,1:T(8,128)(2,1)} async-done(((bf16[16,1,8,4096]{3,2,0,1:T(8,128)(2,1)}), bf16[1,1,8,4096]{3,2,0,1:T(8,128)(2,1)}) %reduce-scatter.3.cloned.1.call-update) | async-done | bytes 65552 | tf_op jit(solution)/shard_map/reduce_scatter | solution.py:92
  180.8 70.9 %reduce-scatter.5.cloned.1.call-done = bf16[1,1,8,4096]{3,2,0,1:T(8,128)(2,1)} async-done(((bf16[16,1,8,4096]{3,2,0,1:T(8,128)(2,1)}), bf16[1,1,8,4096]{3,2,0,1:T(8,128)(2,1)}) %reduce-scatter.5.cloned.1.call-update) | async-done | bytes 65552 | tf_op jit(solution)/shard_map/reduce_scatter | solution.py:95
  (41 shorter events, 2.6 us)
Async XLA Ops:
  7.2 9.4 %copy-start.3 = (bf16[128,4096]{1,0:T(8,128)(2,1)S(1)}, bf16[128,4096]{1,0:T(8,128)(2,1)}, u32[]{:S(2)}) copy-start(bf16[128,4096]{1,0:T(8,128)(2,1)} %param.7) | copy-start | bytes 3145732
  9.5 25.1 %all-to-all-start.1 = ((bf16[128,16,256]{0,2,1:T(8,128)(2,1)}), bf16[128,16,256]{0,2,1:T(8,128)(2,1)S(1)}, u32[]{:S(2)}, u32[]{:S(2)}) async-start(bf16[128,16,256]{0,2,1:T(8,128)(2,1)} %bitcast.8), calls=%async_computation.1 | async-start | bytes 2097152 | tf_op jit(solution)/shard_map/all_to_all | solution.py:20
  34.6 21.6 %all-to-all-start = ((bf16[128,16,256]{0,2,1:T(8,128)(2,1)}), bf16[128,16,256]{0,2,1:T(8,128)(2,1)S(1)}, u32[]{:S(2)}, u32[]{:S(2)}) async-start(bf16[128,16,256]{0,2,1:T(8,128)(2,1)} %bitcast.2), calls=%async_computation | async-start | bytes 2097152 | tf_op jit(solution)/shard_map/all_to_all | solution.py:19
  38.3 142.5 %reduce-scatter.3.cloned.1.call-start = ((), (), s32[]{:S(2)}) async-start(), calls=%async_computation.6 | async-start | bytes 1114112 | tf_op jit(solution)/shard_map/reduce_scatter | solution.py:92
  58.6 1.0 copy-start.1
  58.6 1.4 copy-start.4
  63.7 3.9 %copy-start = (bf16[512,2048]{1,0:T(8,128)(2,1)S(1)}, bf16[512,2048]{1,0:T(8,128)(2,1)}, u32[]{:S(2)}) copy-start(bf16[512,2048]{1,0:T(8,128)(2,1)} %fusion.57) | copy-start | bytes 6291460 | tf_op jit(solution)/shard_map/while
  63.8 3.9 %copy-start.6 = (bf16[2,512,1,256]{3,1,2,0:T(8,128)(2,1)S(1)}, bf16[2,512,1,256]{3,1,2,0:T(8,128)(2,1)}, u32[]{:S(2)}) copy-start(bf16[2,512,1,256]{3,1,2,0:T(8,128)(2,1)} %get-tuple-element.227) | copy-start | bytes 1572868 | tf_op jit(solution)/shard_map/while
  67.7 1.0 copy-start.2
  68.4 2.4 copy-start.7
  68.7 2.1 copy-start.5
  74.0 1.0 copy-start.1
  74.0 1.4 copy-start.4
  79.1 4.5 %copy-start = (bf16[512,2048]{1,0:T(8,128)(2,1)S(1)}, bf16[512,2048]{1,0:T(8,128)(2,1)}, u32[]{:S(2)}) copy-start(bf16[512,2048]{1,0:T(8,128)(2,1)} %fusion.57) | copy-start | bytes 6291460 | tf_op jit(solution)/shard_map/while
  79.1 4.5 %copy-start.6 = (bf16[2,512,1,256]{3,1,2,0:T(8,128)(2,1)S(1)}, bf16[2,512,1,256]{3,1,2,0:T(8,128)(2,1)}, u32[]{:S(2)}) copy-start(bf16[2,512,1,256]{3,1,2,0:T(8,128)(2,1)} %get-tuple-element.227) | copy-start | bytes 1572868 | tf_op jit(solution)/shard_map/while
  83.7 1.0 copy-start.2
  84.4 4.0 %copy-start.7 = (bf16[2,512,1,256]{3,1,2,0:T(8,128)(2,1)}, bf16[2,512,1,256]{3,1,2,0:T(8,128)(2,1)S(1)}, u32[]{:S(2)}) copy-start(bf16[2,512,1,256]{3,1,2,0:T(8,128)(2,1)S(1)} %fusion.61) | copy-start | bytes 1572868 | tf_op jit(solution)/shard_map/while
  84.7 3.7 %copy-start.5 = (bf16[2048,1,256]{2,0,1:T(8,128)(2,1)S(1)}, bf16[2048,1,256]{2,0,1:T(8,128)(2,1)}, u32[]{:S(2)}) copy-start(bf16[2048,1,256]{2,0,1:T(8,128)(2,1)} %get-tuple-element.242) | copy-start | bytes 3145732 | tf_op jit(solution)/shard_map/while
  113.5 138.2 %reduce-scatter.5.cloned.1.call-start = ((), (), s32[]{:S(2)}) async-start(), calls=%async_computation.7 | async-start | bytes 1114112 | tf_op jit(solution)/shard_map/reduce_scatter | solution.py:95
Sparse Core Ops, SparseCore 0:
  113.6 67.1 reduce-scatter.2
  184.0 67.5 reduce-scatter.4
where the time goes:
time: 262 us; the launch traced here: 258 us
  waiting for transfers between devices  148 us (56%)
  blocking collectives  41.2 us (16%)
  matrix products  25.5 us (10%)
  between operations  14.1 us (5%)
  local copies, waits for them, and re-layouts  13.2 us (5%)
  starting transfers between devices  10.8 us (4%)
  other arithmetic  5.74 us (2%)
    reduce_scatter x1, waiting for transfers between devices, per_device(): lax.psum_scatter(value_moved.astype(jnp.bfloat16), 'query', scatter_dimen...  70.9 us
    reduce_scatter x1, waiting for transfers between devices, per_device(): lax.psum_scatter(key_moved.astype(jnp.bfloat16), 'query', scatter_dimensi...  43.6 us
    all_to_all x1, blocking collectives, per_device(): lax.all_to_all(key_parts.astype(jnp.bfloat16), 'head', split_axis=1, conc...  20.6 us
    all_to_all x1, blocking collectives, per_device(): lax.all_to_all(value_parts.astype(jnp.bfloat16), 'head', split_axis=1, co...  20.6 us
    all_to_all x1, waiting for transfers between devices, per_device(): lax.all_to_all(split_values, 'head', split_axis=1, concat_axis=0, tiled=T...  16.7 us
    all_to_all x1, waiting for transfers between devices, per_device(): lax.all_to_all(split_keys, 'head', split_axis=1, concat_axis=0, tiled=True)  16.6 us
    dot_general x2, matrix products, step(): jnp.einsum('gqv,qgw->vgw', score_gradients, query_tile, preferred_element...  8.45 us
    all_to_all x1, starting transfers between devices, per_device(): lax.all_to_all(split_values, 'head', split_axis=1, concat_axis=0, tiled=T...  7.03 us
  transfers between devices with their start and end apart: 4, of which 4 were waited for; matrix products, arithmetic and copies ran while one was open for 2% of the time, Pallas kernels for 0%

commit v1 on v0

v1 whole, which is shorter than its diff:
```python
import functools
import itertools

import jax
import jax.numpy as jnp
from jax import lax
from jax.experimental import pallas as pl
from jax.experimental.pallas import tpu as pltpu
from jax.sharding import PartitionSpec as P

HEAD_DIM = 256
AXES = ("query", "head")
X_LO, Z, Y, X_HI, CORE = 2, 8, 4, 2, 2
TILE = 256
LOG2E = 1.4426950408889634


def device(xl, z, y, xh, c):
    return (xl * Z + z) * (Y * X_HI * CORE) + (y * X_HI + xh) * CORE + c


def permute(array, to):
    pairs = [
        (device(*at), device(*to(*at)))
        for at in itertools.product(range(X_LO), range(Z), range(Y), range(X_HI), range(CORE))
    ]
    return lax.ppermute(array, AXES, pairs)


def exchange(array, groups):
    return lax.all_to_all(
        array, AXES, split_axis=0, concat_axis=0, axis_index_groups=groups, tiled=True
    )


def swap_core_and_x_lo(xl, z, y, xh, c):
    return (c, z, y, xh, xl)


def other_core(xl, z, y, xh, c):
    return (xl, z, y, xh, 1 - c)


def head_groups():
    return [
        [device(xl, z, y, xh, c) for y in range(Y) for xh in range(X_HI)]
        for xl in range(X_LO)
        for z in range(Z)
        for c in range(CORE)
    ]


def z_groups():
    return [
        [device(xl, z, y, xh, c) for z in range(Z)]
        for xl in range(X_LO)
        for y in range(Y)
        for xh in range(X_HI)
        for c in range(CORE)
    ]


def column_groups():
    return [
        [device(xl, z, y, xh, c) for y in range(Y) for xh in range(X_HI) for xl in range(X_LO)]
        for z in range(Z)
        for c in range(CORE)
    ]


def pack_kernel(xl_ref, keys, values, out):
    out[0, 0] = keys[...]
    out[0, 1] = values[...]


def pack(xl, keys, values):
    rows = keys.shape[0]
    column = pl.BlockSpec((rows, HEAD_DIM), lambda chip, xl_ref: (0, chip * 2 + xl_ref[0]))
    return pl.pallas_call(
        pack_kernel,
        out_shape=jax.ShapeDtypeStruct((Y * X_HI, 2, rows, HEAD_DIM), keys.dtype),
        grid_spec=pltpu.PrefetchScalarGridSpec(
            num_scalar_prefetch=1,
            grid=(Y * X_HI,),
            in_specs=[column, column],
            out_specs=pl.BlockSpec((1, 2, rows, HEAD_DIM), lambda chip, xl_ref: (chip, 0, 0, 0)),
        ),
        name="pack",
    )(xl, keys, values)


def nt(a, b):
    return lax.dot_general(a, b, (((1,), (1,)), ((), ())), preferred_element_type=jnp.float32)


def nn(a, b):
    return jnp.dot(a, b, preferred_element_type=jnp.float32)


def attention_kernel(
    core_ref, q_ref, do_ref, own_ref, other_ref,
    att_ref, dq_ref, keep_ref, send_ref,
    k_ref, v_ref, kt_ref, vt_ref, s_ref, e_ref, dk_ref, dv_ref,
):
    core = core_ref[0]
    step = pl.program_id(0)
    memory = k_ref.shape[0]
    block = own_ref.shape[2]
    chunk = 256

    @pl.when(step == 0)
    def _():
        for chip in range(Y * X_HI):
            for source, at in ((own_ref, core), (other_ref, 1 - core)):
                rows = pl.ds(pl.multiple_of((chip * 2 + at) * block, block), block)
                k_ref[rows, :] = source[chip, 0]
                v_ref[rows, :] = source[chip, 1]
        for i in range(memory // chunk):
            rows = pl.ds(i * chunk, chunk)
            kt_ref[:, rows] = k_ref[rows, :].T
            vt_ref[:, rows] = v_ref[rows, :].T
        dk_ref[...] = jnp.zeros_like(dk_ref)
        dv_ref[...] = jnp.zeros_like(dv_ref)

    q = q_ref[...]
    do = do_ref[...]
    top = None
    for i in range(memory // chunk):
        rows = pl.ds(i * chunk, chunk)
        s = nt(k_ref[rows, :], q)
        s_ref[rows, :] = s
        here = jnp.max(s, axis=0, keepdims=True)
        top = here if top is None else jnp.maximum(top, here)
    factor = LOG2E * HEAD_DIM ** (-0.5)
    top = top * factor
    total = None
    att = None
    for i in range(memory // chunk):
        rows = pl.ds(i * chunk, chunk)
        e = jnp.exp2(s_ref[rows, :] * factor - top)
        here = jnp.sum(e, axis=0, keepdims=True)
        total = here if total is None else total + here
        eb = e.astype(jnp.bfloat16)
        e_ref[rows, :] = eb
        part = nn(vt_ref[:, rows], eb)
        att = part if att is None else att + part
    inverse = 1.0 / total
    att = att * inverse
    att_ref[...] = att.T.astype(jnp.bfloat16)
    dot = (do.astype(jnp.float32).T * inverse).astype(jnp.bfloat16)
    delta = jnp.sum(att * dot.astype(jnp.float32), axis=0, keepdims=True)
    dos = dot.T
    dq = None
    for i in range(memory // chunk):
        rows = pl.ds(i * chunk, chunk)
        dp = nn(v_ref[rows, :], dot)
        eb = e_ref[rows, :]
        ds = (eb.astype(jnp.float32) * (dp - delta)).astype(jnp.bfloat16)
        dv_ref[rows, :] += nn(eb, dos)
        dk_ref[rows, :] += nn(ds, q)
        part = nn(kt_ref[:, rows], ds)
        dq = part if dq is None else dq + part
    scale = HEAD_DIM ** (-0.5)
    dq_ref[...] = (dq * scale).T.astype(jnp.bfloat16)

    @pl.when(step == pl.num_programs(0) - 1)
    def _():
        for kind, (source, factor) in enumerate(((dk_ref, scale), (dv_ref, 1.0))):
            for xl in range(X_LO):
                for z in range(Z):
                    rows = pl.ds((xl * Z + z) * 128, 128)
                    full = source[rows, :].reshape(8, 2, 8, HEAD_DIM)
                    low = full[:, 0].reshape(64, HEAD_DIM) * factor
                    high = full[:, 1].reshape(64, HEAD_DIM) * factor
                    first = core == 0
                    at = pl.ds(xl * 64, 64)
                    keep_ref[z, kind, at, :] = jnp.where(first, low, high).astype(jnp.bfloat16)
                    send_ref[z, kind, at, :] = jnp.where(first, high, low).astype(jnp.bfloat16)


def attention(core, q, do, own, other):
    rows = q.shape[0]
    memory = 2 * own.shape[0] * own.shape[2]
    whole = lambda shape: pl.BlockSpec(shape, lambda i: (0,) * len(shape), memory_space=pltpu.VMEM)
    tile = pl.BlockSpec((TILE, HEAD_DIM), lambda i: (i, 0))
    parts = (Z, 2, memory // (2 * Z), HEAD_DIM)
    bf16, f32 = jnp.bfloat16, jnp.float32
    return pl.pallas_call(
        attention_kernel,
        grid=(rows // TILE,),
        out_shape=(
            jax.ShapeDtypeStruct((rows, HEAD_DIM), bf16),
            jax.ShapeDtypeStruct((rows, HEAD_DIM), bf16),
            jax.ShapeDtypeStruct(parts, bf16),
            jax.ShapeDtypeStruct(parts, bf16),
        ),
        in_specs=[
            pl.BlockSpec(memory_space=pltpu.SMEM),
            tile,
            tile,
            whole(own.shape),
            whole(other.shape),
        ],
        out_specs=(tile, tile, whole(parts), whole(parts)),
        scratch_shapes=[
            pltpu.VMEM((memory, HEAD_DIM), bf16),
            pltpu.VMEM((memory, HEAD_DIM), bf16),
            pltpu.VMEM((HEAD_DIM, memory), bf16),
            pltpu.VMEM((HEAD_DIM, memory), bf16),
            pltpu.VMEM((memory, TILE), f32),
            pltpu.VMEM((memory, TILE), bf16),
            pltpu.VMEM((memory, HEAD_DIM), f32),
            pltpu.VMEM((memory, HEAD_DIM), f32),
        ],
        compiler_params=pltpu.CompilerParams(
            dimension_semantics=("arbitrary",), vmem_limit_bytes=40 * 1024 * 1024
        ),
        cost_estimate=pl.CostEstimate(
            flops=12 * rows * memory * HEAD_DIM,
            bytes_accessed=8 * 1024 * 1024,
            transcendentals=rows * memory,
        ),
        name="attention",
    )(core, q, do, own, other)


def per_device(queries, mem_keys, mem_values, grad_out):
    xl = lax.axis_index("query") // Z
    core = lax.axis_index("head") % CORE
    as_ref = lambda value: jnp.reshape(value, (1,)).astype(jnp.int32)
    q = permute(queries, swap_core_and_x_lo)
    do = permute(grad_out, swap_core_and_x_lo)
    own = exchange(pack(as_ref(xl), mem_keys, mem_values), head_groups())
    other = permute(own, other_core)
    att, dq, keep, send = attention(as_ref(core), q, do, own, other)
    attended = permute(att, swap_core_and_x_lo)
    query_gradients = permute(dq, swap_core_and_x_lo)
    came = permute(send, other_core)
    chip_sum = (keep.astype(jnp.float32) + came.astype(jnp.float32)).astype(jnp.bfloat16)
    parts = exchange(chip_sum, z_groups())
    sums = jnp.sum(parts.astype(jnp.float32), axis=0).astype(jnp.bfloat16)
    sums = sums.reshape(2, X_LO, Y * X_HI, 8, HEAD_DIM).transpose(2, 1, 0, 3, 4)
    sums = sums.reshape(Y * X_HI * X_LO, 16, HEAD_DIM)
    final = exchange(sums, column_groups()).reshape(16, 2, 8, HEAD_DIM).transpose(1, 2, 0, 3)
    final = final.reshape(2, 8, 16 * HEAD_DIM)
    return attended, query_gradients, final[0], final[1]


def solution(mesh):
    in_specs = (P("query", "head"), P("head", None), P("head", None), P("query", "head"))
    out_specs = (
        P("query", "head"),
        P("query", "head"),
        P(("query", "head"), None),
        P(("query", "head"), None),
    )
    return jax.shard_map(
        per_device, mesh=mesh, in_specs=in_specs, out_specs=out_specs, check_vma=False
    )
```

time: 262 us -> 119 us (0.45)
  waiting for transfers between devices: 148 us -> 36.6 us
  matrix products: 25.5 us -> 0 us
  starting transfers between devices: 10.8 us -> 30.4 us
  Pallas kernels: 0 us -> 18.4 us
  blocking collectives: 41.2 us -> 24.1 us
  between operations: 14.1 us -> 0.72 us
  local copies, waits for them, and re-layouts: 13.2 us -> 5.54 us
  other arithmetic: 5.74 us -> 1.44 us
    reduce_scatter x2 -> x0, waiting for transfers between devices: 114 us -> none  [the longest x1 70.9 us: per_device(): lax.psum_scatter(value_moved.astype(jnp.bfloat16), 'query', scatter_dimen...]
    dot_general x12 -> x0, matrix products: 25.5 us -> none  [the longest x2 8.45 us: step(): jnp.einsum('gqv,qgw->vgw', score_gradients, query_tile, preferred_element...]
    pallas_call x0 -> x2, Pallas kernels: none -> 18.4 us  [the longest x1 13.3 us: attention(): pl.pallas_call(attention_kernel, grid=(rows // TILE,), out_shape=(jax.Sha...]
    ppermute x0 -> x6, starting transfers between devices: none -> 18.2 us  [permute(): return lax.ppermute(array, AXES, pairs)]
    all_to_all x2 -> x1, blocking collectives: 41.2 us -> 24.1 us  [exchange(): lax.all_to_all(array, AXES, split_axis=0, concat_axis=0, axis_index_group...]
    while x30 -> x0, local copies, waits for them, and re-layouts: 5.28 us -> none  [the longest x2 3.53 us: per_device(): lax.scan(step, (empty, empty), (query_blocks, cotan_blocks))]
    all_to_all x4 -> x0, local copies, waits for them, and re-layouts: 4.08 us -> none  [the longest x1 1.33 us: per_device(): lax.all_to_all(split_values, 'head', split_axis=1, concat_axis=0, tiled=T...]
    convert_element_type x2 -> x1, other arithmetic: 4.1 us -> 1.3 us  [per_device(): (keep.astype(jnp.float32) + came.astype(jnp.float32)).astype(jnp.bfloat16)]
  transfers between devices with their start and end apart: 4 -> 8, of which waited for: 4 -> 3; matrix products, arithmetic and copies ran while one was open for 2% -> 1% of each run, Pallas kernels for 0% -> 0%
where the time goes in v1:
time: 119 us; the launch traced here: 117 us
  waiting for transfers between devices  36.6 us (31%)
  starting transfers between devices  30.4 us (26%)
  blocking collectives  24.1 us (20%)
  Pallas kernels  18.4 us (15%)
  local copies, waits for them, and re-layouts  5.54 us (5%)
  other arithmetic  1.44 us (1%)
    all_to_all x2, waiting for transfers between devices, exchange(): lax.all_to_all(array, AXES, split_axis=0, concat_axis=0, axis_index_group...  34.3 us
    all_to_all x1, blocking collectives, exchange(): lax.all_to_all(array, AXES, split_axis=0, concat_axis=0, axis_index_group...  24.1 us
    ppermute x6, starting transfers between devices, permute(): return lax.ppermute(array, AXES, pairs)  18.2 us
    pallas_call x1, Pallas kernels, attention(): pl.pallas_call(attention_kernel, grid=(rows // TILE,), out_shape=(jax.Sha...  13.3 us
    all_to_all x2, starting transfers between devices, exchange(): lax.all_to_all(array, AXES, split_axis=0, concat_axis=0, axis_index_group...  12.2 us
    pallas_call x1, Pallas kernels, pack(): pl.pallas_call(pack_kernel, out_shape=jax.ShapeDtypeStruct((Y * X_HI, 2,...  5.05 us
    unnamed x10, local copies, waits for them, and re-layouts  4.21 us
  transfers between devices with their start and end apart: 8, of which 3 were waited for; matrix products, arithmetic and copies ran while one was open for 1% of the time, Pallas kernels for 0%

profile of v1, /device:TPU:32, one launch (start us, length us, event | category | flops | bytes accessed | tf_op | source)
XLA Modules:
  0.0 117.3 jit_solution(3828667212376550142)
XLA Ops:
  0.6 5.0 %pack.1 = bf16[8,2,128,256]{3,2,1,0:T(8,128)(2,1)} custom-call(s32[1]{0:T(128)} %bitcast.1.xl_ref, bf16[128,4096]{1,0:T(8,128)(2,1)} %keys.1, bf16[128,4096]{1,0:T(8,128)(2,1)} %values.1), custom_call_target="tpu_custom_call" | custom-call | tf_op jit(solution)/shard_map/pack/pallas_call | solution.py:79
  5.7 24.1 %all_to_all.15.own_ref = bf16[8,2,128,256]{3,2,1,0:T(8,128)(2,1)S(1)} all-to-all(bf16[8,2,128,256]{3,2,1,0:T(8,128)(2,1)} %pack.1), channel_id=1, replica_groups={{0,2,4,6,8,10,12,14},{1,3,5,7,9,11,13,15},{16,18,20,22,24,26,28,30},{17..., dimensions={0} | all-to-all | bytes 2097152 | tf_op jit(solution)/shard_map/all_to_all | solution.py:31
  29.8 0.0 collective-permute-start.2
  29.8 1.7 %collective-permute-start = (bf16[1024,256]{1,0:T(8,128)(2,1)}, bf16[1024,256]{1,0:T(8,128)(2,1)S(1)}, u32[]{:S(2)}, u32[]{:S(2)}) collective-permute-start(bf16[1024,256]{1,0:T(8,128)(2,1)} %param.4), channel_id=1, source_target_pairs={{0,0},{1,128},{2,2},{3,130},{4,4},{5,132},{6,6},{7,134},{8,8},{9,1... | collective-permute-start | bytes 1572872 | tf_op jit(solution)/shard_map/ppermute | solution.py:27
  31.5 1.7 %collective-permute-start.1 = (bf16[1024,256]{1,0:T(8,128)(2,1)}, bf16[1024,256]{1,0:T(8,128)(2,1)S(1)}, u32[]{:S(2)}, u32[]{:S(2)}) collective-permute-start(bf16[1024,256]{1,0:T(8,128)(2,1)} %param.7), channel_id=1, source_target_pairs={{0,0},{1,128},{2,2},{3,130},{4,4},{5,132},{6,6},{7,134},{8,8},{9,1... | collective-permute-start | bytes 1572872 | tf_op jit(solution)/shard_map/ppermute | solution.py:27
  33.2 0.0 collective-permute-done.q_ref
  33.2 0.0 collective-permute-done.1.do_ref
  33.2 0.0 copy-start
  33.2 0.8 copy-done
  34.0 0.0 collective-permute-done.2.other_ref
  34.0 0.0 copy-start.1
  34.0 1.0 copy-done.1
  35.1 13.3 %attention.1 = (bf16[1024,256]{1,0:T(8,128)(2,1)S(1)}, bf16[1024,256]{1,0:T(8,128)(2,1)S(1)}, bf16[8,2,128,256]{3,2,1,0:T(8,128)(2,1)S(1)}, bf16[8,2,128,256]{3,2,1,0:T(8,128)(2,1)S(1)}) custom-call(s32[1]{0:T(128)} %bitcast.core_ref, bf16[1024,256]{1,0:T(8,128)(2,1)S(1)} %collective-permute-done.q_ref, bf16[1024,256]{1,0:T(8,128)(2,1)S(1)} %copy-done.1, ...), custom_call_target="tpu_custom_call" | custom-call | flops 6442450944 | bytes 8388608 | tf_op jit(solution)/shard_map/attention/pallas_call | solution.py:188
  48.4 0.0 copy-start.2
  48.4 0.8 copy-done.2
  49.2 13.4 %collective-permute-start.5 = (bf16[8,2,128,256]{3,2,1,0:T(8,128)(2,1)S(1)}, bf16[8,2,128,256]{3,2,1,0:T(8,128)(2,1)S(1)}, u32[]{:S(2)}, u32[]{:S(2)}) collective-permute-start(bf16[8,2,128,256]{3,2,1,0:T(8,128)(2,1)S(1)} %get-tuple-element.11), channel_id=1, source_target_pairs={{0,1},{1,0},{2,3},{3,2},{4,5},{5,4},{6,7},{7,6},{8,9},{9,8},{10,11... | collective-permute-start | bytes 3145736 | tf_op jit(solution)/shard_map/ppermute | solution.py:27
  62.6 2.3 %collective-permute-done.5 = bf16[8,2,128,256]{3,2,1,0:T(8,128)(2,1)S(1)} collective-permute-done((bf16[8,2,128,256]{3,2,1,0:T(8,128)(2,1)S(1)}, bf16[8,2,128,256]{3,2,1,0:T(8,128)(2,1)S(1)}, u32[]{:S(2)}, u32[]{:S(2)}) %collective-permute-start.5) | collective-permute-done | bytes 1048608 | tf_op jit(solution)/shard_map/ppermute | solution.py:27
  64.9 1.3 %add_convert_fusion = bf16[8,2,128,256]{3,2,1,0:T(8,128)(2,1)} fusion(bf16[8,2,128,256]{3,2,1,0:T(8,128)(2,1)S(1)} %collective-permute-done.5, bf16[8,2,128,256]{3,2,1,0:T(8,128)(2,1)S(1)} %get-tuple-element.10), kind=kLoop, calls=%fused_computation | loop fusion | flops 2097152 | bytes 3145728 | tf_op jit(solution)/shard_map/convert_element_type | solution.py:239
  66.2 8.7 %all-to-all-start.1 = ((bf16[8,2,128,256]{3,2,1,0:T(8,128)(2,1)}), bf16[8,2,128,256]{3,2,1,0:T(8,128)(2,1)S(1)}, u32[]{:S(2)}, u32[]{:S(2)}) async-start(bf16[8,2,128,256]{3,2,1,0:T(8,128)(2,1)} %add_convert_fusion), calls=%async_computation.1 | async-start | bytes 2097152 | tf_op jit(solution)/shard_map/all_to_all | solution.py:31
  74.9 0.0 copy-done.3
  74.9 0.7 collective-permute-start.3
  75.6 0.7 collective-permute-start.4
  76.3 26.4 %all-to-all-done.1 = bf16[8,2,128,256]{3,2,1,0:T(8,128)(2,1)S(1)} async-done(((bf16[8,2,128,256]{3,2,1,0:T(8,128)(2,1)}), bf16[8,2,128,256]{3,2,1,0:T(8,128)(2,1)S(1)}, u32[]{:S(2)}, u32[]{:S(2)}) %all-to-all-start.1) | async-done | bytes 1048608 | tf_op jit(solution)/shard_map/all_to_all | solution.py:31
  102.7 0.1 reduce_sum.12
  102.9 0.7 copy.8
  103.6 3.5 %all-to-all-start.2 = ((bf16[16,16,256]{2,1,0:T(8,128)(2,1)}), bf16[16,16,256]{2,1,0:T(8,128)(2,1)S(1)}, u32[]{:S(2)}, u32[]{:S(2)}) async-start(bf16[16,16,256]{2,1,0:T(8,128)(2,1)} %bitcast.4), calls=%async_computation.2 | async-start | bytes 262144 | tf_op jit(solution)/shard_map/all_to_all | solution.py:31
  107.1 0.0 collective-permute-done.3
  107.1 0.0 collective-permute-done.4
  107.1 7.9 %all-to-all-done.2 = bf16[16,16,256]{2,1,0:T(8,128)(2,1)S(1)} async-done(((bf16[16,16,256]{2,1,0:T(8,128)(2,1)}), bf16[16,16,256]{2,1,0:T(8,128)(2,1)S(1)}, u32[]{:S(2)}, u32[]{:S(2)}) %all-to-all-start.2) | async-done | bytes 131104 | tf_op jit(solution)/shard_map/all_to_all | solution.py:31
  115.0 0.7 fusion
  115.7 0.8 copy.11
  116.5 0.8 copy.12
  (1 shorter events, 0.0 us)
Async XLA Ops:
  29.8 4.2 %collective-permute-start.2 = (bf16[8,2,128,256]{3,2,1,0:T(8,128)(2,1)S(1)}, bf16[8,2,128,256]{3,2,1,0:T(8,128)(2,1)S(1)}, u32[]{:S(2)}, u32[]{:S(2)}) collective-permute-start(bf16[8,2,128,256]{3,2,1,0:T(8,128)(2,1)S(1)} %all_to_all.15.own_ref), channel_id=1, source_target_pairs={{0,1},{1,0},{2,3},{3,2},{4,5},{5,4},{6,7},{7,6},{8,9},{9,8},{10,11... | collective-permute-start | bytes 3145736 | tf_op jit(solution)/shard_map/ppermute | solution.py:27
  29.8 3.4 %collective-permute-start = (bf16[1024,256]{1,0:T(8,128)(2,1)}, bf16[1024,256]{1,0:T(8,128)(2,1)S(1)}, u32[]{:S(2)}, u32[]{:S(2)}) collective-permute-start(bf16[1024,256]{1,0:T(8,128)(2,1)} %param.4), channel_id=1, source_target_pairs={{0,0},{1,128},{2,2},{3,130},{4,4},{5,132},{6,6},{7,134},{8,8},{9,1... | collective-permute-start | bytes 1572872 | tf_op jit(solution)/shard_map/ppermute | solution.py:27
  31.5 1.7 %collective-permute-start.1 = (bf16[1024,256]{1,0:T(8,128)(2,1)}, bf16[1024,256]{1,0:T(8,128)(2,1)S(1)}, u32[]{:S(2)}, u32[]{:S(2)}) collective-permute-start(bf16[1024,256]{1,0:T(8,128)(2,1)} %param.7), channel_id=1, source_target_pairs={{0,0},{1,128},{2,2},{3,130},{4,4},{5,132},{6,6},{7,134},{8,8},{9,1... | collective-permute-start | bytes 1572872 | tf_op jit(solution)/shard_map/ppermute | solution.py:27
  33.2 0.8 copy-start
  34.0 1.0 copy-start.1
  48.4 0.8 copy-start.2
  49.2 15.7 %collective-permute-start.5 = (bf16[8,2,128,256]{3,2,1,0:T(8,128)(2,1)S(1)}, bf16[8,2,128,256]{3,2,1,0:T(8,128)(2,1)S(1)}, u32[]{:S(2)}, u32[]{:S(2)}) collective-permute-start(bf16[8,2,128,256]{3,2,1,0:T(8,128)(2,1)S(1)} %get-tuple-element.11), channel_id=1, source_target_pairs={{0,1},{1,0},{2,3},{3,2},{4,5},{5,4},{6,7},{7,6},{8,9},{9,8},{10,11... | collective-permute-start | bytes 3145736 | tf_op jit(solution)/shard_map/ppermute | solution.py:27
  66.2 8.7 %copy-start.3 = (bf16[1024,256]{1,0:T(8,128)(2,1)S(1)}, bf16[1024,256]{1,0:T(8,128)(2,1)}, u32[]{:S(2)}) copy-start(bf16[1024,256]{1,0:T(8,128)(2,1)} %copy-done.2) | copy-start | bytes 1572868
  66.2 36.5 %all-to-all-start.1 = ((bf16[8,2,128,256]{3,2,1,0:T(8,128)(2,1)}), bf16[8,2,128,256]{3,2,1,0:T(8,128)(2,1)S(1)}, u32[]{:S(2)}, u32[]{:S(2)}) async-start(bf16[8,2,128,256]{3,2,1,0:T(8,128)(2,1)} %add_convert_fusion), calls=%async_computation.1 | async-start | bytes 2097152 | tf_op jit(solution)/shard_map/all_to_all | solution.py:31
  74.9 32.1 %collective-permute-start.3 = (bf16[1024,256]{1,0:T(8,128)(2,1)S(1)}, bf16[1024,256]{1,0:T(8,128)(2,1)S(1)}, u32[]{:S(2)}, u32[]{:S(2)}) collective-permute-start(bf16[1024,256]{1,0:T(8,128)(2,1)S(1)} %copy-done.3), channel_id=1, source_target_pairs={{0,0},{1,128},{2,2},{3,130},{4,4},{5,132},{6,6},{7,134},{8,8},{9,1... | collective-permute-start | bytes 1572872 | tf_op jit(solution)/shard_map/ppermute | solution.py:27
  75.6 31.5 %collective-permute-start.4 = (bf16[1024,256]{1,0:T(8,128)(2,1)S(1)}, bf16[1024,256]{1,0:T(8,128)(2,1)S(1)}, u32[]{:S(2)}, u32[]{:S(2)}) collective-permute-start(bf16[1024,256]{1,0:T(8,128)(2,1)S(1)} %get-tuple-element.9), channel_id=1, source_target_pairs={{0,0},{1,128},{2,2},{3,130},{4,4},{5,132},{6,6},{7,134},{8,8},{9,1... | collective-permute-start | bytes 1572872 | tf_op jit(solution)/shard_map/ppermute | solution.py:27
  103.6 11.5 %all-to-all-start.2 = ((bf16[16,16,256]{2,1,0:T(8,128)(2,1)}), bf16[16,16,256]{2,1,0:T(8,128)(2,1)S(1)}, u32[]{:S(2)}, u32[]{:S(2)}) async-start(bf16[16,16,256]{2,1,0:T(8,128)(2,1)} %bitcast.4), calls=%async_computation.2 | async-start | bytes 262144 | tf_op jit(solution)/shard_map/all_to_all | solution.py:31

commit v2 on v1

v2 whole, which is shorter than its diff:
```python
import functools
import itertools

import jax
import jax.numpy as jnp
from jax import lax
from jax.experimental import pallas as pl
from jax.experimental.pallas import tpu as pltpu
from jax.sharding import PartitionSpec as P

HEAD_DIM = 256
AXES = ("query", "head")
X_LO, Z, Y, X_HI, CORE = 2, 8, 4, 2, 2
CHUNK = 256
LOG2E = 1.4426950408889634


def device(xl, z, y, xh, c):
    return (xl * Z + z) * (Y * X_HI * CORE) + (y * X_HI + xh) * CORE + c


def permute(array, to):
    pairs = [
        (device(*at), device(*to(*at)))
        for at in itertools.product(range(X_LO), range(Z), range(Y), range(X_HI), range(CORE))
    ]
    return lax.ppermute(array, AXES, pairs)


def exchange(array, groups):
    return lax.all_to_all(
        array, AXES, split_axis=0, concat_axis=0, axis_index_groups=groups, tiled=True
    )


def trade(array):
    pairs = []
    for z, y, xh in itertools.product(range(Z), range(Y), range(X_HI)):
        one, two = device(0, z, y, xh, 1), device(1, z, y, xh, 0)
        pairs += [(one, two), (two, one)]
    return lax.ppermute(array, AXES, pairs)


def other_core(xl, z, y, xh, c):
    return (xl, z, y, xh, 1 - c)


def head_groups():
    return [
        [device(xl, z, y, xh, c) for y in range(Y) for xh in range(X_HI)]
        for xl in range(X_LO)
        for z in range(Z)
        for c in range(CORE)
    ]


def column_groups():
    return [
        [device(xl, z, y, xh, c) for y in range(Y) for xh in range(X_HI) for xl in range(X_LO)]
        for z in range(Z)
        for c in range(CORE)
    ]


SMEM = pl.BlockSpec(memory_space=pltpu.SMEM)
VMEM = pl.BlockSpec(memory_space=pltpu.VMEM)
ANY = pl.BlockSpec(memory_space=pl.ANY)
PARAMS = pltpu.CompilerParams(vmem_limit_bytes=32 * 1024 * 1024)
LARGE = pltpu.CompilerParams(vmem_limit_bytes=56 * 1024 * 1024)


def pack_kernel(xl_ref, keys, values, queries, cotangents, memory_out, rows_out, sems, row_sems):
    copies = []
    for chip in range(Y * X_HI):
        start = pl.multiple_of((chip * 2 + xl_ref[0]) * HEAD_DIM, HEAD_DIM)
        for kind, source in enumerate((keys, values)):
            copies.append(
                pltpu.make_async_copy(
                    source.at[:, pl.ds(start, HEAD_DIM)],
                    memory_out.at[chip, kind],
                    sems.at[chip, kind],
                )
            )
    for kind, source in enumerate((queries, cotangents)):
        copies.append(pltpu.make_async_copy(source, rows_out.at[kind], row_sems.at[kind]))
    for copy in copies:
        copy.start()
    for copy in copies:
        copy.wait()


def pack(xl, keys, values, queries, cotangents):
    rows = keys.shape[0]
    return pl.pallas_call(
        pack_kernel,
        out_shape=(
            jax.ShapeDtypeStruct((Y * X_HI, 2, rows, HEAD_DIM), keys.dtype),
            jax.ShapeDtypeStruct((2,) + queries.shape, queries.dtype),
        ),
        in_specs=[SMEM] + [ANY] * 4,
        out_specs=(VMEM, VMEM),
        scratch_shapes=[
            pltpu.SemaphoreType.DMA((Y * X_HI, 2)),
            pltpu.SemaphoreType.DMA((2,)),
        ],
        compiler_params=LARGE,
        name="pack",
    )(xl, keys, values, queries, cotangents)


def unpack_kernel(stay_ref, mine, came, attended, gradients, held, sems):
    def start(source):
        for kind in range(2):
            pltpu.make_async_copy(source.at[kind], held.at[kind], sems.at[0, kind]).start()

    pl.when(stay_ref[0] == 1)(lambda: start(mine))
    pl.when(stay_ref[0] == 0)(lambda: start(came))
    for kind, out in enumerate((attended, gradients)):
        pltpu.make_async_copy(came.at[kind], held.at[kind], sems.at[0, kind]).wait()
        pltpu.make_async_copy(held.at[kind], out, sems.at[1, kind]).start()
    for kind, out in enumerate((attended, gradients)):
        pltpu.make_async_copy(held.at[kind], out, sems.at[1, kind]).wait()


def unpack(stay, mine, came):
    out = jax.ShapeDtypeStruct(mine.shape[1:], mine.dtype)
    return pl.pallas_call(
        unpack_kernel,
        out_shape=(out, out),
        in_specs=[SMEM, ANY, ANY],
        out_specs=(ANY, ANY),
        scratch_shapes=[pltpu.VMEM(mine.shape, mine.dtype), pltpu.SemaphoreType.DMA((2, 2))],
        compiler_params=LARGE,
        name="unpack",
    )(stay, mine, came)


def core_sum_kernel(z_ref, keep, came, up, down, across, ahead, behind, own):
    def chunk(distance):
        at = lax.rem(z_ref[0] + distance, Z)
        return keep[at].astype(jnp.float32) + came[at].astype(jnp.float32)

    bf16 = jnp.bfloat16
    up[0] = chunk(3).astype(bf16)
    up[1] = chunk(1).astype(bf16)
    down[0] = chunk(5).astype(bf16)
    down[1] = chunk(7).astype(bf16)
    across[...] = chunk(4).astype(bf16)
    ahead[...] = chunk(2)
    behind[...] = chunk(6)
    own[...] = chunk(0)


def core_sum(z, keep, came):
    shape = keep.shape[1:]
    bf16, f32 = jnp.bfloat16, jnp.float32
    return pl.pallas_call(
        core_sum_kernel,
        out_shape=(
            jax.ShapeDtypeStruct((2,) + shape, bf16),
            jax.ShapeDtypeStruct((2,) + shape, bf16),
            jax.ShapeDtypeStruct(shape, bf16),
            jax.ShapeDtypeStruct(shape, f32),
            jax.ShapeDtypeStruct(shape, f32),
            jax.ShapeDtypeStruct(shape, f32),
        ),
        in_specs=[SMEM, VMEM, VMEM],
        out_specs=(VMEM,) * 6,
        compiler_params=PARAMS,
        name="core_sum",
    )(z, keep, came)


def middle_sum_kernel(core_ref, ahead, behind, from_below, from_above, across, up, down):
    far = across[...].astype(jnp.float32)
    first = core_ref[0] == 0
    zero = jnp.zeros_like(far)
    below = from_below[0].astype(jnp.float32) + jnp.where(first, far, zero)
    above = from_above[0].astype(jnp.float32) + jnp.where(first, zero, far)
    up[...] = (ahead[...] + below).astype(jnp.bfloat16)
    down[...] = (behind[...] + above).astype(jnp.bfloat16)


def middle_sum(core, ahead, behind, from_below, from_above, across):
    out = jax.ShapeDtypeStruct(ahead.shape, jnp.bfloat16)
    return pl.pallas_call(
        middle_sum_kernel,
        out_shape=(out, out),
        in_specs=[SMEM] + [VMEM] * 5,
        out_specs=(VMEM, VMEM),
        compiler_params=PARAMS,
        name="middle_sum",
    )(core, ahead, behind, from_below, from_above, across)


def last_sum_kernel(own, from_below, from_above, low, high, out):
    f32 = jnp.float32
    total = own[...] + from_below[1].astype(f32) + from_above[1].astype(f32)
    total = total + low[...].astype(f32) + high[...].astype(f32)
    total = total.reshape(2, X_LO, Y * X_HI, 8, HEAD_DIM)
    for xl in range(X_LO):
        for chip in range(Y * X_HI):
            both = jnp.concatenate([total[0, xl, chip], total[1, xl, chip]], axis=0)
            out[chip * 2 + xl] = both.astype(jnp.bfloat16)


def last_sum(own, from_below, from_above, low, high):
    return pl.pallas_call(
        last_sum_kernel,
        out_shape=jax.ShapeDtypeStruct((Y * X_HI * X_LO, 16, HEAD_DIM), jnp.bfloat16),
        in_specs=[VMEM] * 5,
        out_specs=VMEM,
        compiler_params=PARAMS,
        name="last_sum",
    )(own, from_below, from_above, low, high)


def columns_kernel(parts, keys, values):
    for head in range(Y * X_HI * X_LO):
        both = parts[head].astype(jnp.float32)
        at = pl.ds(head * HEAD_DIM, HEAD_DIM)
        keys[:, at] = both[:8].astype(jnp.bfloat16)
        values[:, at] = both[8:].astype(jnp.bfloat16)


def columns(parts):
    out = jax.ShapeDtypeStruct((8, parts.shape[0] * HEAD_DIM), jnp.bfloat16)
    return pl.pallas_call(
        columns_kernel,
        out_shape=(out, out),
        in_specs=[VMEM],
        out_specs=(VMEM, VMEM),
        compiler_params=PARAMS,
        name="columns",
    )(parts)


def sum_over_z(z, core, keep, came):
    above = lambda hops: lambda xl, z, y, xh, c: (xl, (z + hops) % Z, y, xh, c)
    over = lambda xl, z, y, xh, c: (xl, (z + (2 if c == 0 else 6)) % Z, y, xh, c)
    up, down, across, ahead, behind, own = core_sum(z, keep, came)
    from_below = permute(up, above(1))
    from_above = permute(down, above(7))
    far = permute(across, over)
    up, down = middle_sum(core, ahead, behind, from_below, from_above, far)
    low = permute(up, above(2))
    high = permute(down, above(6))
    return last_sum(own, from_below, from_above, low, high)


def nt(a, b):
    return lax.dot_general(a, b, (((1,), (1,)), ((), ())), preferred_element_type=jnp.float32)


def nn(a, b):
    return jnp.dot(a, b, preferred_element_type=jnp.float32)


def attention_kernel(
    core_ref, stay_ref, queries, cotangents, came, own, other,
    rows_out, keep_ref, send_ref,
    q_ref, do_ref, k_ref, v_ref, kt_ref, vt_ref, s_ref, e_ref, ds_ref, dos_ref, row_sems, sems,
):
    core = core_ref[0]
    memory = k_ref.shape[0]
    block = own.shape[2]

    def start_rows(q, do):
        pltpu.make_async_copy(q, q_ref, row_sems.at[0]).start()
        pltpu.make_async_copy(do, do_ref, row_sems.at[1]).start()

    pl.when(stay_ref[0] == 1)(lambda: start_rows(queries, cotangents))
    pl.when(stay_ref[0] == 0)(lambda: start_rows(came.at[0], came.at[1]))
    copies = [[], []]
    for kind, held in enumerate((k_ref, v_ref)):
        for chip in range(Y * X_HI):
            for side, (source, at) in enumerate(((own, core), (other, 1 - core))):
                rows = pl.ds(pl.multiple_of((chip * 2 + at) * block, block), block)
                copies[kind].append(
                    pltpu.make_async_copy(
                        source.at[chip, kind], held.at[rows], sems.at[kind, chip, side]
                    )
                )
                copies[kind][-1].start()
    pltpu.make_async_copy(queries, q_ref, row_sems.at[0]).wait()
    for copy in copies[0]:
        copy.wait()

    chunks = [pl.ds(i * CHUNK, CHUNK) for i in range(memory // CHUNK)]
    factor = LOG2E * HEAD_DIM ** (-0.5)
    scale = HEAD_DIM ** (-0.5)
    q = q_ref[...]
    top = None
    for rows in chunks:
        s = nt(k_ref[rows, :], q)
        s_ref[rows, :] = s
        here = jnp.max(s, axis=0, keepdims=True)
        top = here if top is None else jnp.maximum(top, here)
    top = top * factor
    for copy in copies[1]:
        copy.wait()
    for rows in chunks:
        kt_ref[:, rows] = k_ref[rows, :].T
        vt_ref[:, rows] = v_ref[rows, :].T
    total = None
    att = None
    for rows in chunks:
        e = jnp.exp2(s_ref[rows, :] * factor - top)
        here = jnp.sum(e, axis=0, keepdims=True)
        total = here if total is None else total + here
        eb = e.astype(jnp.bfloat16)
        e_ref[rows, :] = eb
        part = nn(vt_ref[:, rows], eb)
        att = part if att is None else att + part
    inverse = 1.0 / total
    att = att * inverse
    rows_out[0] = att.T.astype(jnp.bfloat16)
    pltpu.make_async_copy(cotangents, do_ref, row_sems.at[1]).wait()
    dot = (do_ref[...].astype(jnp.float32).T * inverse).astype(jnp.bfloat16)
    delta = jnp.sum(att * dot.astype(jnp.float32), axis=0, keepdims=True)
    dos_ref[...] = dot.T
    dq = None
    for rows in chunks:
        dp = nn(v_ref[rows, :], dot)
        ds = (e_ref[rows, :].astype(jnp.float32) * (dp - delta)).astype(jnp.bfloat16)
        ds_ref[rows, :] = ds
        part = nn(kt_ref[:, rows], ds)
        dq = part if dq is None else dq + part
    rows_out[1] = (dq * scale).T.astype(jnp.bfloat16)
    first = core == 0
    for i in range(memory // 256):
        rows = pl.ds(i * 256, 256)
        for kind, full in enumerate(
            (nn(ds_ref[rows, :], q_ref[...]) * scale, nn(e_ref[rows, :], dos_ref[...]))
        ):
            full = full.reshape(2, 8, 2, 8, HEAD_DIM)
            for half in range(2):
                xl, z = divmod(i * 2 + half, Z)
                low = full[half, :, 0].reshape(64, HEAD_DIM)
                high = full[half, :, 1].reshape(64, HEAD_DIM)
                at = pl.ds(xl * 64, 64)
                keep_ref[z, kind, at, :] = jnp.where(first, low, high).astype(jnp.bfloat16)
                send_ref[z, kind, at, :] = jnp.where(first, high, low).astype(jnp.bfloat16)


def attention(core, stay, queries, cotangents, came, own, other):
    rows = queries.shape[0]
    memory = 2 * own.shape[0] * own.shape[2]
    parts = (Z, 2, memory // (2 * Z), HEAD_DIM)
    bf16, f32 = jnp.bfloat16, jnp.float32
    return pl.pallas_call(
        attention_kernel,
        out_shape=(
            jax.ShapeDtypeStruct((2, rows, HEAD_DIM), bf16),
            jax.ShapeDtypeStruct(parts, bf16),
            jax.ShapeDtypeStruct(parts, bf16),
        ),
        in_specs=[SMEM, SMEM] + [ANY] * 5,
        out_specs=(VMEM, VMEM, VMEM),
        scratch_shapes=[
            pltpu.VMEM((rows, HEAD_DIM), bf16),
            pltpu.VMEM((rows, HEAD_DIM), bf16),
            pltpu.VMEM((memory, HEAD_DIM), bf16),
            pltpu.VMEM((memory, HEAD_DIM), bf16),
            pltpu.VMEM((HEAD_DIM, memory), bf16),
            pltpu.VMEM((HEAD_DIM, memory), bf16),
            pltpu.VMEM((memory, rows), f32),
            pltpu.VMEM((memory, rows), bf16),
            pltpu.VMEM((memory, rows), bf16),
            pltpu.VMEM((rows, HEAD_DIM), bf16),
            pltpu.SemaphoreType.DMA((2,)),
            pltpu.SemaphoreType.DMA((2, Y * X_HI, 2)),
        ],
        compiler_params=LARGE,
        cost_estimate=pl.CostEstimate(
            flops=12 * rows * memory * HEAD_DIM,
            bytes_accessed=8 * 1024 * 1024,
            transcendentals=rows * memory,
        ),
        name="attention",
    )(core, stay, queries, cotangents, came, own, other)


def per_device(queries, mem_keys, mem_values, grad_out):
    as_ref = lambda value: jnp.reshape(value, (1,)).astype(jnp.int32)
    xl = as_ref(lax.axis_index("query") // Z)
    z = as_ref(lax.axis_index("query") % Z)
    core = as_ref(lax.axis_index("head") % CORE)
    stay = (xl == core).astype(jnp.int32)
    memory, both = pack(xl, mem_keys, mem_values, queries, grad_out)
    both = trade(both)
    own = exchange(memory, head_groups())
    own, both = lax.optimization_barrier((own, both))
    other = permute(own, other_core)
    rows, keep, send = attention(core, stay, queries, grad_out, both, own, other)
    came = permute(send, other_core)
    traded = trade(rows)
    sums = sum_over_z(z, core, keep, came)
    attended, query_gradients = unpack(stay, rows, traded)
    grad_keys, grad_values = columns(exchange(sums, column_groups()))
    return attended, query_gradients, grad_keys, grad_values


def solution(mesh):
    in_specs = (P("query", "head"), P("head", None), P("head", None), P("query", "head"))
    out_specs = (
        P("query", "head"),
        P("query", "head"),
        P(("query", "head"), None),
        P(("query", "head"), None),
    )
    return jax.shard_map(
        per_device, mesh=mesh, in_specs=in_specs, out_specs=out_specs, check_vma=False
    )
```

time: 119 us -> 96.2 us (0.81); the launches traced: 117 us -> 95.9 us
  waiting for transfers between devices: 36.6 us -> 25.3 us
  starting transfers between devices: 30.4 us -> 21.9 us
  local copies, waits for them, and re-layouts: 5.54 us -> 3.18 us
  blocking collectives: 24.1 us -> 25.6 us
  other arithmetic: 1.44 us -> 0 us
    all_to_all x2 -> x1, waiting for transfers between devices: 34.3 us -> 4.92 us  [exchange(): lax.all_to_all(array, AXES, split_axis=0, concat_axis=0, axis_index_group...]
    ppermute x6 -> x7, waiting for transfers between devices: 2.3 us -> 20.4 us  [permute(): return lax.ppermute(array, AXES, pairs)]
    all_to_all x2 -> x1, starting transfers between devices: 12.2 us -> 3.51 us  [exchange(): lax.all_to_all(array, AXES, split_axis=0, concat_axis=0, axis_index_group...]
    all_to_all x1, blocking collectives: 24.1 us -> 25.6 us  [exchange(): lax.all_to_all(array, AXES, split_axis=0, concat_axis=0, axis_index_group...]
    ppermute x0 -> x2, starting transfers between devices: none -> 1.44 us  [trade(): return lax.ppermute(array, AXES, pairs)]
    convert_element_type x1 -> x0, other arithmetic: 1.3 us -> none  [per_device(): (keep.astype(jnp.float32) + came.astype(jnp.float32)).astype(jnp.bfloat16)]
    ppermute x6 -> x7, starting transfers between devices: 18.2 us -> 17 us  [permute(): return lax.ppermute(array, AXES, pairs)]
    pallas_call x2 -> x7, Pallas kernels: 18.4 us -> 19.1 us  [the longest x1 12.3 us: attention(): pl.pallas_call(attention_kernel, out_shape=(jax.ShapeDtypeStruct((2, rows...]
  transfers between devices with their start and end apart: 8 -> 10, of which waited for: 3 -> 6; matrix products, arithmetic and copies ran while one was open for 1% -> 0% of each run, Pallas kernels for 0% -> 3%
where the time goes in v2:
time: 96.2 us; the launch traced here: 95.9 us
  blocking collectives  25.6 us (27%)
  waiting for transfers between devices  25.3 us (26%)
  starting transfers between devices  21.9 us (23%)
  Pallas kernels  19.1 us (20%)
  local copies, waits for them, and re-layouts  3.18 us (3%)
    all_to_all x1, blocking collectives, exchange(): lax.all_to_all(array, AXES, split_axis=0, concat_axis=0, axis_index_group...  25.6 us
    ppermute x7, waiting for transfers between devices, permute(): return lax.ppermute(array, AXES, pairs)  20.4 us
    ppermute x7, starting transfers between devices, permute(): return lax.ppermute(array, AXES, pairs)  17 us
    pallas_call x1, Pallas kernels, attention(): pl.pallas_call(attention_kernel, out_shape=(jax.ShapeDtypeStruct((2, rows...  12.3 us
    all_to_all x1, waiting for transfers between devices, exchange(): lax.all_to_all(array, AXES, split_axis=0, concat_axis=0, axis_index_group...  4.92 us
    all_to_all x1, starting transfers between devices, exchange(): lax.all_to_all(array, AXES, split_axis=0, concat_axis=0, axis_index_group...  3.51 us
    unnamed x10, local copies, waits for them, and re-layouts  3.18 us
    pallas_call x1, Pallas kernels, pack(): pl.pallas_call(pack_kernel, out_shape=(jax.ShapeDtypeStruct((Y * X_HI, 2,...  3.14 us
  transfers between devices with their start and end apart: 10, of which 6 were waited for; matrix products, arithmetic and copies ran while one was open for 0% of the time, Pallas kernels for 3%

profile of v2, /device:TPU:32, one launch (start us, length us, event | category | flops | bytes accessed | tf_op | source)
XLA Modules:
  0.0 95.9 jit_solution(10271233166248326905)
XLA Ops:
  0.6 3.1 %pack.1 = (bf16[8,2,128,256]{3,2,1,0:T(8,128)(2,1)}, bf16[2,1024,256]{2,1,0:T(8,128)(2,1)}) custom-call(s32[1]{0:T(128)} %bitcast.xl_ref, bf16[128,4096]{1,0:T(8,128)(2,1)} %keys.1, bf16[128,4096]{1,0:T(8,128)(2,1)} %values.1, bf16[1024,256]{1,0:T(8,128)(2,1)} %queries.3, bf16[1024,256]{1,0:T(8,128)(2,1)} %cotangents.3), custom_call_target="tpu_custom_call" | custom-call | tf_op jit(solution)/shard_map/pack/pallas_call | solution.py:94
  3.8 0.7 collective-permute-start
  4.5 25.6 %all_to_all.10.own = bf16[8,2,128,256]{3,2,1,0:T(8,128)(2,1)S(1)} all-to-all(bf16[8,2,128,256]{3,2,1,0:T(8,128)(2,1)} %get-tuple-element.23), channel_id=1, replica_groups={{0,2,4,6,8,10,12,14},{1,3,5,7,9,11,13,15},{16,18,20,22,24,26,28,30},{17..., dimensions={0} | all-to-all | bytes 2097152 | tf_op jit(solution)/shard_map/all_to_all | solution.py:31
  30.2 0.0 collective-permute-done.came
  30.2 5.8 %collective-permute-start.1 = (bf16[8,2,128,256]{3,2,1,0:T(8,128)(2,1)S(1)}, bf16[8,2,128,256]{3,2,1,0:T(8,128)(2,1)S(1)}, u32[]{:S(2)}, u32[]{:S(2)}) collective-permute-start(bf16[8,2,128,256]{3,2,1,0:T(8,128)(2,1)S(1)} %all_to_all.10.own), channel_id=1, source_target_pairs={{0,1},{1,0},{2,3},{3,2},{4,5},{5,4},{6,7},{7,6},{8,9},{9,8},{10,11... | collective-permute-start | bytes 3145736 | tf_op jit(solution)/shard_map/ppermute | solution.py:27
  35.9 2.3 %collective-permute-done.1.other = bf16[8,2,128,256]{3,2,1,0:T(8,128)(2,1)S(1)} collective-permute-done((bf16[8,2,128,256]{3,2,1,0:T(8,128)(2,1)S(1)}, bf16[8,2,128,256]{3,2,1,0:T(8,128)(2,1)S(1)}, u32[]{:S(2)}, u32[]{:S(2)}) %collective-permute-start.1) | collective-permute-done | bytes 1048608 | tf_op jit(solution)/shard_map/ppermute | solution.py:27
  38.2 0.0 copy-done.2
  38.2 1.0 %copy-done.4 = bf16[8,2,128,256]{3,2,1,0:T(8,128)(2,1)} copy-done((bf16[8,2,128,256]{3,2,1,0:T(8,128)(2,1)}, bf16[8,2,128,256]{3,2,1,0:T(8,128)(2,1)S(1)}, u32[]{:S(2)}) %copy-start.4) | copy-done | bytes 1048600
  39.2 12.3 %attention.1 = (bf16[2,1024,256]{2,1,0:T(8,128)(2,1)}, bf16[8,2,128,256]{3,2,1,0:T(8,128)(2,1)}, bf16[8,2,128,256]{3,2,1,0:T(8,128)(2,1)}) custom-call(s32[1]{0:T(128)} %bitcast.1.core_ref, s32[1]{0:T(128)S(6)} %convert_element_type.3.stay_ref, bf16[1024,256]{1,0:T(8,128)(2,1)} %queries.3, bf16[1024,256]{1,0:T(8,128)(2,1)} %cotangents.3, ...), custom_call_target="tpu_custom_call" | custom-call | flops 6442450944 | bytes 8388608 | tf_op jit(solution)/shard_map/attention/pallas_call | solution.py:351
  51.4 0.5 collective-permute-start.3
  51.9 0.7 collective-permute-start.2
  52.7 1.8 %collective-permute-done.3.came = bf16[8,2,128,256]{3,2,1,0:T(8,128)(2,1)S(1)} collective-permute-done((bf16[8,2,128,256]{3,2,1,0:T(8,128)(2,1)}, bf16[8,2,128,256]{3,2,1,0:T(8,128)(2,1)S(1)}, u32[]{:S(2)}, u32[]{:S(2)}) %collective-permute-start.3) | collective-permute-done | bytes 1048608 | tf_op jit(solution)/shard_map/ppermute | solution.py:27
  54.4 1.2 %copy-done = bf16[8,2,128,256]{3,2,1,0:T(8,128)(2,1)S(1)} copy-done((bf16[8,2,128,256]{3,2,1,0:T(8,128)(2,1)S(1)}, bf16[8,2,128,256]{3,2,1,0:T(8,128)(2,1)}, u32[]{:S(2)}) %copy-start) | copy-done | bytes 1048600
  55.7 0.2 core_sum.1
  55.9 2.0 %collective-permute-start.4 = (bf16[2,2,128,256]{3,2,1,0:T(8,128)(2,1)S(1)}, bf16[2,2,128,256]{3,2,1,0:T(8,128)(2,1)S(1)}, u32[]{:S(2)}, u32[]{:S(2)}) collective-permute-start(bf16[2,2,128,256]{3,2,1,0:T(8,128)(2,1)S(1)} %get-tuple-element.33), channel_id=1, source_target_pairs={{0,16},{1,17},{2,18},{3,19},{4,20},{5,21},{6,22},{7,23},{8,24},{9,... | collective-permute-start | bytes 786440 | tf_op jit(solution)/shard_map/ppermute | solution.py:27
  57.9 0.1 collective-permute-start.5
  58.0 4.4 %collective-permute-start.6 = (bf16[2,128,256]{2,1,0:T(8,128)(2,1)S(1)}, bf16[2,128,256]{2,1,0:T(8,128)(2,1)S(1)}, u32[]{:S(2)}, u32[]{:S(2)}) collective-permute-start(bf16[2,128,256]{2,1,0:T(8,128)(2,1)S(1)} %get-tuple-element.37), channel_id=1, source_target_pairs={{0,32},{1,97},{2,34},{3,99},{4,36},{5,101},{6,38},{7,103},{8,40},{... | collective-permute-start | bytes 393224 | tf_op jit(solution)/shard_map/ppermute | solution.py:27
  62.4 7.8 %collective-permute-done.6.across = bf16[2,128,256]{2,1,0:T(8,128)(2,1)S(1)} collective-permute-done((bf16[2,128,256]{2,1,0:T(8,128)(2,1)S(1)}, bf16[2,128,256]{2,1,0:T(8,128)(2,1)S(1)}, u32[]{:S(2)}, u32[]{:S(2)}) %collective-permute-start.6) | collective-permute-done | bytes 131104 | tf_op jit(solution)/shard_map/ppermute | solution.py:27
  70.2 0.0 collective-permute-done.4.from_below
  70.2 0.0 collective-permute-done.5.from_above
  70.2 0.1 middle_sum.1
  70.3 4.1 %collective-permute-start.7 = (bf16[2,128,256]{2,1,0:T(8,128)(2,1)S(1)}, bf16[2,128,256]{2,1,0:T(8,128)(2,1)S(1)}, u32[]{:S(2)}, u32[]{:S(2)}) collective-permute-start(bf16[2,128,256]{2,1,0:T(8,128)(2,1)S(1)} %get-tuple-element.38), channel_id=1, source_target_pairs={{0,32},{1,33},{2,34},{3,35},{4,36},{5,37},{6,38},{7,39},{8,40},{9,... | collective-permute-start | bytes 393224 | tf_op jit(solution)/shard_map/ppermute | solution.py:27
  74.3 0.1 collective-permute-start.8
  74.5 5.0 %collective-permute-done.7.low = bf16[2,128,256]{2,1,0:T(8,128)(2,1)S(1)} collective-permute-done((bf16[2,128,256]{2,1,0:T(8,128)(2,1)S(1)}, bf16[2,128,256]{2,1,0:T(8,128)(2,1)S(1)}, u32[]{:S(2)}, u32[]{:S(2)}) %collective-permute-start.7) | collective-permute-done | bytes 131104 | tf_op jit(solution)/shard_map/ppermute | solution.py:27
  79.5 3.5 %collective-permute-done.8.high = bf16[2,128,256]{2,1,0:T(8,128)(2,1)S(1)} collective-permute-done((bf16[2,128,256]{2,1,0:T(8,128)(2,1)S(1)}, bf16[2,128,256]{2,1,0:T(8,128)(2,1)S(1)}, u32[]{:S(2)}, u32[]{:S(2)}) %collective-permute-start.8) | collective-permute-done | bytes 131104 | tf_op jit(solution)/shard_map/ppermute | solution.py:27
  83.0 0.7 last_sum.1
  83.7 3.5 %all-to-all-start.1 = ((bf16[16,16,256]{2,1,0:T(8,128)(2,1)}), bf16[16,16,256]{2,1,0:T(8,128)(2,1)S(1)}, u32[]{:S(2)}, u32[]{:S(2)}) async-start(bf16[16,16,256]{2,1,0:T(8,128)(2,1)} %last_sum.1), calls=%async_computation.1 | async-start | bytes 262144 | tf_op jit(solution)/shard_map/all_to_all | solution.py:31
  87.3 0.0 collective-permute-done.2.came
  87.3 1.0 %copy-done.1 = bf16[2,1024,256]{2,1,0:T(8,128)(2,1)} copy-done((bf16[2,1024,256]{2,1,0:T(8,128)(2,1)}, bf16[2,1024,256]{2,1,0:T(8,128)(2,1)S(1)}, u32[]{:S(2)}) %copy-start.1) | copy-done | bytes 1048600
  88.2 2.0 %unpack.1 = (bf16[1024,256]{1,0:T(8,128)(2,1)}, bf16[1024,256]{1,0:T(8,128)(2,1)}) custom-call(s32[1]{0:T(128)S(6)} %convert_element_type.3.stay_ref, bf16[2,1024,256]{2,1,0:T(8,128)(2,1)} %get-tuple-element.27.mine, bf16[2,1024,256]{2,1,0:T(8,128)(2,1)} %copy-done.1), custom_call_target="tpu_custom_call" | custom-call | tf_op jit(solution)/shard_map/unpack/pallas_call | solution.py:127
  90.3 4.9 %all-to-all-done.1.parts = bf16[16,16,256]{2,1,0:T(8,128)(2,1)S(1)} async-done(((bf16[16,16,256]{2,1,0:T(8,128)(2,1)}), bf16[16,16,256]{2,1,0:T(8,128)(2,1)S(1)}, u32[]{:S(2)}, u32[]{:S(2)}) %all-to-all-start.1) | async-done | bytes 131104 | tf_op jit(solution)/shard_map/all_to_all | solution.py:31
  95.2 0.7 columns.1
  (6 shorter events, 0.0 us)
Async XLA Ops:
  3.8 26.4 %collective-permute-start = (bf16[2,1024,256]{2,1,0:T(8,128)(2,1)}, bf16[2,1024,256]{2,1,0:T(8,128)(2,1)S(1)}, u32[]{:S(2)}, u32[]{:S(2)}) collective-permute-start(bf16[2,1024,256]{2,1,0:T(8,128)(2,1)} %get-tuple-element.24), channel_id=1, source_target_pairs={{1,128},{128,1},{3,130},{130,3},{5,132},{132,5},{7,134},{134,7},{9... | collective-permute-start | bytes 3145736 | tf_op jit(solution)/shard_map/ppermute | solution.py:41
  30.2 8.1 %copy-start.2 = (bf16[8,2,128,256]{3,2,1,0:T(8,128)(2,1)}, bf16[8,2,128,256]{3,2,1,0:T(8,128)(2,1)S(1)}, u32[]{:S(2)}) copy-start(bf16[8,2,128,256]{3,2,1,0:T(8,128)(2,1)S(1)} %all_to_all.10.own) | copy-start | bytes 3145732
  30.2 8.1 %copy-start.3 = (bf16[2,1024,256]{2,1,0:T(8,128)(2,1)}, bf16[2,1024,256]{2,1,0:T(8,128)(2,1)S(1)}, u32[]{:S(2)}) copy-start(bf16[2,1024,256]{2,1,0:T(8,128)(2,1)S(1)} %collective-permute-done.came) | copy-start | bytes 3145732
  30.2 8.0 %collective-permute-start.1 = (bf16[8,2,128,256]{3,2,1,0:T(8,128)(2,1)S(1)}, bf16[8,2,128,256]{3,2,1,0:T(8,128)(2,1)S(1)}, u32[]{:S(2)}, u32[]{:S(2)}) collective-permute-start(bf16[8,2,128,256]{3,2,1,0:T(8,128)(2,1)S(1)} %all_to_all.10.own), channel_id=1, source_target_pairs={{0,1},{1,0},{2,3},{3,2},{4,5},{5,4},{6,7},{7,6},{8,9},{9,8},{10,11... | collective-permute-start | bytes 3145736 | tf_op jit(solution)/shard_map/ppermute | solution.py:27
  38.2 1.0 %copy-start.4 = (bf16[8,2,128,256]{3,2,1,0:T(8,128)(2,1)}, bf16[8,2,128,256]{3,2,1,0:T(8,128)(2,1)S(1)}, u32[]{:S(2)}) copy-start(bf16[8,2,128,256]{3,2,1,0:T(8,128)(2,1)S(1)} %collective-permute-done.1.other) | copy-start | bytes 3145732
  51.4 3.0 %collective-permute-start.3 = (bf16[8,2,128,256]{3,2,1,0:T(8,128)(2,1)}, bf16[8,2,128,256]{3,2,1,0:T(8,128)(2,1)S(1)}, u32[]{:S(2)}, u32[]{:S(2)}) collective-permute-start(bf16[8,2,128,256]{3,2,1,0:T(8,128)(2,1)} %get-tuple-element.31), channel_id=1, source_target_pairs={{0,1},{1,0},{2,3},{3,2},{4,5},{5,4},{6,7},{7,6},{8,9},{9,8},{10,11... | collective-permute-start | bytes 3145736 | tf_op jit(solution)/shard_map/ppermute | solution.py:27
  51.9 35.3 %collective-permute-start.2 = (bf16[2,1024,256]{2,1,0:T(8,128)(2,1)}, bf16[2,1024,256]{2,1,0:T(8,128)(2,1)S(1)}, u32[]{:S(2)}, u32[]{:S(2)}) collective-permute-start(bf16[2,1024,256]{2,1,0:T(8,128)(2,1)} %get-tuple-element.27.mine), channel_id=1, source_target_pairs={{1,128},{128,1},{3,130},{130,3},{5,132},{132,5},{7,134},{134,7},{9... | collective-permute-start | bytes 3145736 | tf_op jit(solution)/shard_map/ppermute | solution.py:41
  54.4 1.2 %copy-start = (bf16[8,2,128,256]{3,2,1,0:T(8,128)(2,1)S(1)}, bf16[8,2,128,256]{3,2,1,0:T(8,128)(2,1)}, u32[]{:S(2)}) copy-start(bf16[8,2,128,256]{3,2,1,0:T(8,128)(2,1)} %get-tuple-element.30.keep) | copy-start | bytes 3145732
  55.9 14.3 %collective-permute-start.4 = (bf16[2,2,128,256]{3,2,1,0:T(8,128)(2,1)S(1)}, bf16[2,2,128,256]{3,2,1,0:T(8,128)(2,1)S(1)}, u32[]{:S(2)}, u32[]{:S(2)}) collective-permute-start(bf16[2,2,128,256]{3,2,1,0:T(8,128)(2,1)S(1)} %get-tuple-element.33), channel_id=1, source_target_pairs={{0,16},{1,17},{2,18},{3,19},{4,20},{5,21},{6,22},{7,23},{8,24},{9,... | collective-permute-start | bytes 786440 | tf_op jit(solution)/shard_map/ppermute | solution.py:27
  57.9 12.3 %collective-permute-start.5 = (bf16[2,2,128,256]{3,2,1,0:T(8,128)(2,1)S(1)}, bf16[2,2,128,256]{3,2,1,0:T(8,128)(2,1)S(1)}, u32[]{:S(2)}, u32[]{:S(2)}) collective-permute-start(bf16[2,2,128,256]{3,2,1,0:T(8,128)(2,1)S(1)} %get-tuple-element.34), channel_id=1, source_target_pairs={{0,112},{1,113},{2,114},{3,115},{4,116},{5,117},{6,118},{7,119},{8... | collective-permute-start | bytes 786440 | tf_op jit(solution)/shard_map/ppermute | solution.py:27
  58.0 12.2 %collective-permute-start.6 = (bf16[2,128,256]{2,1,0:T(8,128)(2,1)S(1)}, bf16[2,128,256]{2,1,0:T(8,128)(2,1)S(1)}, u32[]{:S(2)}, u32[]{:S(2)}) collective-permute-start(bf16[2,128,256]{2,1,0:T(8,128)(2,1)S(1)} %get-tuple-element.37), channel_id=1, source_target_pairs={{0,32},{1,97},{2,34},{3,99},{4,36},{5,101},{6,38},{7,103},{8,40},{... | collective-permute-start | bytes 393224 | tf_op jit(solution)/shard_map/ppermute | solution.py:27
  70.3 9.3 %collective-permute-start.7 = (bf16[2,128,256]{2,1,0:T(8,128)(2,1)S(1)}, bf16[2,128,256]{2,1,0:T(8,128)(2,1)S(1)}, u32[]{:S(2)}, u32[]{:S(2)}) collective-permute-start(bf16[2,128,256]{2,1,0:T(8,128)(2,1)S(1)} %get-tuple-element.38), channel_id=1, source_target_pairs={{0,32},{1,33},{2,34},{3,35},{4,36},{5,37},{6,38},{7,39},{8,40},{9,... | collective-permute-start | bytes 393224 | tf_op jit(solution)/shard_map/ppermute | solution.py:27
  74.3 8.7 %collective-permute-start.8 = (bf16[2,128,256]{2,1,0:T(8,128)(2,1)S(1)}, bf16[2,128,256]{2,1,0:T(8,128)(2,1)S(1)}, u32[]{:S(2)}, u32[]{:S(2)}) collective-permute-start(bf16[2,128,256]{2,1,0:T(8,128)(2,1)S(1)} %get-tuple-element.39), channel_id=1, source_target_pairs={{0,96},{1,97},{2,98},{3,99},{4,100},{5,101},{6,102},{7,103},{8,104... | collective-permute-start | bytes 393224 | tf_op jit(solution)/shard_map/ppermute | solution.py:27
  83.7 11.5 %all-to-all-start.1 = ((bf16[16,16,256]{2,1,0:T(8,128)(2,1)}), bf16[16,16,256]{2,1,0:T(8,128)(2,1)S(1)}, u32[]{:S(2)}, u32[]{:S(2)}) async-start(bf16[16,16,256]{2,1,0:T(8,128)(2,1)} %last_sum.1), calls=%async_computation.1 | async-start | bytes 262144 | tf_op jit(solution)/shard_map/all_to_all | solution.py:31
  87.3 1.0 %copy-start.1 = (bf16[2,1024,256]{2,1,0:T(8,128)(2,1)}, bf16[2,1024,256]{2,1,0:T(8,128)(2,1)S(1)}, u32[]{:S(2)}) copy-start(bf16[2,1024,256]{2,1,0:T(8,128)(2,1)S(1)} %collective-permute-done.2.came) | copy-start | bytes 3145732

commit v3 on v2

v3 whole, which is shorter than its diff:
```python
import functools
import itertools

import jax
import jax.numpy as jnp
from jax import lax
from jax.experimental import pallas as pl
from jax.experimental.pallas import tpu as pltpu
from jax.sharding import PartitionSpec as P

HEAD_DIM = 256
AXES = ("query", "head")
X_LO, Z, Y, X_HI, CORE = 2, 8, 4, 2, 2
SCALE = HEAD_DIM ** (-0.5)
CHUNK_CHIPS = 4
LOG2E = 1.4426950408889634


def position():
    query, head = lax.axis_index("query"), lax.axis_index("head")
    return lax.div(query, Z), lax.rem(query, Z), lax.rem(head, CORE)


def device(xl, z, y, xh, c):
    return (xl * Z + z) * (Y * X_HI * CORE) + (y * X_HI + xh) * CORE + c


def permute(array, to):
    pairs = [
        (device(*at), device(*to(*at)))
        for at in itertools.product(range(X_LO), range(Z), range(Y), range(X_HI), range(CORE))
    ]
    return lax.ppermute(array, AXES, pairs)


def exchange(array, groups):
    return lax.all_to_all(
        array, AXES, split_axis=0, concat_axis=0, axis_index_groups=groups, tiled=True
    )


def trade(array):
    pairs = []
    for z, y, xh in itertools.product(range(Z), range(Y), range(X_HI)):
        one, two = device(0, z, y, xh, 1), device(1, z, y, xh, 0)
        pairs += [(one, two), (two, one)]
    return lax.ppermute(array, AXES, pairs)


def other_core(xl, z, y, xh, c):
    return (xl, z, y, xh, 1 - c)


def head_groups():
    return [
        [device(xl, z, y, xh, c) for y in range(Y) for xh in range(X_HI)]
        for xl in range(X_LO)
        for z in range(Z)
        for c in range(CORE)
    ]


def column_groups():
    return [
        [device(xl, z, y, xh, c) for y in range(Y) for xh in range(X_HI) for xl in range(X_LO)]
        for z in range(Z)
        for c in range(CORE)
    ]


VMEM = pl.BlockSpec(memory_space=pltpu.VMEM)
ANY = pl.BlockSpec(memory_space=pl.ANY)


def params(mib):
    return pltpu.CompilerParams(vmem_limit_bytes=mib * 1024 * 1024)


def pack_kernel(keys, values, out, held, sems):
    xl, _, _ = position()
    copies = [
        pltpu.make_async_copy(source, held.at[kind], sems.at[kind])
        for kind, source in enumerate((keys, values))
    ]
    for copy in copies:
        copy.start()
    for kind, copy in enumerate(copies):
        copy.wait()
        for chip in range(Y * X_HI):
            start = pl.multiple_of((chip * 2 + xl) * HEAD_DIM, HEAD_DIM)
            out[chip, kind] = held[kind, :, pl.ds(start, HEAD_DIM)]


def pack(keys, values):
    shape = (Y * X_HI, 2, keys.shape[0], HEAD_DIM)
    return pl.pallas_call(
        pack_kernel,
        out_shape=jax.ShapeDtypeStruct(shape, keys.dtype),
        in_specs=[ANY, ANY],
        out_specs=VMEM,
        scratch_shapes=[
            pltpu.VMEM((2,) + keys.shape, keys.dtype),
            pltpu.SemaphoreType.DMA((2,)),
        ],
        compiler_params=params(56),
        name="pack",
    )(keys, values)


def select_kernel(queries, cotangents, q_came, do_came, q, do):
    xl, _, core = position()
    stay = xl == core
    q[...] = jnp.where(stay, queries[...], q_came[...])
    do[...] = jnp.where(stay, cotangents[...], do_came[...])


def select(queries, cotangents, q_came, do_came):
    out = jax.ShapeDtypeStruct(queries.shape, queries.dtype)
    return pl.pallas_call(
        select_kernel,
        out_shape=(out, out),
        in_specs=[VMEM] * 4,
        out_specs=(VMEM, VMEM),
        compiler_params=params(8),
        cost_estimate=pl.CostEstimate(flops=0, bytes_accessed=3 * 1024 * 1024, transcendentals=0),
        name="select",
    )(queries, cotangents, q_came, do_came)


def unpack_kernel(mine, came, attended, gradients):
    xl, _, core = position()
    stay = xl == core
    attended[...] = jnp.where(stay, mine[0], came[0])
    gradients[...] = jnp.where(stay, mine[1], came[1])


def unpack(mine, came):
    out = jax.ShapeDtypeStruct(mine.shape[1:], mine.dtype)
    return pl.pallas_call(
        unpack_kernel,
        out_shape=(out, out),
        in_specs=[VMEM, VMEM],
        out_specs=(VMEM, VMEM),
        compiler_params=params(12),
        name="unpack",
    )(mine, came)


def core_sum_kernel(keep, came, up, down, across, ahead, behind, own):
    _, z, _ = position()

    def chunk(distance):
        at = lax.rem(z + distance, Z)
        return keep[at].astype(jnp.float32) + came[at].astype(jnp.float32)

    bf16 = jnp.bfloat16
    up[0] = chunk(3).astype(bf16)
    up[1] = chunk(1).astype(bf16)
    down[0] = chunk(5).astype(bf16)
    down[1] = chunk(7).astype(bf16)
    across[...] = chunk(4).astype(bf16)
    ahead[...] = chunk(2)
    behind[...] = chunk(6)
    own[...] = chunk(0)


def core_sum(keep, came):
    shape = keep.shape[1:]
    bf16, f32 = jnp.bfloat16, jnp.float32
    return pl.pallas_call(
        core_sum_kernel,
        out_shape=(
            jax.ShapeDtypeStruct((2,) + shape, bf16),
            jax.ShapeDtypeStruct((2,) + shape, bf16),
            jax.ShapeDtypeStruct(shape, bf16),
            jax.ShapeDtypeStruct(shape, f32),
            jax.ShapeDtypeStruct(shape, f32),
            jax.ShapeDtypeStruct(shape, f32),
        ),
        in_specs=[VMEM, VMEM],
        out_specs=(VMEM,) * 6,
        compiler_params=params(12),
        name="core_sum",
    )(keep, came)


def middle_sum_kernel(ahead, behind, from_below, from_above, across, up, down):
    far = across[...].astype(jnp.float32)
    first = position()[2] == 0
    zero = jnp.zeros_like(far)
    below = from_below[0].astype(jnp.float32) + jnp.where(first, far, zero)
    above = from_above[0].astype(jnp.float32) + jnp.where(first, zero, far)
    up[...] = (ahead[...] + below).astype(jnp.bfloat16)
    down[...] = (behind[...] + above).astype(jnp.bfloat16)


def middle_sum(ahead, behind, from_below, from_above, across):
    out = jax.ShapeDtypeStruct(ahead.shape, jnp.bfloat16)
    return pl.pallas_call(
        middle_sum_kernel,
        out_shape=(out, out),
        in_specs=[VMEM] * 5,
        out_specs=(VMEM, VMEM),
        compiler_params=params(12),
        name="middle_sum",
    )(ahead, behind, from_below, from_above, across)


def last_sum_kernel(own, from_below, from_above, low, high, out):
    f32 = jnp.float32
    total = own[...] + from_below[1].astype(f32) + from_above[1].astype(f32)
    total = total + low[...].astype(f32) + high[...].astype(f32)
    total = total.reshape(2, X_LO, Y * X_HI, 8, HEAD_DIM)
    for xl in range(X_LO):
        for chip in range(Y * X_HI):
            both = jnp.concatenate([total[0, xl, chip], total[1, xl, chip]], axis=0)
            out[chip * 2 + xl] = both.astype(jnp.bfloat16)


def last_sum(own, from_below, from_above, low, high):
    return pl.pallas_call(
        last_sum_kernel,
        out_shape=jax.ShapeDtypeStruct((Y * X_HI * X_LO, 16, HEAD_DIM), jnp.bfloat16),
        in_specs=[VMEM] * 5,
        out_specs=VMEM,
        compiler_params=params(12),
        name="last_sum",
    )(own, from_below, from_above, low, high)


def columns_kernel(parts, keys, values):
    for head in range(Y * X_HI * X_LO):
        both = parts[head].astype(jnp.float32)
        at = pl.ds(head * HEAD_DIM, HEAD_DIM)
        keys[:, at] = both[:8].astype(jnp.bfloat16)
        values[:, at] = both[8:].astype(jnp.bfloat16)


def columns(parts):
    out = jax.ShapeDtypeStruct((8, parts.shape[0] * HEAD_DIM), jnp.bfloat16)
    return pl.pallas_call(
        columns_kernel,
        out_shape=(out, out),
        in_specs=[VMEM],
        out_specs=(VMEM, VMEM),
        compiler_params=params(12),
        name="columns",
    )(parts)


def sum_over_z(keep, came):
    above = lambda hops: lambda xl, z, y, xh, c: (xl, (z + hops) % Z, y, xh, c)
    over = lambda xl, z, y, xh, c: (xl, (z + (2 if c == 0 else 6)) % Z, y, xh, c)
    up, down, across, ahead, behind, own = core_sum(keep, came)
    from_below = permute(up, above(1))
    from_above = permute(down, above(7))
    far = permute(across, over)
    up, down = middle_sum(ahead, behind, from_below, from_above, far)
    low = permute(up, above(2))
    high = permute(down, above(6))
    return last_sum(own, from_below, from_above, low, high)


def nt(a, b):
    return lax.dot_general(a, b, (((1,), (1,)), ((), ())), preferred_element_type=jnp.float32)


def nn(a, b):
    return jnp.dot(a, b, preferred_element_type=jnp.float32)


def attention_kernel(
    queries, cotangents, own, other, rows_out, keep_ref, send_ref, s_ref, e_ref, ds_ref
):
    _, _, core = position()
    q = queries[...]
    do = cotangents[...]
    block = own.shape[2]
    chunks = [
        (source, at, chip)
        for source, at in ((own, core), (other, 1 - core))
        for chip in range(0, Y * X_HI, CHUNK_CHIPS)
    ]
    size = CHUNK_CHIPS * block
    places = [pl.ds(i * size, size) for i in range(len(chunks))]

    def rows_of(chunk, kind):
        source, _, chip = chunk
        return source[chip : chip + CHUNK_CHIPS, kind].reshape(size, HEAD_DIM)

    factor = LOG2E * SCALE
    top = None
    for chunk, rows in zip(chunks, places):
        s = nt(rows_of(chunk, 0), q)
        s_ref[rows, :] = s
        here = jnp.max(s, axis=0, keepdims=True)
        top = here if top is None else jnp.maximum(top, here)
    top = top * factor
    total = None
    att = None
    for chunk, rows in zip(chunks, places):
        e = jnp.exp2(s_ref[rows, :] * factor - top)
        here = jnp.sum(e, axis=0, keepdims=True)
        total = here if total is None else total + here
        eb = e.astype(jnp.bfloat16)
        e_ref[rows, :] = eb
        part = nn(rows_of(chunk, 1).T, eb)
        att = part if att is None else att + part
    inverse = 1.0 / total
    att = att * inverse
    rows_out[0] = att.T.astype(jnp.bfloat16)
    dot = (do.astype(jnp.float32).T * inverse).astype(jnp.bfloat16)
    delta = jnp.sum(att * dot.astype(jnp.float32), axis=0, keepdims=True)
    dos = dot.T
    dq = None
    for chunk, rows in zip(chunks, places):
        dp = nn(rows_of(chunk, 1), dot)
        ds = (e_ref[rows, :].astype(jnp.float32) * (dp - delta)).astype(jnp.bfloat16)
        ds_ref[rows, :] = ds
        part = nn(rows_of(chunk, 0).T, ds)
        dq = part if dq is None else dq + part
    rows_out[1] = (dq * SCALE).T.astype(jnp.bfloat16)
    first = core == 0
    for (_, side, first_chip), rows in zip(chunks, places):
        for kind, full in enumerate((nn(ds_ref[rows, :], q) * SCALE, nn(e_ref[rows, :], dos))):
            full = full.reshape(CHUNK_CHIPS, block // 16, 2, 8, HEAD_DIM)
            for i in range(CHUNK_CHIPS):
                xl, low_z = divmod(first_chip + i, Y * X_HI // X_LO)
                z = low_z * 2 + side
                low = full[i, :, 0].reshape(block // 2, HEAD_DIM)
                high = full[i, :, 1].reshape(block // 2, HEAD_DIM)
                at = pl.ds(xl * (block // 2), block // 2)
                keep_ref[z, kind, at, :] = jnp.where(first, low, high).astype(jnp.bfloat16)
                send_ref[z, kind, at, :] = jnp.where(first, high, low).astype(jnp.bfloat16)


def attention(queries, cotangents, own, other):
    rows = queries.shape[0]
    memory = 2 * own.shape[0] * own.shape[2]
    parts = (Z, 2, memory // (2 * Z), HEAD_DIM)
    bf16, f32 = jnp.bfloat16, jnp.float32
    return pl.pallas_call(
        attention_kernel,
        out_shape=(
            jax.ShapeDtypeStruct((2, rows, HEAD_DIM), bf16),
            jax.ShapeDtypeStruct(parts, bf16),
            jax.ShapeDtypeStruct(parts, bf16),
        ),
        in_specs=[VMEM] * 4,
        out_specs=(VMEM, VMEM, VMEM),
        scratch_shapes=[
            pltpu.VMEM((memory, rows), f32),
            pltpu.VMEM((memory, rows), bf16),
            pltpu.VMEM((memory, rows), bf16),
        ],
        compiler_params=params(24),
        cost_estimate=pl.CostEstimate(
            flops=12 * rows * memory * HEAD_DIM,
            bytes_accessed=8 * 1024 * 1024,
            transcendentals=rows * memory,
        ),
        name="attention",
    )(queries, cotangents, own, other)


def per_device(queries, mem_keys, mem_values, grad_out):
    q, do = select(queries, grad_out, trade(queries), trade(grad_out))
    own = exchange(pack(mem_keys, mem_values), head_groups())
    own, q, do = lax.optimization_barrier((own, q, do))
    other = permute(own, other_core)
    rows, keep, send = attention(q, do, own, other)
    came = permute(send, other_core)
    traded = trade(rows)
    sums = sum_over_z(keep, came)
    attended, query_gradients = unpack(rows, traded)
    grad_keys, grad_values = columns(exchange(sums, column_groups()))
    return attended, query_gradients, grad_keys, grad_values


def solution(mesh):
    in_specs = (P("query", "head"), P("head", None), P("head", None), P("query", "head"))
    out_specs = (
        P("query", "head"),
        P("query", "head"),
        P(("query", "head"), None),
        P(("query", "head"), None),
    )
    return jax.shard_map(
        per_device, mesh=mesh, in_specs=in_specs, out_specs=out_specs, check_vma=False
    )
```

time: 96.2 us -> 92 us (0.956)
  blocking collectives: 25.6 us -> 0 us
  waiting for transfers between devices: 25.3 us -> 42.3 us
  starting transfers between devices: 21.9 us -> 34.4 us
  Pallas kernels: 19.1 us -> 14.1 us
  local copies, waits for them, and re-layouts: 3.18 us -> 0.01 us
    all_to_all x1 -> x0, blocking collectives: 25.6 us -> none  [exchange(): lax.all_to_all(array, AXES, split_axis=0, concat_axis=0, axis_index_group...]
    all_to_all x1 -> x2, waiting for transfers between devices: 4.92 us -> 24 us  [exchange(): lax.all_to_all(array, AXES, split_axis=0, concat_axis=0, axis_index_group...]
    all_to_all x1 -> x2, starting transfers between devices: 3.51 us -> 16.1 us  [exchange(): lax.all_to_all(array, AXES, split_axis=0, concat_axis=0, axis_index_group...]
    pallas_call x1, Pallas kernels: 12.3 us -> 8.57 us  [attention(): pl.pallas_call(attention_kernel, out_shape=(jax.ShapeDtypeStruct((2, rows...]
    unnamed x10 -> x4, local copies, waits for them, and re-layouts: 3.18 us -> 0.01 us
    ppermute x7, waiting for transfers between devices: 20.4 us -> 18.3 us  [permute(): return lax.ppermute(array, AXES, pairs)]
    pallas_call x3 -> x4, Pallas kernels: 5.27 us -> 3.91 us  [the longest x1 2.61 us: pack(): pl.pallas_call(pack_kernel, out_shape=jax.ShapeDtypeStruct(shape, keys.dt...]
    ppermute x2 -> x3, starting transfers between devices: 1.44 us -> 2.1 us  [trade(): return lax.ppermute(array, AXES, pairs)]
  transfers between devices with their start and end apart: 10 -> 12, of which waited for: 6 -> 6; matrix products, arithmetic and copies ran while one was open for 0% -> 0% of each run, Pallas kernels for 3% -> 2%
where the time goes in v3:
time: 92 us; the launch traced here: 91.6 us
  waiting for transfers between devices  42.3 us (46%)
  starting transfers between devices  34.4 us (37%)
  Pallas kernels  14.1 us (15%)
    all_to_all x2, waiting for transfers between devices, exchange(): lax.all_to_all(array, AXES, split_axis=0, concat_axis=0, axis_index_group...  24 us
    ppermute x7, waiting for transfers between devices, permute(): return lax.ppermute(array, AXES, pairs)  18.3 us
    ppermute x7, starting transfers between devices, permute(): return lax.ppermute(array, AXES, pairs)  16.2 us
    all_to_all x2, starting transfers between devices, exchange(): lax.all_to_all(array, AXES, split_axis=0, concat_axis=0, axis_index_group...  16.1 us
    pallas_call x1, Pallas kernels, attention(): pl.pallas_call(attention_kernel, out_shape=(jax.ShapeDtypeStruct((2, rows...  8.57 us
    pallas_call x1, Pallas kernels, pack(): pl.pallas_call(pack_kernel, out_shape=jax.ShapeDtypeStruct(shape, keys.dt...  2.61 us
    ppermute x3, starting transfers between devices, trade(): return lax.ppermute(array, AXES, pairs)  2.1 us
  transfers between devices with their start and end apart: 12, of which 6 were waited for; matrix products, arithmetic and copies ran while one was open for 0% of the time, Pallas kernels for 2%

profile of v3, /device:TPU:32, one launch (start us, length us, event | category | flops | bytes accessed | tf_op | source)
XLA Modules:
  0.0 91.6 jit_solution(7585761737563295248)
XLA Ops:
  0.6 2.6 %pack.1 = bf16[8,2,128,256]{3,2,1,0:T(8,128)(2,1)} custom-call(bf16[128,4096]{1,0:T(8,128)(2,1)} %keys.1, bf16[128,4096]{1,0:T(8,128)(2,1)} %values.1), custom_call_target="tpu_custom_call" | custom-call | tf_op jit(solution)/shard_map/pack/pallas_call | solution.py:96
  3.2 0.0 copy-start
  3.3 0.0 copy-start.1
  3.3 7.1 %all-to-all-start = ((bf16[8,2,128,256]{3,2,1,0:T(8,128)(2,1)}), bf16[8,2,128,256]{3,2,1,0:T(8,128)(2,1)S(1)}, u32[]{:S(2)}, u32[]{:S(2)}) async-start(bf16[8,2,128,256]{3,2,1,0:T(8,128)(2,1)} %pack.1), calls=%async_computation | async-start | bytes 2097152 | tf_op jit(solution)/shard_map/all_to_all | solution.py:37
  10.4 0.7 collective-permute-start
  11.1 0.7 collective-permute-start.1
  11.8 0.0 collective-permute-done.1.do_came
  11.8 0.1 select.1
  11.9 17.1 %all-to-all-done.own = bf16[8,2,128,256]{3,2,1,0:T(8,128)(2,1)S(1)} async-done(((bf16[8,2,128,256]{3,2,1,0:T(8,128)(2,1)}), bf16[8,2,128,256]{3,2,1,0:T(8,128)(2,1)S(1)}, u32[]{:S(2)}, u32[]{:S(2)}) %all-to-all-start) | async-done | bytes 1048608 | tf_op jit(solution)/shard_map/all_to_all | solution.py:37
  29.0 5.0 %collective-permute-start.2 = (bf16[8,2,128,256]{3,2,1,0:T(8,128)(2,1)S(1)}, bf16[8,2,128,256]{3,2,1,0:T(8,128)(2,1)S(1)}, u32[]{:S(2)}, u32[]{:S(2)}) collective-permute-start(bf16[8,2,128,256]{3,2,1,0:T(8,128)(2,1)S(1)} %all-to-all-done.own), channel_id=1, source_target_pairs={{0,1},{1,0},{2,3},{3,2},{4,5},{5,4},{6,7},{7,6},{8,9},{9,8},{10,11... | collective-permute-start | bytes 3145736 | tf_op jit(solution)/shard_map/ppermute | solution.py:33
  34.1 2.3 %collective-permute-done.2.other = bf16[8,2,128,256]{3,2,1,0:T(8,128)(2,1)S(1)} collective-permute-done((bf16[8,2,128,256]{3,2,1,0:T(8,128)(2,1)S(1)}, bf16[8,2,128,256]{3,2,1,0:T(8,128)(2,1)S(1)}, u32[]{:S(2)}, u32[]{:S(2)}) %collective-permute-start.2) | collective-permute-done | bytes 1048608 | tf_op jit(solution)/shard_map/ppermute | solution.py:33
  36.3 8.6 %attention.1 = (bf16[2,1024,256]{2,1,0:T(8,128)(2,1)S(1)}, bf16[8,2,128,256]{3,2,1,0:T(8,128)(2,1)S(1)}, bf16[8,2,128,256]{3,2,1,0:T(8,128)(2,1)S(1)}) custom-call(bf16[1024,256]{1,0:T(8,128)(2,1)S(1)} %get-tuple-element.26.queries, bf16[1024,256]{1,0:T(8,128)(2,1)S(1)} %get-tuple-element.27.cotangents, bf16[8,2,128,256]{3,2,1,0:T(8,128)(2,1)S(1)} %all-to-all-done.own, ...), custom_call_target="tpu_custom_call" | custom-call | flops 6442450944 | bytes 8388608 | tf_op jit(solution)/shard_map/attention/pallas_call | solution.py:342
  44.9 0.5 collective-permute-start.4
  45.4 0.7 collective-permute-start.3
  46.1 1.6 %collective-permute-done.4.came = bf16[8,2,128,256]{3,2,1,0:T(8,128)(2,1)S(1)} collective-permute-done((bf16[8,2,128,256]{3,2,1,0:T(8,128)(2,1)S(1)}, bf16[8,2,128,256]{3,2,1,0:T(8,128)(2,1)S(1)}, u32[]{:S(2)}, u32[]{:S(2)}) %collective-permute-start.4) | collective-permute-done | bytes 1048608 | tf_op jit(solution)/shard_map/ppermute | solution.py:33
  47.7 0.2 core_sum.1
  47.9 2.0 %collective-permute-start.5 = (bf16[2,2,128,256]{3,2,1,0:T(8,128)(2,1)S(1)}, bf16[2,2,128,256]{3,2,1,0:T(8,128)(2,1)S(1)}, u32[]{:S(2)}, u32[]{:S(2)}) collective-permute-start(bf16[2,2,128,256]{3,2,1,0:T(8,128)(2,1)S(1)} %get-tuple-element.35), channel_id=1, source_target_pairs={{0,16},{1,17},{2,18},{3,19},{4,20},{5,21},{6,22},{7,23},{8,24},{9,... | collective-permute-start | bytes 786440 | tf_op jit(solution)/shard_map/ppermute | solution.py:33
  49.9 0.1 collective-permute-start.6
  50.0 4.4 %collective-permute-start.7 = (bf16[2,128,256]{2,1,0:T(8,128)(2,1)S(1)}, bf16[2,128,256]{2,1,0:T(8,128)(2,1)S(1)}, u32[]{:S(2)}, u32[]{:S(2)}) collective-permute-start(bf16[2,128,256]{2,1,0:T(8,128)(2,1)S(1)} %get-tuple-element.39), channel_id=1, source_target_pairs={{0,32},{1,97},{2,34},{3,99},{4,36},{5,101},{6,38},{7,103},{8,40},{... | collective-permute-start | bytes 393224 | tf_op jit(solution)/shard_map/ppermute | solution.py:33
  54.4 7.9 %collective-permute-done.7.across = bf16[2,128,256]{2,1,0:T(8,128)(2,1)S(1)} collective-permute-done((bf16[2,128,256]{2,1,0:T(8,128)(2,1)S(1)}, bf16[2,128,256]{2,1,0:T(8,128)(2,1)S(1)}, u32[]{:S(2)}, u32[]{:S(2)}) %collective-permute-start.7) | collective-permute-done | bytes 131104 | tf_op jit(solution)/shard_map/ppermute | solution.py:33
  62.3 0.0 collective-permute-done.5.from_below
  62.3 0.1 middle_sum.1
  62.4 2.9 %collective-permute-start.8 = (bf16[2,128,256]{2,1,0:T(8,128)(2,1)S(1)}, bf16[2,128,256]{2,1,0:T(8,128)(2,1)S(1)}, u32[]{:S(2)}, u32[]{:S(2)}) collective-permute-start(bf16[2,128,256]{2,1,0:T(8,128)(2,1)S(1)} %get-tuple-element.40), channel_id=1, source_target_pairs={{0,32},{1,33},{2,34},{3,35},{4,36},{5,37},{6,38},{7,39},{8,40},{9,... | collective-permute-start | bytes 393224 | tf_op jit(solution)/shard_map/ppermute | solution.py:33
  65.3 1.3 %collective-permute-start.9 = (bf16[2,128,256]{2,1,0:T(8,128)(2,1)S(1)}, bf16[2,128,256]{2,1,0:T(8,128)(2,1)S(1)}, u32[]{:S(2)}, u32[]{:S(2)}) collective-permute-start(bf16[2,128,256]{2,1,0:T(8,128)(2,1)S(1)} %get-tuple-element.41), channel_id=1, source_target_pairs={{0,96},{1,97},{2,98},{3,99},{4,100},{5,101},{6,102},{7,103},{8,104... | collective-permute-start | bytes 393224 | tf_op jit(solution)/shard_map/ppermute | solution.py:33
  66.6 6.6 %collective-permute-done.8.low = bf16[2,128,256]{2,1,0:T(8,128)(2,1)S(1)} collective-permute-done((bf16[2,128,256]{2,1,0:T(8,128)(2,1)S(1)}, bf16[2,128,256]{2,1,0:T(8,128)(2,1)S(1)}, u32[]{:S(2)}, u32[]{:S(2)}) %collective-permute-start.8) | collective-permute-done | bytes 131104 | tf_op jit(solution)/shard_map/ppermute | solution.py:33
  73.2 0.0 collective-permute-done.9.high
  73.2 0.7 last_sum.1
  73.9 9.0 %all-to-all-start.1 = ((bf16[16,16,256]{2,1,0:T(8,128)(2,1)}), bf16[16,16,256]{2,1,0:T(8,128)(2,1)S(1)}, u32[]{:S(2)}, u32[]{:S(2)}) async-start(bf16[16,16,256]{2,1,0:T(8,128)(2,1)} %last_sum.1), calls=%async_computation.1 | async-start | bytes 262144 | tf_op jit(solution)/shard_map/all_to_all | solution.py:37
  83.0 0.0 collective-permute-done.3.came
  83.0 1.1 %unpack.1 = (bf16[1024,256]{1,0:T(8,128)(2,1)}, bf16[1024,256]{1,0:T(8,128)(2,1)}) custom-call(bf16[2,1024,256]{2,1,0:T(8,128)(2,1)S(1)} %get-tuple-element.29.mine, bf16[2,1024,256]{2,1,0:T(8,128)(2,1)S(1)} %collective-permute-done.3.came), custom_call_target="tpu_custom_call" | custom-call | tf_op jit(solution)/shard_map/unpack/pallas_call | solution.py:139
  84.0 6.9 %all-to-all-done.1.parts = bf16[16,16,256]{2,1,0:T(8,128)(2,1)S(1)} async-done(((bf16[16,16,256]{2,1,0:T(8,128)(2,1)}), bf16[16,16,256]{2,1,0:T(8,128)(2,1)S(1)}, u32[]{:S(2)}, u32[]{:S(2)}) %all-to-all-start.1) | async-done | bytes 131104 | tf_op jit(solution)/shard_map/all_to_all | solution.py:37
  90.9 0.7 columns.1
  (4 shorter events, 0.0 us)
Async XLA Ops:
  3.2 7.1 %copy-start = (bf16[1024,256]{1,0:T(8,128)(2,1)S(1)}, bf16[1024,256]{1,0:T(8,128)(2,1)}, u32[]{:S(2)}) copy-start(bf16[1024,256]{1,0:T(8,128)(2,1)} %queries.1) | copy-start | bytes 1572868
  3.3 7.8 %copy-start.1 = (bf16[1024,256]{1,0:T(8,128)(2,1)S(1)}, bf16[1024,256]{1,0:T(8,128)(2,1)}, u32[]{:S(2)}) copy-start(bf16[1024,256]{1,0:T(8,128)(2,1)} %cotangents.1) | copy-start | bytes 1572868
  3.3 25.7 %all-to-all-start = ((bf16[8,2,128,256]{3,2,1,0:T(8,128)(2,1)}), bf16[8,2,128,256]{3,2,1,0:T(8,128)(2,1)S(1)}, u32[]{:S(2)}, u32[]{:S(2)}) async-start(bf16[8,2,128,256]{3,2,1,0:T(8,128)(2,1)} %pack.1), calls=%async_computation | async-start | bytes 2097152 | tf_op jit(solution)/shard_map/all_to_all | solution.py:37
  10.4 1.4 %collective-permute-start = (bf16[1024,256]{1,0:T(8,128)(2,1)S(1)}, bf16[1024,256]{1,0:T(8,128)(2,1)S(1)}, u32[]{:S(2)}, u32[]{:S(2)}) collective-permute-start(bf16[1024,256]{1,0:T(8,128)(2,1)S(1)} %copy-done), channel_id=1, source_target_pairs={{1,128},{128,1},{3,130},{130,3},{5,132},{132,5},{7,134},{134,7},{9... | collective-permute-start | bytes 1572872 | tf_op jit(solution)/shard_map/ppermute | solution.py:47
  11.1 0.7 collective-permute-start.1
  29.0 7.3 %collective-permute-start.2 = (bf16[8,2,128,256]{3,2,1,0:T(8,128)(2,1)S(1)}, bf16[8,2,128,256]{3,2,1,0:T(8,128)(2,1)S(1)}, u32[]{:S(2)}, u32[]{:S(2)}) collective-permute-start(bf16[8,2,128,256]{3,2,1,0:T(8,128)(2,1)S(1)} %all-to-all-done.own), channel_id=1, source_target_pairs={{0,1},{1,0},{2,3},{3,2},{4,5},{5,4},{6,7},{7,6},{8,9},{9,8},{10,11... | collective-permute-start | bytes 3145736 | tf_op jit(solution)/shard_map/ppermute | solution.py:33
  44.9 2.7 %collective-permute-start.4 = (bf16[8,2,128,256]{3,2,1,0:T(8,128)(2,1)S(1)}, bf16[8,2,128,256]{3,2,1,0:T(8,128)(2,1)S(1)}, u32[]{:S(2)}, u32[]{:S(2)}) collective-permute-start(bf16[8,2,128,256]{3,2,1,0:T(8,128)(2,1)S(1)} %get-tuple-element.33), channel_id=1, source_target_pairs={{0,1},{1,0},{2,3},{3,2},{4,5},{5,4},{6,7},{7,6},{8,9},{9,8},{10,11... | collective-permute-start | bytes 3145736 | tf_op jit(solution)/shard_map/ppermute | solution.py:33
  45.4 37.6 %collective-permute-start.3 = (bf16[2,1024,256]{2,1,0:T(8,128)(2,1)S(1)}, bf16[2,1024,256]{2,1,0:T(8,128)(2,1)S(1)}, u32[]{:S(2)}, u32[]{:S(2)}) collective-permute-start(bf16[2,1024,256]{2,1,0:T(8,128)(2,1)S(1)} %get-tuple-element.29.mine), channel_id=1, source_target_pairs={{1,128},{128,1},{3,130},{130,3},{5,132},{132,5},{7,134},{134,7},{9... | collective-permute-start | bytes 3145736 | tf_op jit(solution)/shard_map/ppermute | solution.py:47
  47.9 14.4 %collective-permute-start.5 = (bf16[2,2,128,256]{3,2,1,0:T(8,128)(2,1)S(1)}, bf16[2,2,128,256]{3,2,1,0:T(8,128)(2,1)S(1)}, u32[]{:S(2)}, u32[]{:S(2)}) collective-permute-start(bf16[2,2,128,256]{3,2,1,0:T(8,128)(2,1)S(1)} %get-tuple-element.35), channel_id=1, source_target_pairs={{0,16},{1,17},{2,18},{3,19},{4,20},{5,21},{6,22},{7,23},{8,24},{9,... | collective-permute-start | bytes 786440 | tf_op jit(solution)/shard_map/ppermute | solution.py:33
  49.9 12.3 %collective-permute-start.6 = (bf16[2,2,128,256]{3,2,1,0:T(8,128)(2,1)S(1)}, bf16[2,2,128,256]{3,2,1,0:T(8,128)(2,1)S(1)}, u32[]{:S(2)}, u32[]{:S(2)}) collective-permute-start(bf16[2,2,128,256]{3,2,1,0:T(8,128)(2,1)S(1)} %get-tuple-element.36), channel_id=1, source_target_pairs={{0,112},{1,113},{2,114},{3,115},{4,116},{5,117},{6,118},{7,119},{8... | collective-permute-start | bytes 786440 | tf_op jit(solution)/shard_map/ppermute | solution.py:33
  50.0 12.2 %collective-permute-start.7 = (bf16[2,128,256]{2,1,0:T(8,128)(2,1)S(1)}, bf16[2,128,256]{2,1,0:T(8,128)(2,1)S(1)}, u32[]{:S(2)}, u32[]{:S(2)}) collective-permute-start(bf16[2,128,256]{2,1,0:T(8,128)(2,1)S(1)} %get-tuple-element.39), channel_id=1, source_target_pairs={{0,32},{1,97},{2,34},{3,99},{4,36},{5,101},{6,38},{7,103},{8,40},{... | collective-permute-start | bytes 393224 | tf_op jit(solution)/shard_map/ppermute | solution.py:33
  62.4 10.8 %collective-permute-start.8 = (bf16[2,128,256]{2,1,0:T(8,128)(2,1)S(1)}, bf16[2,128,256]{2,1,0:T(8,128)(2,1)S(1)}, u32[]{:S(2)}, u32[]{:S(2)}) collective-permute-start(bf16[2,128,256]{2,1,0:T(8,128)(2,1)S(1)} %get-tuple-element.40), channel_id=1, source_target_pairs={{0,32},{1,33},{2,34},{3,35},{4,36},{5,37},{6,38},{7,39},{8,40},{9,... | collective-permute-start | bytes 393224 | tf_op jit(solution)/shard_map/ppermute | solution.py:33
  65.3 7.9 %collective-permute-start.9 = (bf16[2,128,256]{2,1,0:T(8,128)(2,1)S(1)}, bf16[2,128,256]{2,1,0:T(8,128)(2,1)S(1)}, u32[]{:S(2)}, u32[]{:S(2)}) collective-permute-start(bf16[2,128,256]{2,1,0:T(8,128)(2,1)S(1)} %get-tuple-element.41), channel_id=1, source_target_pairs={{0,96},{1,97},{2,98},{3,99},{4,100},{5,101},{6,102},{7,103},{8,104... | collective-permute-start | bytes 393224 | tf_op jit(solution)/shard_map/ppermute | solution.py:33
  73.9 17.0 %all-to-all-start.1 = ((bf16[16,16,256]{2,1,0:T(8,128)(2,1)}), bf16[16,16,256]{2,1,0:T(8,128)(2,1)S(1)}, u32[]{:S(2)}, u32[]{:S(2)}) async-start(bf16[16,16,256]{2,1,0:T(8,128)(2,1)} %last_sum.1), calls=%async_computation.1 | async-start | bytes 262144 | tf_op jit(solution)/shard_map/all_to_all | solution.py:37

commit v4 on v3

--- a/solution.py
+++ b/solution.py
@@ -121,6 +121,7 @@
         out_shape=(out, out),
         in_specs=[VMEM] * 4,
         out_specs=(VMEM, VMEM),
+        input_output_aliases={2: 0, 3: 1},
         compiler_params=params(8),
         cost_estimate=pl.CostEstimate(flops=0, bytes_accessed=3 * 1024 * 1024, transcendentals=0),
         name="select",
@@ -364,7 +365,9 @@
 
 
 def per_device(queries, mem_keys, mem_values, grad_out):
-    q, do = select(queries, grad_out, trade(queries), trade(grad_out))
+    q_came = trade(queries)
+    grad_out, q_came = lax.optimization_barrier((grad_out, q_came))
+    q, do = select(queries, grad_out, q_came, trade(grad_out))
     own = exchange(pack(mem_keys, mem_values), head_groups())
     own, q, do = lax.optimization_barrier((own, q, do))
     other = permute(own, other_core)

time: 92 us -> 88.6 us (0.963)
  starting transfers between devices: 34.4 us -> 32.2 us
  waiting for transfers between devices: 42.3 us -> 41.1 us
    ppermute x7, starting transfers between devices: 16.2 us -> 12.4 us  [permute(): return lax.ppermute(array, AXES, pairs)]
    all_to_all x2, starting transfers between devices: 16.1 us -> 17.7 us  [exchange(): lax.all_to_all(array, AXES, split_axis=0, concat_axis=0, axis_index_group...]
  transfers between devices with their start and end apart: 12 -> 12, of which waited for: 6 -> 7; matrix products, arithmetic and copies ran while one was open for 0% -> 0% of each run, Pallas kernels for 2% -> 6%
where the time goes in v4:
time: 88.6 us; the launch traced here: 88.3 us
  waiting for transfers between devices  41.1 us (46%)
  starting transfers between devices  32.2 us (36%)
  Pallas kernels  14.2 us (16%)
    all_to_all x2, waiting for transfers between devices, exchange(): lax.all_to_all(array, AXES, split_axis=0, concat_axis=0, axis_index_group...  23.3 us
    ppermute x7, waiting for transfers between devices, permute(): return lax.ppermute(array, AXES, pairs)  17.8 us
    all_to_all x2, starting transfers between devices, exchange(): lax.all_to_all(array, AXES, split_axis=0, concat_axis=0, axis_index_group...  17.7 us
    ppermute x7, starting transfers between devices, permute(): return lax.ppermute(array, AXES, pairs)  12.4 us
    pallas_call x1, Pallas kernels, attention(): pl.pallas_call(attention_kernel, out_shape=(jax.ShapeDtypeStruct((2, rows...  8.58 us
    pallas_call x1, Pallas kernels, pack(): pl.pallas_call(pack_kernel, out_shape=jax.ShapeDtypeStruct(shape, keys.dt...  2.61 us
    ppermute x3, starting transfers between devices, trade(): return lax.ppermute(array, AXES, pairs)  2.1 us
  transfers between devices with their start and end apart: 12, of which 7 were waited for; matrix products, arithmetic and copies ran while one was open for 0% of the time, Pallas kernels for 6%

profile of v4, /device:TPU:32, one launch (start us, length us, event | category | flops | bytes accessed | tf_op | source)
XLA Modules:
  0.0 88.3 jit_solution(11265531459036942040)
XLA Ops:
  0.6 0.7 collective-permute-start
  1.3 2.6 %pack.1 = bf16[8,2,128,256]{3,2,1,0:T(8,128)(2,1)} custom-call(bf16[128,4096]{1,0:T(8,128)(2,1)} %keys.1, bf16[128,4096]{1,0:T(8,128)(2,1)} %values.1), custom_call_target="tpu_custom_call" | custom-call | tf_op jit(solution)/shard_map/pack/pallas_call | solution.py:96
  4.0 0.0 copy-start.1
  4.0 0.0 copy-start
  4.0 7.1 %all-to-all-start = ((bf16[8,2,128,256]{3,2,1,0:T(8,128)(2,1)}), bf16[8,2,128,256]{3,2,1,0:T(8,128)(2,1)S(1)}, u32[]{:S(2)}, u32[]{:S(2)}) async-start(bf16[8,2,128,256]{3,2,1,0:T(8,128)(2,1)} %pack.1), calls=%async_computation | async-start | bytes 2097152 | tf_op jit(solution)/shard_map/all_to_all | solution.py:37
  11.1 0.0 collective-permute-done.q_came
  11.1 0.7 collective-permute-start.1
  11.8 0.0 collective-permute-done.1.do_came
  11.8 0.2 select.1
  12.0 16.4 %all-to-all-done.own = bf16[8,2,128,256]{3,2,1,0:T(8,128)(2,1)S(1)} async-done(((bf16[8,2,128,256]{3,2,1,0:T(8,128)(2,1)}), bf16[8,2,128,256]{3,2,1,0:T(8,128)(2,1)S(1)}, u32[]{:S(2)}, u32[]{:S(2)}) %all-to-all-start) | async-done | bytes 1048608 | tf_op jit(solution)/shard_map/all_to_all | solution.py:37
  28.4 1.2 %collective-permute-start.2 = (bf16[8,2,128,256]{3,2,1,0:T(8,128)(2,1)S(1)}, bf16[8,2,128,256]{3,2,1,0:T(8,128)(2,1)S(1)}, u32[]{:S(2)}, u32[]{:S(2)}) collective-permute-start(bf16[8,2,128,256]{3,2,1,0:T(8,128)(2,1)S(1)} %all-to-all-done.own), channel_id=1, source_target_pairs={{0,1},{1,0},{2,3},{3,2},{4,5},{5,4},{6,7},{7,6},{8,9},{9,8},{10,11... | collective-permute-start | bytes 3145736 | tf_op jit(solution)/shard_map/ppermute | solution.py:33
  29.6 2.3 %collective-permute-done.2.other = bf16[8,2,128,256]{3,2,1,0:T(8,128)(2,1)S(1)} collective-permute-done((bf16[8,2,128,256]{3,2,1,0:T(8,128)(2,1)S(1)}, bf16[8,2,128,256]{3,2,1,0:T(8,128)(2,1)S(1)}, u32[]{:S(2)}, u32[]{:S(2)}) %collective-permute-start.2) | collective-permute-done | bytes 1048608 | tf_op jit(solution)/shard_map/ppermute | solution.py:33
  31.9 8.6 %attention.1 = (bf16[2,1024,256]{2,1,0:T(8,128)(2,1)S(1)}, bf16[8,2,128,256]{3,2,1,0:T(8,128)(2,1)S(1)}, bf16[8,2,128,256]{3,2,1,0:T(8,128)(2,1)S(1)}) custom-call(bf16[1024,256]{1,0:T(8,128)(2,1)S(1)} %get-tuple-element.30.queries, bf16[1024,256]{1,0:T(8,128)(2,1)S(1)} %get-tuple-element.31.cotangents, bf16[8,2,128,256]{3,2,1,0:T(8,128)(2,1)S(1)} %all-to-all-done.own, ...), custom_call_target="tpu_custom_call" | custom-call | flops 6442450944 | bytes 8388608 | tf_op jit(solution)/shard_map/attention/pallas_call | solution.py:343
  40.5 0.5 collective-permute-start.4
  40.9 0.7 collective-permute-start.3
  41.7 1.6 %collective-permute-done.4.came = bf16[8,2,128,256]{3,2,1,0:T(8,128)(2,1)S(1)} collective-permute-done((bf16[8,2,128,256]{3,2,1,0:T(8,128)(2,1)S(1)}, bf16[8,2,128,256]{3,2,1,0:T(8,128)(2,1)S(1)}, u32[]{:S(2)}, u32[]{:S(2)}) %collective-permute-start.4) | collective-permute-done | bytes 1048608 | tf_op jit(solution)/shard_map/ppermute | solution.py:33
  43.2 0.2 core_sum.1
  43.4 2.0 %collective-permute-start.5 = (bf16[2,2,128,256]{3,2,1,0:T(8,128)(2,1)S(1)}, bf16[2,2,128,256]{3,2,1,0:T(8,128)(2,1)S(1)}, u32[]{:S(2)}, u32[]{:S(2)}) collective-permute-start(bf16[2,2,128,256]{3,2,1,0:T(8,128)(2,1)S(1)} %get-tuple-element.39), channel_id=1, source_target_pairs={{0,16},{1,17},{2,18},{3,19},{4,20},{5,21},{6,22},{7,23},{8,24},{9,... | collective-permute-start | bytes 786440 | tf_op jit(solution)/shard_map/ppermute | solution.py:33
  45.4 0.1 collective-permute-start.6
  45.6 4.4 %collective-permute-start.7 = (bf16[2,128,256]{2,1,0:T(8,128)(2,1)S(1)}, bf16[2,128,256]{2,1,0:T(8,128)(2,1)S(1)}, u32[]{:S(2)}, u32[]{:S(2)}) collective-permute-start(bf16[2,128,256]{2,1,0:T(8,128)(2,1)S(1)} %get-tuple-element.43), channel_id=1, source_target_pairs={{0,32},{1,97},{2,34},{3,99},{4,36},{5,101},{6,38},{7,103},{8,40},{... | collective-permute-start | bytes 393224 | tf_op jit(solution)/shard_map/ppermute | solution.py:33
  49.9 7.9 %collective-permute-done.7.across = bf16[2,128,256]{2,1,0:T(8,128)(2,1)S(1)} collective-permute-done((bf16[2,128,256]{2,1,0:T(8,128)(2,1)S(1)}, bf16[2,128,256]{2,1,0:T(8,128)(2,1)S(1)}, u32[]{:S(2)}, u32[]{:S(2)}) %collective-permute-start.7) | collective-permute-done | bytes 131104 | tf_op jit(solution)/shard_map/ppermute | solution.py:33
  57.9 0.0 collective-permute-done.5.from_below
  57.9 0.1 middle_sum.1
  58.0 1.6 %collective-permute-start.8 = (bf16[2,128,256]{2,1,0:T(8,128)(2,1)S(1)}, bf16[2,128,256]{2,1,0:T(8,128)(2,1)S(1)}, u32[]{:S(2)}, u32[]{:S(2)}) collective-permute-start(bf16[2,128,256]{2,1,0:T(8,128)(2,1)S(1)} %get-tuple-element.44), channel_id=1, source_target_pairs={{0,32},{1,33},{2,34},{3,35},{4,36},{5,37},{6,38},{7,39},{8,40},{9,... | collective-permute-start | bytes 393224 | tf_op jit(solution)/shard_map/ppermute | solution.py:33
  59.6 2.6 %collective-permute-start.9 = (bf16[2,128,256]{2,1,0:T(8,128)(2,1)S(1)}, bf16[2,128,256]{2,1,0:T(8,128)(2,1)S(1)}, u32[]{:S(2)}, u32[]{:S(2)}) collective-permute-start(bf16[2,128,256]{2,1,0:T(8,128)(2,1)S(1)} %get-tuple-element.45), channel_id=1, source_target_pairs={{0,96},{1,97},{2,98},{3,99},{4,100},{5,101},{6,102},{7,103},{8,104... | collective-permute-start | bytes 393224 | tf_op jit(solution)/shard_map/ppermute | solution.py:33
  62.2 5.5 %collective-permute-done.8.low = bf16[2,128,256]{2,1,0:T(8,128)(2,1)S(1)} collective-permute-done((bf16[2,128,256]{2,1,0:T(8,128)(2,1)S(1)}, bf16[2,128,256]{2,1,0:T(8,128)(2,1)S(1)}, u32[]{:S(2)}, u32[]{:S(2)}) %collective-permute-start.8) | collective-permute-done | bytes 131104 | tf_op jit(solution)/shard_map/ppermute | solution.py:33
  67.7 0.6 collective-permute-done.9.high
  68.2 0.7 last_sum.1
  69.0 10.7 %all-to-all-start.1 = ((bf16[16,16,256]{2,1,0:T(8,128)(2,1)}), bf16[16,16,256]{2,1,0:T(8,128)(2,1)S(1)}, u32[]{:S(2)}, u32[]{:S(2)}) async-start(bf16[16,16,256]{2,1,0:T(8,128)(2,1)} %last_sum.1), calls=%async_computation.1 | async-start | bytes 262144 | tf_op jit(solution)/shard_map/all_to_all | solution.py:37
  79.6 1.1 %unpack.1 = (bf16[1024,256]{1,0:T(8,128)(2,1)}, bf16[1024,256]{1,0:T(8,128)(2,1)}) custom-call(bf16[2,1024,256]{2,1,0:T(8,128)(2,1)S(1)} %get-tuple-element.33.mine, bf16[2,1024,256]{2,1,0:T(8,128)(2,1)S(1)} %collective-permute-done.3.came), custom_call_target="tpu_custom_call" | custom-call | tf_op jit(solution)/shard_map/unpack/pallas_call | solution.py:140
  80.7 6.9 %all-to-all-done.1.parts = bf16[16,16,256]{2,1,0:T(8,128)(2,1)S(1)} async-done(((bf16[16,16,256]{2,1,0:T(8,128)(2,1)}), bf16[16,16,256]{2,1,0:T(8,128)(2,1)S(1)}, u32[]{:S(2)}, u32[]{:S(2)}) %all-to-all-start.1) | async-done | bytes 131104 | tf_op jit(solution)/shard_map/all_to_all | solution.py:37
  87.6 0.7 columns.1
  (4 shorter events, 0.0 us)
Async XLA Ops:
  0.6 10.4 %collective-permute-start = (bf16[1024,256]{1,0:T(8,128)(2,1)}, bf16[1024,256]{1,0:T(8,128)(2,1)S(1)}, u32[]{:S(2)}, u32[]{:S(2)}) collective-permute-start(bf16[1024,256]{1,0:T(8,128)(2,1)} %queries.1), channel_id=1, source_target_pairs={{1,128},{128,1},{3,130},{130,3},{5,132},{132,5},{7,134},{134,7},{9... | collective-permute-start | bytes 1572872 | tf_op jit(solution)/shard_map/ppermute | solution.py:47
  4.0 7.1 %copy-start.1 = (bf16[1024,256]{1,0:T(8,128)(2,1)S(1)}, bf16[1024,256]{1,0:T(8,128)(2,1)}, u32[]{:S(2)}) copy-start(bf16[1024,256]{1,0:T(8,128)(2,1)} %cotangents) | copy-start | bytes 1572868
  4.0 7.8 %copy-start = (bf16[1024,256]{1,0:T(8,128)(2,1)S(1)}, bf16[1024,256]{1,0:T(8,128)(2,1)}, u32[]{:S(2)}) copy-start(bf16[1024,256]{1,0:T(8,128)(2,1)} %queries.1) | copy-start | bytes 1572868
  4.0 24.4 %all-to-all-start = ((bf16[8,2,128,256]{3,2,1,0:T(8,128)(2,1)}), bf16[8,2,128,256]{3,2,1,0:T(8,128)(2,1)S(1)}, u32[]{:S(2)}, u32[]{:S(2)}) async-start(bf16[8,2,128,256]{3,2,1,0:T(8,128)(2,1)} %pack.1), calls=%async_computation | async-start | bytes 2097152 | tf_op jit(solution)/shard_map/all_to_all | solution.py:37
  11.1 0.7 collective-permute-start.1
  28.4 3.5 %collective-permute-start.2 = (bf16[8,2,128,256]{3,2,1,0:T(8,128)(2,1)S(1)}, bf16[8,2,128,256]{3,2,1,0:T(8,128)(2,1)S(1)}, u32[]{:S(2)}, u32[]{:S(2)}) collective-permute-start(bf16[8,2,128,256]{3,2,1,0:T(8,128)(2,1)S(1)} %all-to-all-done.own), channel_id=1, source_target_pairs={{0,1},{1,0},{2,3},{3,2},{4,5},{5,4},{6,7},{7,6},{8,9},{9,8},{10,11... | collective-permute-start | bytes 3145736 | tf_op jit(solution)/shard_map/ppermute | solution.py:33
  40.5 2.7 %collective-permute-start.4 = (bf16[8,2,128,256]{3,2,1,0:T(8,128)(2,1)S(1)}, bf16[8,2,128,256]{3,2,1,0:T(8,128)(2,1)S(1)}, u32[]{:S(2)}, u32[]{:S(2)}) collective-permute-start(bf16[8,2,128,256]{3,2,1,0:T(8,128)(2,1)S(1)} %get-tuple-element.37), channel_id=1, source_target_pairs={{0,1},{1,0},{2,3},{3,2},{4,5},{5,4},{6,7},{7,6},{8,9},{9,8},{10,11... | collective-permute-start | bytes 3145736 | tf_op jit(solution)/shard_map/ppermute | solution.py:33
  40.9 38.7 %collective-permute-start.3 = (bf16[2,1024,256]{2,1,0:T(8,128)(2,1)S(1)}, bf16[2,1024,256]{2,1,0:T(8,128)(2,1)S(1)}, u32[]{:S(2)}, u32[]{:S(2)}) collective-permute-start(bf16[2,1024,256]{2,1,0:T(8,128)(2,1)S(1)} %get-tuple-element.33.mine), channel_id=1, source_target_pairs={{1,128},{128,1},{3,130},{130,3},{5,132},{132,5},{7,134},{134,7},{9... | collective-permute-start | bytes 3145736 | tf_op jit(solution)/shard_map/ppermute | solution.py:47
  43.4 14.4 %collective-permute-start.5 = (bf16[2,2,128,256]{3,2,1,0:T(8,128)(2,1)S(1)}, bf16[2,2,128,256]{3,2,1,0:T(8,128)(2,1)S(1)}, u32[]{:S(2)}, u32[]{:S(2)}) collective-permute-start(bf16[2,2,128,256]{3,2,1,0:T(8,128)(2,1)S(1)} %get-tuple-element.39), channel_id=1, source_target_pairs={{0,16},{1,17},{2,18},{3,19},{4,20},{5,21},{6,22},{7,23},{8,24},{9,... | collective-permute-start | bytes 786440 | tf_op jit(solution)/shard_map/ppermute | solution.py:33
  45.4 12.4 %collective-permute-start.6 = (bf16[2,2,128,256]{3,2,1,0:T(8,128)(2,1)S(1)}, bf16[2,2,128,256]{3,2,1,0:T(8,128)(2,1)S(1)}, u32[]{:S(2)}, u32[]{:S(2)}) collective-permute-start(bf16[2,2,128,256]{3,2,1,0:T(8,128)(2,1)S(1)} %get-tuple-element.40), channel_id=1, source_target_pairs={{0,112},{1,113},{2,114},{3,115},{4,116},{5,117},{6,118},{7,119},{8... | collective-permute-start | bytes 786440 | tf_op jit(solution)/shard_map/ppermute | solution.py:33
  45.6 12.3 %collective-permute-start.7 = (bf16[2,128,256]{2,1,0:T(8,128)(2,1)S(1)}, bf16[2,128,256]{2,1,0:T(8,128)(2,1)S(1)}, u32[]{:S(2)}, u32[]{:S(2)}) collective-permute-start(bf16[2,128,256]{2,1,0:T(8,128)(2,1)S(1)} %get-tuple-element.43), channel_id=1, source_target_pairs={{0,32},{1,97},{2,34},{3,99},{4,36},{5,101},{6,38},{7,103},{8,40},{... | collective-permute-start | bytes 393224 | tf_op jit(solution)/shard_map/ppermute | solution.py:33
  58.0 9.7 %collective-permute-start.8 = (bf16[2,128,256]{2,1,0:T(8,128)(2,1)S(1)}, bf16[2,128,256]{2,1,0:T(8,128)(2,1)S(1)}, u32[]{:S(2)}, u32[]{:S(2)}) collective-permute-start(bf16[2,128,256]{2,1,0:T(8,128)(2,1)S(1)} %get-tuple-element.44), channel_id=1, source_target_pairs={{0,32},{1,33},{2,34},{3,35},{4,36},{5,37},{6,38},{7,39},{8,40},{9,... | collective-permute-start | bytes 393224 | tf_op jit(solution)/shard_map/ppermute | solution.py:33
  59.6 8.6 %collective-permute-start.9 = (bf16[2,128,256]{2,1,0:T(8,128)(2,1)S(1)}, bf16[2,128,256]{2,1,0:T(8,128)(2,1)S(1)}, u32[]{:S(2)}, u32[]{:S(2)}) collective-permute-start(bf16[2,128,256]{2,1,0:T(8,128)(2,1)S(1)} %get-tuple-element.45), channel_id=1, source_target_pairs={{0,96},{1,97},{2,98},{3,99},{4,100},{5,101},{6,102},{7,103},{8,104... | collective-permute-start | bytes 393224 | tf_op jit(solution)/shard_map/ppermute | solution.py:33
  69.0 18.7 %all-to-all-start.1 = ((bf16[16,16,256]{2,1,0:T(8,128)(2,1)}), bf16[16,16,256]{2,1,0:T(8,128)(2,1)S(1)}, u32[]{:S(2)}, u32[]{:S(2)}) async-start(bf16[16,16,256]{2,1,0:T(8,128)(2,1)} %last_sum.1), calls=%async_computation.1 | async-start | bytes 262144 | tf_op jit(solution)/shard_map/all_to_all | solution.py:37

commit v5 on v4

--- a/solution.py
+++ b/solution.py
@@ -12,7 +12,7 @@
 AXES = ("query", "head")
 X_LO, Z, Y, X_HI, CORE = 2, 8, 4, 2, 2
 SCALE = HEAD_DIM ** (-0.5)
-CHUNK_CHIPS = 4
+CHUNK_CHIPS = 8
 LOG2E = 1.4426950408889634
 
 
@@ -270,98 +270,166 @@
     return jnp.dot(a, b, preferred_element_type=jnp.float32)
 
 
-def attention_kernel(
-    queries, cotangents, own, other, rows_out, keep_ref, send_ref, s_ref, e_ref, ds_ref
+def half_chunks(source):
+    size = CHUNK_CHIPS * source.shape[2]
+    found = []
+    for chip in range(0, Y * X_HI, CHUNK_CHIPS):
+        load = lambda kind, chip=chip: source[chip : chip + CHUNK_CHIPS, kind].reshape(
+            size, HEAD_DIM
+        )
+        found.append((pl.ds(len(found) * size, size), load, chip))
+    return found
+
+
+def scores_of(chunks, q, s_ref):
+    top = None
+    for rows, load, _ in chunks:
+        s = nt(load(0), q)
+        s_ref[rows, :] = s
+        here = jnp.max(s, axis=0, keepdims=True)
+        top = here if top is None else jnp.maximum(top, here)
+    return top * (LOG2E * SCALE)
+
+
+def weights_of(chunks, top, s_ref, e_ref):
+    total, att = 0.0, 0.0
+    for rows, load, _ in chunks:
+        e = jnp.exp2(s_ref[rows, :] * (LOG2E * SCALE) - top)
+        total = total + jnp.sum(e, axis=0, keepdims=True)
+        eb = e.astype(jnp.bfloat16)
+        e_ref[rows, :] = eb
+        att = att + nn(load(1).T, eb)
+    return total, att
+
+
+def share_rows(core, full, side, first_chip, kind, keep_ref, send_ref):
+    first = core == 0
+    block = full.shape[0] // CHUNK_CHIPS
+    full = full.reshape(CHUNK_CHIPS, block // 16, 2, 8, HEAD_DIM)
+    for i in range(CHUNK_CHIPS):
+        xl, low_z = divmod(first_chip + i, Y * X_HI // X_LO)
+        z = low_z * 2 + side
+        low = full[i, :, 0].reshape(block // 2, HEAD_DIM)
+        high = full[i, :, 1].reshape(block // 2, HEAD_DIM)
+        at = pl.ds(xl * (block // 2), block // 2)
+        keep_ref[z, kind, at, :] = jnp.where(first, low, high).astype(jnp.bfloat16)
+        send_ref[z, kind, at, :] = jnp.where(first, high, low).astype(jnp.bfloat16)
+
+
+def own_half_kernel(queries, own, e_ref, att_ref, stats_ref, s_ref):
+    chunks = half_chunks(own)
+    top = scores_of(chunks, queries[...], s_ref)
+    total, att = weights_of(chunks, top, s_ref, e_ref)
+    att_ref[...] = att
+    stats_ref[0:8, :] = jnp.broadcast_to(top, (8, top.shape[1]))
+    stats_ref[8:16, :] = jnp.broadcast_to(total, (8, top.shape[1]))
+
+
+def own_half(queries, own):
+    rows = queries.shape[0]
+    memory = own.shape[0] * own.shape[2]
+    bf16, f32 = jnp.bfloat16, jnp.float32
+    return pl.pallas_call(
+        own_half_kernel,
+        out_shape=(
+            jax.ShapeDtypeStruct((memory, rows), bf16),
+            jax.ShapeDtypeStruct((HEAD_DIM, rows), f32),
+            jax.ShapeDtypeStruct((16, rows), f32),
+        ),
+        in_specs=[VMEM] * 2,
+        out_specs=(VMEM,) * 3,
+        scratch_shapes=[pltpu.VMEM((memory, rows), f32)],
+        compiler_params=params(16),
+        cost_estimate=pl.CostEstimate(
+            flops=4 * rows * memory * HEAD_DIM,
+            bytes_accessed=2 * 1024 * 1024,
+            transcendentals=rows * memory,
+        ),
+        name="own_half",
+    )(queries, own)
+
+
+def both_halves_kernel(
+    queries, cotangents, own, other, own_e_ref, own_att_ref, stats_ref,
+    att_ref, ds_ref, keep_ref, send_ref, s_ref, e_ref,
 ):
     _, _, core = position()
     q = queries[...]
-    do = cotangents[...]
-    block = own.shape[2]
-    chunks = [
-        (source, at, chip)
-        for source, at in ((own, core), (other, 1 - core))
-        for chip in range(0, Y * X_HI, CHUNK_CHIPS)
-    ]
-    size = CHUNK_CHIPS * block
-    places = [pl.ds(i * size, size) for i in range(len(chunks))]
-
-    def rows_of(chunk, kind):
-        source, _, chip = chunk
-        return source[chip : chip + CHUNK_CHIPS, kind].reshape(size, HEAD_DIM)
-
-    factor = LOG2E * SCALE
-    top = None
-    for chunk, rows in zip(chunks, places):
-        s = nt(rows_of(chunk, 0), q)
-        s_ref[rows, :] = s
-        here = jnp.max(s, axis=0, keepdims=True)
-        top = here if top is None else jnp.maximum(top, here)
-    top = top * factor
-    total = None
-    att = None
-    for chunk, rows in zip(chunks, places):
-        e = jnp.exp2(s_ref[rows, :] * factor - top)
-        here = jnp.sum(e, axis=0, keepdims=True)
-        total = here if total is None else total + here
-        eb = e.astype(jnp.bfloat16)
-        e_ref[rows, :] = eb
-        part = nn(rows_of(chunk, 1).T, eb)
-        att = part if att is None else att + part
-    inverse = 1.0 / total
-    att = att * inverse
-    rows_out[0] = att.T.astype(jnp.bfloat16)
-    dot = (do.astype(jnp.float32).T * inverse).astype(jnp.bfloat16)
-    delta = jnp.sum(att * dot.astype(jnp.float32), axis=0, keepdims=True)
-    dos = dot.T
-    dq = None
-    for chunk, rows in zip(chunks, places):
-        dp = nn(rows_of(chunk, 1), dot)
-        ds = (e_ref[rows, :].astype(jnp.float32) * (dp - delta)).astype(jnp.bfloat16)
-        ds_ref[rows, :] = ds
-        part = nn(rows_of(chunk, 0).T, ds)
-        dq = part if dq is None else dq + part
+    chunks = half_chunks(other)
+    own_top, own_total = stats_ref[0:1, :], stats_ref[8:9, :]
+    top = jnp.maximum(own_top, scores_of(chunks, q, s_ref))
+    total, att = weights_of(chunks, top, s_ref, e_ref)
+    shrink = jnp.exp2(own_top - top)
+    inverse = 1.0 / (own_total * shrink + total)
+    att = (own_att_ref[...] * shrink + att) * inverse
+    att_ref[...] = att.T.astype(jnp.bfloat16)
+    dot = cotangents[...].astype(jnp.float32).T * inverse
+    half = own_e_ref.shape[0]
+    for base, source, side, weights, scaled in (
+        (0, own, core, own_e_ref, dot * shrink),
+        (half, other, 1 - core, e_ref, dot),
+    ):
+        scaled = scaled.astype(jnp.bfloat16)
+        delta = jnp.sum(att * scaled.astype(jnp.float32), axis=0, keepdims=True)
+        rows_scaled = scaled.T
+        for rows, load, chip in half_chunks(source):
+            e = weights[rows, :]
+            dp = nn(load(1), scaled)
+            ds = (e.astype(jnp.float32) * (dp - delta)).astype(jnp.bfloat16)
+            ds_ref[pl.ds(base + rows.start, rows.size), :] = ds
+            share_rows(core, nn(ds, q) * SCALE, side, chip, 0, keep_ref, send_ref)
+            share_rows(core, nn(e, rows_scaled), side, chip, 1, keep_ref, send_ref)
+
+
+def both_halves(queries, cotangents, own, other, own_e, own_att, stats):
+    half, rows = own_e.shape
+    bf16, f32 = jnp.bfloat16, jnp.float32
+    parts = jax.ShapeDtypeStruct((Z, 2, 2 * half // (2 * Z), HEAD_DIM), bf16)
+    return pl.pallas_call(
+        both_halves_kernel,
+        out_shape=(
+            jax.ShapeDtypeStruct((rows, HEAD_DIM), bf16),
+            jax.ShapeDtypeStruct((2 * half, rows), bf16),
+            parts,
+            parts,
+        ),
+        in_specs=[VMEM] * 7,
+        out_specs=(VMEM,) * 4,
+        scratch_shapes=[pltpu.VMEM((half, rows), f32), pltpu.VMEM((half, rows), bf16)],
+        compiler_params=params(20),
+        cost_estimate=pl.CostEstimate(
+            flops=12 * rows * half * HEAD_DIM,
+            bytes_accessed=4 * 1024 * 1024,
+            transcendentals=rows * half,
+        ),
+        name="both_halves",
+    )(queries, cotangents, own, other, own_e, own_att, stats)
+
+
+def queries_kernel(own, other, ds_ref, att_ref, rows_out):
+    rows_out[0] = att_ref[...]
+    dq = 0.0
+    base = 0
+    for source in (own, other):
+        for rows, load, _ in half_chunks(source):
+            dq = dq + nn(load(0).T, ds_ref[pl.ds(base + rows.start, rows.size), :])
+        base = ds_ref.shape[0] // 2
     rows_out[1] = (dq * SCALE).T.astype(jnp.bfloat16)
-    first = core == 0
-    for (_, side, first_chip), rows in zip(chunks, places):
-        for kind, full in enumerate((nn(ds_ref[rows, :], q) * SCALE, nn(e_ref[rows, :], dos))):
-            full = full.reshape(CHUNK_CHIPS, block // 16, 2, 8, HEAD_DIM)
-            for i in range(CHUNK_CHIPS):
-                xl, low_z = divmod(first_chip + i, Y * X_HI // X_LO)
-                z = low_z * 2 + side
-                low = full[i, :, 0].reshape(block // 2, HEAD_DIM)
-                high = full[i, :, 1].reshape(block // 2, HEAD_DIM)
-                at = pl.ds(xl * (block // 2), block // 2)
-                keep_ref[z, kind, at, :] = jnp.where(first, low, high).astype(jnp.bfloat16)
-                send_ref[z, kind, at, :] = jnp.where(first, high, low).astype(jnp.bfloat16)
-
-
-def attention(queries, cotangents, own, other):
-    rows = queries.shape[0]
-    memory = 2 * own.shape[0] * own.shape[2]
-    parts = (Z, 2, memory // (2 * Z), HEAD_DIM)
-    bf16, f32 = jnp.bfloat16, jnp.float32
-    return pl.pallas_call(
-        attention_kernel,
-        out_shape=(
-            jax.ShapeDtypeStruct((2, rows, HEAD_DIM), bf16),
-            jax.ShapeDtypeStruct(parts, bf16),
-            jax.ShapeDtypeStruct(parts, bf16),
-        ),
+
+
+def queries_step(own, other, ds, att):
+    memory, rows = ds.shape
+    return pl.pallas_call(
+        queries_kernel,
+        out_shape=jax.ShapeDtypeStruct((2,) + att.shape, att.dtype),
         in_specs=[VMEM] * 4,
-        out_specs=(VMEM, VMEM, VMEM),
-        scratch_shapes=[
-            pltpu.VMEM((memory, rows), f32),
-            pltpu.VMEM((memory, rows), bf16),
-            pltpu.VMEM((memory, rows), bf16),
-        ],
-        compiler_params=params(24),
+        out_specs=VMEM,
+        compiler_params=params(12),
         cost_estimate=pl.CostEstimate(
-            flops=12 * rows * memory * HEAD_DIM,
-            bytes_accessed=8 * 1024 * 1024,
-            transcendentals=rows * memory,
-        ),
-        name="attention",
-    )(queries, cotangents, own, other)
+            flops=2 * rows * memory * HEAD_DIM, bytes_accessed=2 * 1024 * 1024, transcendentals=0
+        ),
+        name="queries_step",
+    )(own, other, ds, att)
 
 
 def per_device(queries, mem_keys, mem_values, grad_out):
@@ -371,8 +439,9 @@
     own = exchange(pack(mem_keys, mem_values), head_groups())
     own, q, do = lax.optimization_barrier((own, q, do))
     other = permute(own, other_core)
-    rows, keep, send = attention(q, do, own, other)
+    att, ds, keep, send = both_halves(q, do, own, other, *own_half(q, own))
     came = permute(send, other_core)
+    rows = queries_step(own, other, ds, att)
     traded = trade(rows)
     sums = sum_over_z(keep, came)
     attended, query_gradients = unpack(rows, traded)

time: 88.6 us -> 84.9 us (0.958)
  waiting for transfers between devices: 41.1 us -> 36.2 us
    ppermute x7, waiting for transfers between devices: 17.8 us -> 12.9 us  [permute(): return lax.ppermute(array, AXES, pairs)]
    pallas_call x1 -> x3, Pallas kernels: 8.58 us -> 9.09 us  [the longest x1 5.47 us: both_halves(): pl.pallas_call(both_halves_kernel, out_shape=(jax.ShapeDtypeStruct((rows,...]
  transfers between devices with their start and end apart: 12 -> 12, of which waited for: 7 -> 6; matrix products, arithmetic and copies ran while one was open for 0% -> 0% of each run, Pallas kernels for 6% -> 10%
where the time goes in v5:
time: 84.9 us; the launch traced here: 84.5 us
  waiting for transfers between devices  36.2 us (43%)
  starting transfers between devices  32.9 us (39%)
  Pallas kernels  14.7 us (17%)
    all_to_all x2, waiting for transfers between devices, exchange(): lax.all_to_all(array, AXES, split_axis=0, concat_axis=0, axis_index_group...  23.3 us
    all_to_all x2, starting transfers between devices, exchange(): lax.all_to_all(array, AXES, split_axis=0, concat_axis=0, axis_index_group...  18.3 us
    ppermute x7, waiting for transfers between devices, permute(): return lax.ppermute(array, AXES, pairs)  12.9 us
    ppermute x7, starting transfers between devices, permute(): return lax.ppermute(array, AXES, pairs)  12.3 us
    pallas_call x1, Pallas kernels, both_halves(): pl.pallas_call(both_halves_kernel, out_shape=(jax.ShapeDtypeStruct((rows,...  5.47 us
    pallas_call x1, Pallas kernels, pack(): pl.pallas_call(pack_kernel, out_shape=jax.ShapeDtypeStruct(shape, keys.dt...  2.63 us
    pallas_call x1, Pallas kernels, own_half(): pl.pallas_call(own_half_kernel, out_shape=(jax.ShapeDtypeStruct((memory,...  2.28 us
    ppermute x3, starting transfers between devices, trade(): return lax.ppermute(array, AXES, pairs)  2.25 us
  transfers between devices with their start and end apart: 12, of which 6 were waited for; matrix products, arithmetic and copies ran while one was open for 0% of the time, Pallas kernels for 10%

profile of v5, /device:TPU:32, one launch (start us, length us, event | category | flops | bytes accessed | tf_op | source)
XLA Modules:
  0.0 84.5 jit_solution(9638262982916705053)
XLA Ops:
  0.7 0.8 collective-permute-start
  1.5 2.6 %pack.1 = bf16[8,2,128,256]{3,2,1,0:T(8,128)(2,1)} custom-call(bf16[128,4096]{1,0:T(8,128)(2,1)} %keys.1, bf16[128,4096]{1,0:T(8,128)(2,1)} %values.1), custom_call_target="tpu_custom_call" | custom-call | tf_op jit(solution)/shard_map/pack/pallas_call | solution.py:96
  4.1 6.9 %all-to-all-start = ((bf16[8,2,128,256]{3,2,1,0:T(8,128)(2,1)}), bf16[8,2,128,256]{3,2,1,0:T(8,128)(2,1)S(1)}, u32[]{:S(2)}, u32[]{:S(2)}) async-start(bf16[8,2,128,256]{3,2,1,0:T(8,128)(2,1)} %pack.1), calls=%async_computation | async-start | bytes 2097152 | tf_op jit(solution)/shard_map/all_to_all | solution.py:37
  11.1 0.0 collective-permute-done.q_came
  11.1 0.7 collective-permute-start.1
  11.8 0.0 collective-permute-done.1.do_came
  11.8 0.2 select.1
  12.0 16.4 %all-to-all-done.own = bf16[8,2,128,256]{3,2,1,0:T(8,128)(2,1)S(1)} async-done(((bf16[8,2,128,256]{3,2,1,0:T(8,128)(2,1)}), bf16[8,2,128,256]{3,2,1,0:T(8,128)(2,1)S(1)}, u32[]{:S(2)}, u32[]{:S(2)}) %all-to-all-start) | async-done | bytes 1048608 | tf_op jit(solution)/shard_map/all_to_all | solution.py:37
  28.4 1.2 %collective-permute-start.2 = (bf16[8,2,128,256]{3,2,1,0:T(8,128)(2,1)S(1)}, bf16[8,2,128,256]{3,2,1,0:T(8,128)(2,1)S(1)}, u32[]{:S(2)}, u32[]{:S(2)}) collective-permute-start(bf16[8,2,128,256]{3,2,1,0:T(8,128)(2,1)S(1)} %all-to-all-done.own), channel_id=1, source_target_pairs={{0,1},{1,0},{2,3},{3,2},{4,5},{5,4},{6,7},{7,6},{8,9},{9,8},{10,11... | collective-permute-start | bytes 3145736 | tf_op jit(solution)/shard_map/ppermute | solution.py:33
  29.6 2.3 %own_half.1 = (bf16[1024,1024]{1,0:T(8,128)(2,1)S(1)}, f32[256,1024]{1,0:T(8,128)S(1)}, f32[16,1024]{1,0:T(8,128)S(1)}) custom-call(bf16[1024,256]{1,0:T(8,128)(2,1)S(1)} %get-tuple-element.35.queries, bf16[8,2,128,256]{3,2,1,0:T(8,128)(2,1)S(1)} %all-to-all-done.own), custom_call_target="tpu_custom_call" | custom-call | flops 1073741824 | bytes 2097152 | tf_op jit(solution)/shard_map/own_half/pallas_call | solution.py:332
  31.9 0.0 collective-permute-done.2.other
  31.9 5.5 %both_halves.1 = (bf16[1024,256]{1,0:T(8,128)(2,1)S(1)}, bf16[2048,1024]{1,0:T(8,128)(2,1)S(1)}, bf16[8,2,128,256]{3,2,1,0:T(8,128)(2,1)S(1)}, bf16[8,2,128,256]{3,2,1,0:T(8,128)(2,1)S(1)}) custom-call(bf16[1024,256]{1,0:T(8,128)(2,1)S(1)} %get-tuple-element.35.queries, bf16[1024,256]{1,0:T(8,128)(2,1)S(1)} %get-tuple-element.36.cotangents, ...), custom_call_target="tpu_custom_call" | custom-call | flops 3221225472 | bytes 4194304 | tf_op jit(solution)/shard_map/both_halves/pallas_call | solution.py:388
  37.4 0.4 collective-permute-start.4
  37.8 1.3 %queries_step.1.mine = bf16[2,1024,256]{2,1,0:T(8,128)(2,1)S(1)} custom-call(bf16[8,2,128,256]{3,2,1,0:T(8,128)(2,1)S(1)} %all-to-all-done.own, bf16[8,2,128,256]{3,2,1,0:T(8,128)(2,1)S(1)} %collective-permute-done.2.other, bf16[2048,1024]{1,0:T(8,128)(2,1)S(1)} %get-tuple-element.40.ds_ref, bf16[1024,256]{1,0:T(8,128)(2,1)S(1)} %get-tuple-element.41.att_ref), custom_call_target="tpu_custom_call" | custom-call | flops 1073741824 | bytes 2097152 | tf_op jit(solution)/shard_map/queries_step/pallas_call | solution.py:422
  39.2 0.7 collective-permute-start.3
  39.9 0.2 collective-permute-done.4.came
  40.1 0.2 core_sum.1
  40.4 2.0 %collective-permute-start.5 = (bf16[2,2,128,256]{3,2,1,0:T(8,128)(2,1)S(1)}, bf16[2,2,128,256]{3,2,1,0:T(8,128)(2,1)S(1)}, u32[]{:S(2)}, u32[]{:S(2)}) collective-permute-start(bf16[2,2,128,256]{3,2,1,0:T(8,128)(2,1)S(1)} %get-tuple-element.47), channel_id=1, source_target_pairs={{0,16},{1,17},{2,18},{3,19},{4,20},{5,21},{6,22},{7,23},{8,24},{9,... | collective-permute-start | bytes 786440 | tf_op jit(solution)/shard_map/ppermute | solution.py:33
  42.3 0.1 collective-permute-start.6
  42.5 4.4 %collective-permute-start.7 = (bf16[2,128,256]{2,1,0:T(8,128)(2,1)S(1)}, bf16[2,128,256]{2,1,0:T(8,128)(2,1)S(1)}, u32[]{:S(2)}, u32[]{:S(2)}) collective-permute-start(bf16[2,128,256]{2,1,0:T(8,128)(2,1)S(1)} %get-tuple-element.51), channel_id=1, source_target_pairs={{0,32},{1,97},{2,34},{3,99},{4,36},{5,101},{6,38},{7,103},{8,40},{... | collective-permute-start | bytes 393224 | tf_op jit(solution)/shard_map/ppermute | solution.py:33
  46.8 6.5 %collective-permute-done.7.across = bf16[2,128,256]{2,1,0:T(8,128)(2,1)S(1)} collective-permute-done((bf16[2,128,256]{2,1,0:T(8,128)(2,1)S(1)}, bf16[2,128,256]{2,1,0:T(8,128)(2,1)S(1)}, u32[]{:S(2)}, u32[]{:S(2)}) %collective-permute-start.7) | collective-permute-done | bytes 131104 | tf_op jit(solution)/shard_map/ppermute | solution.py:33
  53.4 0.0 collective-permute-done.5.from_below
  53.4 0.1 middle_sum.1
  53.5 1.9 %collective-permute-start.8 = (bf16[2,128,256]{2,1,0:T(8,128)(2,1)S(1)}, bf16[2,128,256]{2,1,0:T(8,128)(2,1)S(1)}, u32[]{:S(2)}, u32[]{:S(2)}) collective-permute-start(bf16[2,128,256]{2,1,0:T(8,128)(2,1)S(1)} %get-tuple-element.52), channel_id=1, source_target_pairs={{0,32},{1,33},{2,34},{3,35},{4,36},{5,37},{6,38},{7,39},{8,40},{9,... | collective-permute-start | bytes 393224 | tf_op jit(solution)/shard_map/ppermute | solution.py:33
  55.4 2.3 %collective-permute-start.9 = (bf16[2,128,256]{2,1,0:T(8,128)(2,1)S(1)}, bf16[2,128,256]{2,1,0:T(8,128)(2,1)S(1)}, u32[]{:S(2)}, u32[]{:S(2)}) collective-permute-start(bf16[2,128,256]{2,1,0:T(8,128)(2,1)S(1)} %get-tuple-element.53), channel_id=1, source_target_pairs={{0,96},{1,97},{2,98},{3,99},{4,100},{5,101},{6,102},{7,103},{8,104... | collective-permute-start | bytes 393224 | tf_op jit(solution)/shard_map/ppermute | solution.py:33
  57.7 4.9 %collective-permute-done.8.low = bf16[2,128,256]{2,1,0:T(8,128)(2,1)S(1)} collective-permute-done((bf16[2,128,256]{2,1,0:T(8,128)(2,1)S(1)}, bf16[2,128,256]{2,1,0:T(8,128)(2,1)S(1)}, u32[]{:S(2)}, u32[]{:S(2)}) %collective-permute-start.8) | collective-permute-done | bytes 131104 | tf_op jit(solution)/shard_map/ppermute | solution.py:33
  62.6 1.2 %collective-permute-done.9.high = bf16[2,128,256]{2,1,0:T(8,128)(2,1)S(1)} collective-permute-done((bf16[2,128,256]{2,1,0:T(8,128)(2,1)S(1)}, bf16[2,128,256]{2,1,0:T(8,128)(2,1)S(1)}, u32[]{:S(2)}, u32[]{:S(2)}) %collective-permute-start.9) | collective-permute-done | bytes 131104 | tf_op jit(solution)/shard_map/ppermute | solution.py:33
  63.8 0.7 last_sum.1
  64.5 11.4 %all-to-all-start.1 = ((bf16[16,16,256]{2,1,0:T(8,128)(2,1)}), bf16[16,16,256]{2,1,0:T(8,128)(2,1)S(1)}, u32[]{:S(2)}, u32[]{:S(2)}) async-start(bf16[16,16,256]{2,1,0:T(8,128)(2,1)} %last_sum.1), calls=%async_computation.1 | async-start | bytes 262144 | tf_op jit(solution)/shard_map/all_to_all | solution.py:37
  75.9 1.1 %unpack.1 = (bf16[1024,256]{1,0:T(8,128)(2,1)}, bf16[1024,256]{1,0:T(8,128)(2,1)}) custom-call(bf16[2,1024,256]{2,1,0:T(8,128)(2,1)S(1)} %queries_step.1.mine, bf16[2,1024,256]{2,1,0:T(8,128)(2,1)S(1)} %collective-permute-done.3.came), custom_call_target="tpu_custom_call" | custom-call | tf_op jit(solution)/shard_map/unpack/pallas_call | solution.py:140
  77.0 6.9 %all-to-all-done.1.parts = bf16[16,16,256]{2,1,0:T(8,128)(2,1)S(1)} async-done(((bf16[16,16,256]{2,1,0:T(8,128)(2,1)}), bf16[16,16,256]{2,1,0:T(8,128)(2,1)S(1)}, u32[]{:S(2)}, u32[]{:S(2)}) %all-to-all-start.1) | async-done | bytes 131104 | tf_op jit(solution)/shard_map/all_to_all | solution.py:37
  83.9 0.7 columns.1
  (6 shorter events, 0.0 us)
Async XLA Ops:
  0.6 11.2 %copy-start = (bf16[1024,256]{1,0:T(8,128)(2,1)S(1)}, bf16[1024,256]{1,0:T(8,128)(2,1)}, u32[]{:S(2)}) copy-start(bf16[1024,256]{1,0:T(8,128)(2,1)} %queries.1) | copy-start | bytes 1572868
  0.6 10.4 %copy-start.1 = (bf16[1024,256]{1,0:T(8,128)(2,1)S(1)}, bf16[1024,256]{1,0:T(8,128)(2,1)}, u32[]{:S(2)}) copy-start(bf16[1024,256]{1,0:T(8,128)(2,1)} %cotangents) | copy-start | bytes 1572868
  0.7 10.4 %collective-permute-start = (bf16[1024,256]{1,0:T(8,128)(2,1)}, bf16[1024,256]{1,0:T(8,128)(2,1)S(1)}, u32[]{:S(2)}, u32[]{:S(2)}) collective-permute-start(bf16[1024,256]{1,0:T(8,128)(2,1)} %queries.1), channel_id=1, source_target_pairs={{1,128},{128,1},{3,130},{130,3},{5,132},{132,5},{7,134},{134,7},{9... | collective-permute-start | bytes 1572872 | tf_op jit(solution)/shard_map/ppermute | solution.py:47
  4.1 24.3 %all-to-all-start = ((bf16[8,2,128,256]{3,2,1,0:T(8,128)(2,1)}), bf16[8,2,128,256]{3,2,1,0:T(8,128)(2,1)S(1)}, u32[]{:S(2)}, u32[]{:S(2)}) async-start(bf16[8,2,128,256]{3,2,1,0:T(8,128)(2,1)} %pack.1), calls=%async_computation | async-start | bytes 2097152 | tf_op jit(solution)/shard_map/all_to_all | solution.py:37
  11.1 0.7 collective-permute-start.1
  28.4 3.5 %collective-permute-start.2 = (bf16[8,2,128,256]{3,2,1,0:T(8,128)(2,1)S(1)}, bf16[8,2,128,256]{3,2,1,0:T(8,128)(2,1)S(1)}, u32[]{:S(2)}, u32[]{:S(2)}) collective-permute-start(bf16[8,2,128,256]{3,2,1,0:T(8,128)(2,1)S(1)} %all-to-all-done.own), channel_id=1, source_target_pairs={{0,1},{1,0},{2,3},{3,2},{4,5},{5,4},{6,7},{7,6},{8,9},{9,8},{10,11... | collective-permute-start | bytes 3145736 | tf_op jit(solution)/shard_map/ppermute | solution.py:33
  37.4 2.7 %collective-permute-start.4 = (bf16[8,2,128,256]{3,2,1,0:T(8,128)(2,1)S(1)}, bf16[8,2,128,256]{3,2,1,0:T(8,128)(2,1)S(1)}, u32[]{:S(2)}, u32[]{:S(2)}) collective-permute-start(bf16[8,2,128,256]{3,2,1,0:T(8,128)(2,1)S(1)} %get-tuple-element.45), channel_id=1, source_target_pairs={{0,1},{1,0},{2,3},{3,2},{4,5},{5,4},{6,7},{7,6},{8,9},{9,8},{10,11... | collective-permute-start | bytes 3145736 | tf_op jit(solution)/shard_map/ppermute | solution.py:33
  39.2 36.7 %collective-permute-start.3 = (bf16[2,1024,256]{2,1,0:T(8,128)(2,1)S(1)}, bf16[2,1024,256]{2,1,0:T(8,128)(2,1)S(1)}, u32[]{:S(2)}, u32[]{:S(2)}) collective-permute-start(bf16[2,1024,256]{2,1,0:T(8,128)(2,1)S(1)} %queries_step.1.mine), channel_id=1, source_target_pairs={{1,128},{128,1},{3,130},{130,3},{5,132},{132,5},{7,134},{134,7},{9... | collective-permute-start | bytes 3145736 | tf_op jit(solution)/shard_map/ppermute | solution.py:47
  40.4 13.0 %collective-permute-start.5 = (bf16[2,2,128,256]{3,2,1,0:T(8,128)(2,1)S(1)}, bf16[2,2,128,256]{3,2,1,0:T(8,128)(2,1)S(1)}, u32[]{:S(2)}, u32[]{:S(2)}) collective-permute-start(bf16[2,2,128,256]{3,2,1,0:T(8,128)(2,1)S(1)} %get-tuple-element.47), channel_id=1, source_target_pairs={{0,16},{1,17},{2,18},{3,19},{4,20},{5,21},{6,22},{7,23},{8,24},{9,... | collective-permute-start | bytes 786440 | tf_op jit(solution)/shard_map/ppermute | solution.py:33
  42.3 11.0 %collective-permute-start.6 = (bf16[2,2,128,256]{3,2,1,0:T(8,128)(2,1)S(1)}, bf16[2,2,128,256]{3,2,1,0:T(8,128)(2,1)S(1)}, u32[]{:S(2)}, u32[]{:S(2)}) collective-permute-start(bf16[2,2,128,256]{3,2,1,0:T(8,128)(2,1)S(1)} %get-tuple-element.48), channel_id=1, source_target_pairs={{0,112},{1,113},{2,114},{3,115},{4,116},{5,117},{6,118},{7,119},{8... | collective-permute-start | bytes 786440 | tf_op jit(solution)/shard_map/ppermute | solution.py:33
  42.5 10.9 %collective-permute-start.7 = (bf16[2,128,256]{2,1,0:T(8,128)(2,1)S(1)}, bf16[2,128,256]{2,1,0:T(8,128)(2,1)S(1)}, u32[]{:S(2)}, u32[]{:S(2)}) collective-permute-start(bf16[2,128,256]{2,1,0:T(8,128)(2,1)S(1)} %get-tuple-element.51), channel_id=1, source_target_pairs={{0,32},{1,97},{2,34},{3,99},{4,36},{5,101},{6,38},{7,103},{8,40},{... | collective-permute-start | bytes 393224 | tf_op jit(solution)/shard_map/ppermute | solution.py:33
  53.5 9.1 %collective-permute-start.8 = (bf16[2,128,256]{2,1,0:T(8,128)(2,1)S(1)}, bf16[2,128,256]{2,1,0:T(8,128)(2,1)S(1)}, u32[]{:S(2)}, u32[]{:S(2)}) collective-permute-start(bf16[2,128,256]{2,1,0:T(8,128)(2,1)S(1)} %get-tuple-element.52), channel_id=1, source_target_pairs={{0,32},{1,33},{2,34},{3,35},{4,36},{5,37},{6,38},{7,39},{8,40},{9,... | collective-permute-start | bytes 393224 | tf_op jit(solution)/shard_map/ppermute | solution.py:33
  55.4 8.4 %collective-permute-start.9 = (bf16[2,128,256]{2,1,0:T(8,128)(2,1)S(1)}, bf16[2,128,256]{2,1,0:T(8,128)(2,1)S(1)}, u32[]{:S(2)}, u32[]{:S(2)}) collective-permute-start(bf16[2,128,256]{2,1,0:T(8,128)(2,1)S(1)} %get-tuple-element.53), channel_id=1, source_target_pairs={{0,96},{1,97},{2,98},{3,99},{4,100},{5,101},{6,102},{7,103},{8,104... | collective-permute-start | bytes 393224 | tf_op jit(solution)/shard_map/ppermute | solution.py:33
  64.5 19.4 %all-to-all-start.1 = ((bf16[16,16,256]{2,1,0:T(8,128)(2,1)}), bf16[16,16,256]{2,1,0:T(8,128)(2,1)S(1)}, u32[]{:S(2)}, u32[]{:S(2)}) async-start(bf16[16,16,256]{2,1,0:T(8,128)(2,1)} %last_sum.1), calls=%async_computation.1 | async-start | bytes 262144 | tf_op jit(solution)/shard_map/all_to_all | solution.py:37

commit v6 on v5

--- a/solution.py
+++ b/solution.py
@@ -45,6 +45,16 @@
         one, two = device(0, z, y, xh, 1), device(1, z, y, xh, 0)
         pairs += [(one, two), (two, one)]
     return lax.ppermute(array, AXES, pairs)
+
+
+def trade_in_two(array):
+    over, home = [], []
+    for z, y, xh in itertools.product(range(Z), range(Y), range(X_HI)):
+        for xl in range(X_LO):
+            middle = device(1 - xl, z, y, xh, 1 - xl)
+            over.append((device(xl, z, y, xh, 1 - xl), middle))
+            home.append((middle, device(1 - xl, z, y, xh, xl)))
+    return lax.ppermute(lax.ppermute(array, AXES, over), AXES, home)
 
 
 def other_core(xl, z, y, xh, c):
@@ -433,9 +443,7 @@
 
 
 def per_device(queries, mem_keys, mem_values, grad_out):
-    q_came = trade(queries)
-    grad_out, q_came = lax.optimization_barrier((grad_out, q_came))
-    q, do = select(queries, grad_out, q_came, trade(grad_out))
+    q, do = select(queries, grad_out, trade_in_two(queries), trade_in_two(grad_out))
     own = exchange(pack(mem_keys, mem_values), head_groups())
     own, q, do = lax.optimization_barrier((own, q, do))
     other = permute(own, other_core)

time: 84.9 us -> 83 us (0.978)
  waiting for transfers between devices: 36.2 us -> 34 us
    all_to_all x2, waiting for transfers between devices: 23.3 us -> 14 us  [exchange(): lax.all_to_all(array, AXES, split_axis=0, concat_axis=0, axis_index_group...]
    ppermute x0 -> x4, starting transfers between devices: none -> 8.63 us  [trade_in_two(): return lax.ppermute(lax.ppermute(array, AXES, over), AXES, home)]
    all_to_all x2, starting transfers between devices: 18.3 us -> 11.9 us  [exchange(): lax.all_to_all(array, AXES, split_axis=0, concat_axis=0, axis_index_group...]
    ppermute x0 -> x4, waiting for transfers between devices: none -> 5.39 us  [trade_in_two(): return lax.ppermute(lax.ppermute(array, AXES, over), AXES, home)]
    ppermute x7, waiting for transfers between devices: 12.9 us -> 14.7 us  [permute(): return lax.ppermute(array, AXES, pairs)]
    ppermute x3 -> x1, starting transfers between devices: 2.25 us -> 0.73 us  [trade(): return lax.ppermute(array, AXES, pairs)]
  transfers between devices with their start and end apart: 12 -> 14, of which waited for: 6 -> 7; matrix products, arithmetic and copies ran while one was open for 0% -> 0% of each run, Pallas kernels for 10% -> 10%
where the time goes in v6:
time: 83 us; the launch traced here: 82.6 us
  waiting for transfers between devices  34 us (41%)
  starting transfers between devices  33.1 us (40%)
  Pallas kernels  14.7 us (18%)
    ppermute x7, waiting for transfers between devices, permute(): return lax.ppermute(array, AXES, pairs)  14.7 us
    all_to_all x2, waiting for transfers between devices, exchange(): lax.all_to_all(array, AXES, split_axis=0, concat_axis=0, axis_index_group...  14 us
    all_to_all x2, starting transfers between devices, exchange(): lax.all_to_all(array, AXES, split_axis=0, concat_axis=0, axis_index_group...  11.9 us
    ppermute x7, starting transfers between devices, permute(): return lax.ppermute(array, AXES, pairs)  11.9 us
    ppermute x4, starting transfers between devices, trade_in_two(): return lax.ppermute(lax.ppermute(array, AXES, over), AXES, home)  8.63 us
    pallas_call x1, Pallas kernels, both_halves(): pl.pallas_call(both_halves_kernel, out_shape=(jax.ShapeDtypeStruct((rows,...  5.47 us
    ppermute x4, waiting for transfers between devices, trade_in_two(): return lax.ppermute(lax.ppermute(array, AXES, over), AXES, home)  5.39 us
    pallas_call x1, Pallas kernels, pack(): pl.pallas_call(pack_kernel, out_shape=jax.ShapeDtypeStruct(shape, keys.dt...  2.62 us
  transfers between devices with their start and end apart: 14, of which 7 were waited for; matrix products, arithmetic and copies ran while one was open for 0% of the time, Pallas kernels for 10%

profile of v6, /device:TPU:32, one launch (start us, length us, event | category | flops | bytes accessed | tf_op | source)
XLA Modules:
  0.0 82.6 jit_solution(2897462163101698922)
XLA Ops:
  0.7 1.4 %collective-permute-start = (bf16[1024,256]{1,0:T(8,128)(2,1)}, bf16[1024,256]{1,0:T(8,128)(2,1)}, u32[]{:S(2)}, u32[]{:S(2)}) collective-permute-start(bf16[1024,256]{1,0:T(8,128)(2,1)} %queries.1), channel_id=1, source_target_pairs={{1,129},{128,0},{3,131},{130,2},{5,133},{132,4},{7,135},{134,6},{9... | collective-permute-start | bytes 1572872 | tf_op jit(solution)/shard_map/ppermute | solution.py:57
  2.1 1.3 %collective-permute-start.2 = (bf16[1024,256]{1,0:T(8,128)(2,1)}, bf16[1024,256]{1,0:T(8,128)(2,1)}, u32[]{:S(2)}, u32[]{:S(2)}) collective-permute-start(bf16[1024,256]{1,0:T(8,128)(2,1)} %cotangents.1), channel_id=1, source_target_pairs={{1,129},{128,0},{3,131},{130,2},{5,133},{132,4},{7,135},{134,6},{9... | collective-permute-start | bytes 1572872 | tf_op jit(solution)/shard_map/ppermute | solution.py:57
  3.4 2.6 %pack.1 = bf16[8,2,128,256]{3,2,1,0:T(8,128)(2,1)} custom-call(bf16[128,4096]{1,0:T(8,128)(2,1)} %keys.1, bf16[128,4096]{1,0:T(8,128)(2,1)} %values.1), custom_call_target="tpu_custom_call" | custom-call | tf_op jit(solution)/shard_map/pack/pallas_call | solution.py:106
  6.0 6.9 %all-to-all-start = ((bf16[8,2,128,256]{3,2,1,0:T(8,128)(2,1)}), bf16[8,2,128,256]{3,2,1,0:T(8,128)(2,1)S(1)}, u32[]{:S(2)}, u32[]{:S(2)}) async-start(bf16[8,2,128,256]{3,2,1,0:T(8,128)(2,1)} %pack.1), calls=%async_computation | async-start | bytes 2097152 | tf_op jit(solution)/shard_map/all_to_all | solution.py:37
  12.9 0.0 collective-permute-done
  13.0 4.6 %collective-permute-start.1 = (bf16[1024,256]{1,0:T(8,128)(2,1)}, bf16[1024,256]{1,0:T(8,128)(2,1)S(1)}, u32[]{:S(2)}, u32[]{:S(2)}) collective-permute-start(bf16[1024,256]{1,0:T(8,128)(2,1)} %collective-permute-done), channel_id=1, source_target_pairs={{129,128},{0,1},{131,130},{2,3},{133,132},{4,5},{135,134},{6,7},{1... | collective-permute-start | bytes 1572872 | tf_op jit(solution)/shard_map/ppermute | solution.py:57
  17.6 3.7 %collective-permute-done.2 = bf16[1024,256]{1,0:T(8,128)(2,1)} collective-permute-done((bf16[1024,256]{1,0:T(8,128)(2,1)}, bf16[1024,256]{1,0:T(8,128)(2,1)}, u32[]{:S(2)}, u32[]{:S(2)}) %collective-permute-start.2) | collective-permute-done | bytes 524320 | tf_op jit(solution)/shard_map/ppermute | solution.py:57
  21.3 1.3 %collective-permute-start.3 = (bf16[1024,256]{1,0:T(8,128)(2,1)}, bf16[1024,256]{1,0:T(8,128)(2,1)S(1)}, u32[]{:S(2)}, u32[]{:S(2)}) collective-permute-start(bf16[1024,256]{1,0:T(8,128)(2,1)} %collective-permute-done.2), channel_id=1, source_target_pairs={{129,128},{0,1},{131,130},{2,3},{133,132},{4,5},{135,134},{6,7},{1... | collective-permute-start | bytes 1572872 | tf_op jit(solution)/shard_map/ppermute | solution.py:57
  22.6 1.7 %collective-permute-done.3.do_came = bf16[1024,256]{1,0:T(8,128)(2,1)S(1)} collective-permute-done((bf16[1024,256]{1,0:T(8,128)(2,1)}, bf16[1024,256]{1,0:T(8,128)(2,1)S(1)}, u32[]{:S(2)}, u32[]{:S(2)}) %collective-permute-start.3) | collective-permute-done | bytes 524320 | tf_op jit(solution)/shard_map/ppermute | solution.py:57
  24.3 0.2 select.1
  24.5 7.1 %all-to-all-done.own = bf16[8,2,128,256]{3,2,1,0:T(8,128)(2,1)S(1)} async-done(((bf16[8,2,128,256]{3,2,1,0:T(8,128)(2,1)}), bf16[8,2,128,256]{3,2,1,0:T(8,128)(2,1)S(1)}, u32[]{:S(2)}, u32[]{:S(2)}) %all-to-all-start) | async-done | bytes 1048608 | tf_op jit(solution)/shard_map/all_to_all | solution.py:37
  31.5 0.7 collective-permute-start.4
  32.3 2.3 %own_half.1 = (bf16[1024,1024]{1,0:T(8,128)(2,1)S(1)}, f32[256,1024]{1,0:T(8,128)S(1)}, f32[16,1024]{1,0:T(8,128)S(1)}) custom-call(bf16[1024,256]{1,0:T(8,128)(2,1)S(1)} %get-tuple-element.31.queries, bf16[8,2,128,256]{3,2,1,0:T(8,128)(2,1)S(1)} %all-to-all-done.own), custom_call_target="tpu_custom_call" | custom-call | flops 1073741824 | bytes 2097152 | tf_op jit(solution)/shard_map/own_half/pallas_call | solution.py:342
  34.5 5.5 %both_halves.1 = (bf16[1024,256]{1,0:T(8,128)(2,1)S(1)}, bf16[2048,1024]{1,0:T(8,128)(2,1)S(1)}, bf16[8,2,128,256]{3,2,1,0:T(8,128)(2,1)S(1)}, bf16[8,2,128,256]{3,2,1,0:T(8,128)(2,1)S(1)}) custom-call(bf16[1024,256]{1,0:T(8,128)(2,1)S(1)} %get-tuple-element.31.queries, bf16[1024,256]{1,0:T(8,128)(2,1)S(1)} %get-tuple-element.32.cotangents, ...), custom_call_target="tpu_custom_call" | custom-call | flops 3221225472 | bytes 4194304 | tf_op jit(solution)/shard_map/both_halves/pallas_call | solution.py:398
  40.0 0.4 collective-permute-start.6
  40.5 1.4 %queries_step.1.mine = bf16[2,1024,256]{2,1,0:T(8,128)(2,1)S(1)} custom-call(bf16[8,2,128,256]{3,2,1,0:T(8,128)(2,1)S(1)} %all-to-all-done.own, bf16[8,2,128,256]{3,2,1,0:T(8,128)(2,1)S(1)} %collective-permute-done.4.other, bf16[2048,1024]{1,0:T(8,128)(2,1)S(1)} %get-tuple-element.36.ds_ref, bf16[1024,256]{1,0:T(8,128)(2,1)S(1)} %get-tuple-element.37.att_ref), custom_call_target="tpu_custom_call" | custom-call | flops 1073741824 | bytes 2097152 | tf_op jit(solution)/shard_map/queries_step/pallas_call | solution.py:432
  41.8 0.7 collective-permute-start.5
  42.6 0.2 collective-permute-done.6.came
  42.8 0.2 core_sum.1
  43.0 2.0 %collective-permute-start.7 = (bf16[2,2,128,256]{3,2,1,0:T(8,128)(2,1)S(1)}, bf16[2,2,128,256]{3,2,1,0:T(8,128)(2,1)S(1)}, u32[]{:S(2)}, u32[]{:S(2)}) collective-permute-start(bf16[2,2,128,256]{3,2,1,0:T(8,128)(2,1)S(1)} %get-tuple-element.43), channel_id=1, source_target_pairs={{0,16},{1,17},{2,18},{3,19},{4,20},{5,21},{6,22},{7,23},{8,24},{9,... | collective-permute-start | bytes 786440 | tf_op jit(solution)/shard_map/ppermute | solution.py:33
  45.0 0.1 collective-permute-start.8
  45.1 4.4 %collective-permute-start.9 = (bf16[2,128,256]{2,1,0:T(8,128)(2,1)S(1)}, bf16[2,128,256]{2,1,0:T(8,128)(2,1)S(1)}, u32[]{:S(2)}, u32[]{:S(2)}) collective-permute-start(bf16[2,128,256]{2,1,0:T(8,128)(2,1)S(1)} %get-tuple-element.47), channel_id=1, source_target_pairs={{0,32},{1,97},{2,34},{3,99},{4,36},{5,101},{6,38},{7,103},{8,40},{... | collective-permute-start | bytes 393224 | tf_op jit(solution)/shard_map/ppermute | solution.py:33
  49.5 7.4 %collective-permute-done.9.across = bf16[2,128,256]{2,1,0:T(8,128)(2,1)S(1)} collective-permute-done((bf16[2,128,256]{2,1,0:T(8,128)(2,1)S(1)}, bf16[2,128,256]{2,1,0:T(8,128)(2,1)S(1)}, u32[]{:S(2)}, u32[]{:S(2)}) %collective-permute-start.9) | collective-permute-done | bytes 131104 | tf_op jit(solution)/shard_map/ppermute | solution.py:33
  56.9 0.1 middle_sum.1
  57.0 1.5 %collective-permute-start.10 = (bf16[2,128,256]{2,1,0:T(8,128)(2,1)S(1)}, bf16[2,128,256]{2,1,0:T(8,128)(2,1)S(1)}, u32[]{:S(2)}, u32[]{:S(2)}) collective-permute-start(bf16[2,128,256]{2,1,0:T(8,128)(2,1)S(1)} %get-tuple-element.48), channel_id=1, source_target_pairs={{0,32},{1,33},{2,34},{3,35},{4,36},{5,37},{6,38},{7,39},{8,40},{9,... | collective-permute-start | bytes 393224 | tf_op jit(solution)/shard_map/ppermute | solution.py:33
  58.5 2.7 %collective-permute-start.11 = (bf16[2,128,256]{2,1,0:T(8,128)(2,1)S(1)}, bf16[2,128,256]{2,1,0:T(8,128)(2,1)S(1)}, u32[]{:S(2)}, u32[]{:S(2)}) collective-permute-start(bf16[2,128,256]{2,1,0:T(8,128)(2,1)S(1)} %get-tuple-element.49), channel_id=1, source_target_pairs={{0,96},{1,97},{2,98},{3,99},{4,100},{5,101},{6,102},{7,103},{8,104... | collective-permute-start | bytes 393224 | tf_op jit(solution)/shard_map/ppermute | solution.py:33
  61.2 7.1 %collective-permute-done.10.low = bf16[2,128,256]{2,1,0:T(8,128)(2,1)S(1)} collective-permute-done((bf16[2,128,256]{2,1,0:T(8,128)(2,1)S(1)}, bf16[2,128,256]{2,1,0:T(8,128)(2,1)S(1)}, u32[]{:S(2)}, u32[]{:S(2)}) %collective-permute-start.10) | collective-permute-done | bytes 131104 | tf_op jit(solution)/shard_map/ppermute | solution.py:33
  68.3 0.7 last_sum.1
  69.0 4.9 %all-to-all-start.1 = ((bf16[16,16,256]{2,1,0:T(8,128)(2,1)}), bf16[16,16,256]{2,1,0:T(8,128)(2,1)S(1)}, u32[]{:S(2)}, u32[]{:S(2)}) async-start(bf16[16,16,256]{2,1,0:T(8,128)(2,1)} %last_sum.1), calls=%async_computation.1 | async-start | bytes 262144 | tf_op jit(solution)/shard_map/all_to_all | solution.py:37
  73.9 1.1 %unpack.1 = (bf16[1024,256]{1,0:T(8,128)(2,1)}, bf16[1024,256]{1,0:T(8,128)(2,1)}) custom-call(bf16[2,1024,256]{2,1,0:T(8,128)(2,1)S(1)} %queries_step.1.mine, bf16[2,1024,256]{2,1,0:T(8,128)(2,1)S(1)} %collective-permute-done.5.came), custom_call_target="tpu_custom_call" | custom-call | tf_op jit(solution)/shard_map/unpack/pallas_call | solution.py:150
  75.0 6.9 %all-to-all-done.1.parts = bf16[16,16,256]{2,1,0:T(8,128)(2,1)S(1)} async-done(((bf16[16,16,256]{2,1,0:T(8,128)(2,1)}), bf16[16,16,256]{2,1,0:T(8,128)(2,1)S(1)}, u32[]{:S(2)}, u32[]{:S(2)}) %all-to-all-start.1) | async-done | bytes 131104 | tf_op jit(solution)/shard_map/all_to_all | solution.py:37
  81.9 0.7 columns.1
  (10 shorter events, 0.0 us)
Async XLA Ops:
  0.6 23.6 %copy-start = (bf16[1024,256]{1,0:T(8,128)(2,1)S(1)}, bf16[1024,256]{1,0:T(8,128)(2,1)}, u32[]{:S(2)}) copy-start(bf16[1024,256]{1,0:T(8,128)(2,1)} %queries.1) | copy-start | bytes 1572868
  0.6 23.6 %copy-start.1 = (bf16[1024,256]{1,0:T(8,128)(2,1)S(1)}, bf16[1024,256]{1,0:T(8,128)(2,1)}, u32[]{:S(2)}) copy-start(bf16[1024,256]{1,0:T(8,128)(2,1)} %cotangents.1) | copy-start | bytes 1572868
  0.7 12.3 %collective-permute-start = (bf16[1024,256]{1,0:T(8,128)(2,1)}, bf16[1024,256]{1,0:T(8,128)(2,1)}, u32[]{:S(2)}, u32[]{:S(2)}) collective-permute-start(bf16[1024,256]{1,0:T(8,128)(2,1)} %queries.1), channel_id=1, source_target_pairs={{1,129},{128,0},{3,131},{130,2},{5,133},{132,4},{7,135},{134,6},{9... | collective-permute-start | bytes 1572872 | tf_op jit(solution)/shard_map/ppermute | solution.py:57
  2.1 19.2 %collective-permute-start.2 = (bf16[1024,256]{1,0:T(8,128)(2,1)}, bf16[1024,256]{1,0:T(8,128)(2,1)}, u32[]{:S(2)}, u32[]{:S(2)}) collective-permute-start(bf16[1024,256]{1,0:T(8,128)(2,1)} %cotangents.1), channel_id=1, source_target_pairs={{1,129},{128,0},{3,131},{130,2},{5,133},{132,4},{7,135},{134,6},{9... | collective-permute-start | bytes 1572872 | tf_op jit(solution)/shard_map/ppermute | solution.py:57
  6.0 25.5 %all-to-all-start = ((bf16[8,2,128,256]{3,2,1,0:T(8,128)(2,1)}), bf16[8,2,128,256]{3,2,1,0:T(8,128)(2,1)S(1)}, u32[]{:S(2)}, u32[]{:S(2)}) async-start(bf16[8,2,128,256]{3,2,1,0:T(8,128)(2,1)} %pack.1), calls=%async_computation | async-start | bytes 2097152 | tf_op jit(solution)/shard_map/all_to_all | solution.py:37
  13.0 9.6 %collective-permute-start.1 = (bf16[1024,256]{1,0:T(8,128)(2,1)}, bf16[1024,256]{1,0:T(8,128)(2,1)S(1)}, u32[]{:S(2)}, u32[]{:S(2)}) collective-permute-start(bf16[1024,256]{1,0:T(8,128)(2,1)} %collective-permute-done), channel_id=1, source_target_pairs={{129,128},{0,1},{131,130},{2,3},{133,132},{4,5},{135,134},{6,7},{1... | collective-permute-start | bytes 1572872 | tf_op jit(solution)/shard_map/ppermute | solution.py:57
  21.3 3.0 %collective-permute-start.3 = (bf16[1024,256]{1,0:T(8,128)(2,1)}, bf16[1024,256]{1,0:T(8,128)(2,1)S(1)}, u32[]{:S(2)}, u32[]{:S(2)}) collective-permute-start(bf16[1024,256]{1,0:T(8,128)(2,1)} %collective-permute-done.2), channel_id=1, source_target_pairs={{129,128},{0,1},{131,130},{2,3},{133,132},{4,5},{135,134},{6,7},{1... | collective-permute-start | bytes 1572872 | tf_op jit(solution)/shard_map/ppermute | solution.py:57
  31.5 3.0 %collective-permute-start.4 = (bf16[8,2,128,256]{3,2,1,0:T(8,128)(2,1)S(1)}, bf16[8,2,128,256]{3,2,1,0:T(8,128)(2,1)S(1)}, u32[]{:S(2)}, u32[]{:S(2)}) collective-permute-start(bf16[8,2,128,256]{3,2,1,0:T(8,128)(2,1)S(1)} %all-to-all-done.own), channel_id=1, source_target_pairs={{0,1},{1,0},{2,3},{3,2},{4,5},{5,4},{6,7},{7,6},{8,9},{9,8},{10,11... | collective-permute-start | bytes 3145736 | tf_op jit(solution)/shard_map/ppermute | solution.py:33
  40.0 2.7 %collective-permute-start.6 = (bf16[8,2,128,256]{3,2,1,0:T(8,128)(2,1)S(1)}, bf16[8,2,128,256]{3,2,1,0:T(8,128)(2,1)S(1)}, u32[]{:S(2)}, u32[]{:S(2)}) collective-permute-start(bf16[8,2,128,256]{3,2,1,0:T(8,128)(2,1)S(1)} %get-tuple-element.41), channel_id=1, source_target_pairs={{0,1},{1,0},{2,3},{3,2},{4,5},{5,4},{6,7},{7,6},{8,9},{9,8},{10,11... | collective-permute-start | bytes 3145736 | tf_op jit(solution)/shard_map/ppermute | solution.py:33
  41.8 32.1 %collective-permute-start.5 = (bf16[2,1024,256]{2,1,0:T(8,128)(2,1)S(1)}, bf16[2,1024,256]{2,1,0:T(8,128)(2,1)S(1)}, u32[]{:S(2)}, u32[]{:S(2)}) collective-permute-start(bf16[2,1024,256]{2,1,0:T(8,128)(2,1)S(1)} %queries_step.1.mine), channel_id=1, source_target_pairs={{1,128},{128,1},{3,130},{130,3},{5,132},{132,5},{7,134},{134,7},{9... | collective-permute-start | bytes 3145736 | tf_op jit(solution)/shard_map/ppermute | solution.py:47
  43.0 13.9 %collective-permute-start.7 = (bf16[2,2,128,256]{3,2,1,0:T(8,128)(2,1)S(1)}, bf16[2,2,128,256]{3,2,1,0:T(8,128)(2,1)S(1)}, u32[]{:S(2)}, u32[]{:S(2)}) collective-permute-start(bf16[2,2,128,256]{3,2,1,0:T(8,128)(2,1)S(1)} %get-tuple-element.43), channel_id=1, source_target_pairs={{0,16},{1,17},{2,18},{3,19},{4,20},{5,21},{6,22},{7,23},{8,24},{9,... | collective-permute-start | bytes 786440 | tf_op jit(solution)/shard_map/ppermute | solution.py:33
  45.0 11.9 %collective-permute-start.8 = (bf16[2,2,128,256]{3,2,1,0:T(8,128)(2,1)S(1)}, bf16[2,2,128,256]{3,2,1,0:T(8,128)(2,1)S(1)}, u32[]{:S(2)}, u32[]{:S(2)}) collective-permute-start(bf16[2,2,128,256]{3,2,1,0:T(8,128)(2,1)S(1)} %get-tuple-element.44), channel_id=1, source_target_pairs={{0,112},{1,113},{2,114},{3,115},{4,116},{5,117},{6,118},{7,119},{8... | collective-permute-start | bytes 786440 | tf_op jit(solution)/shard_map/ppermute | solution.py:33
  45.1 11.8 %collective-permute-start.9 = (bf16[2,128,256]{2,1,0:T(8,128)(2,1)S(1)}, bf16[2,128,256]{2,1,0:T(8,128)(2,1)S(1)}, u32[]{:S(2)}, u32[]{:S(2)}) collective-permute-start(bf16[2,128,256]{2,1,0:T(8,128)(2,1)S(1)} %get-tuple-element.47), channel_id=1, source_target_pairs={{0,32},{1,97},{2,34},{3,99},{4,36},{5,101},{6,38},{7,103},{8,40},{... | collective-permute-start | bytes 393224 | tf_op jit(solution)/shard_map/ppermute | solution.py:33
  57.0 11.3 %collective-permute-start.10 = (bf16[2,128,256]{2,1,0:T(8,128)(2,1)S(1)}, bf16[2,128,256]{2,1,0:T(8,128)(2,1)S(1)}, u32[]{:S(2)}, u32[]{:S(2)}) collective-permute-start(bf16[2,128,256]{2,1,0:T(8,128)(2,1)S(1)} %get-tuple-element.48), channel_id=1, source_target_pairs={{0,32},{1,33},{2,34},{3,35},{4,36},{5,37},{6,38},{7,39},{8,40},{9,... | collective-permute-start | bytes 393224 | tf_op jit(solution)/shard_map/ppermute | solution.py:33
  58.5 9.7 %collective-permute-start.11 = (bf16[2,128,256]{2,1,0:T(8,128)(2,1)S(1)}, bf16[2,128,256]{2,1,0:T(8,128)(2,1)S(1)}, u32[]{:S(2)}, u32[]{:S(2)}) collective-permute-start(bf16[2,128,256]{2,1,0:T(8,128)(2,1)S(1)} %get-tuple-element.49), channel_id=1, source_target_pairs={{0,96},{1,97},{2,98},{3,99},{4,100},{5,101},{6,102},{7,103},{8,104... | collective-permute-start | bytes 393224 | tf_op jit(solution)/shard_map/ppermute | solution.py:33
  69.0 12.9 %all-to-all-start.1 = ((bf16[16,16,256]{2,1,0:T(8,128)(2,1)}), bf16[16,16,256]{2,1,0:T(8,128)(2,1)S(1)}, u32[]{:S(2)}, u32[]{:S(2)}) async-start(bf16[16,16,256]{2,1,0:T(8,128)(2,1)} %last_sum.1), calls=%async_computation.1 | async-start | bytes 262144 | tf_op jit(solution)/shard_map/all_to_all | solution.py:37

commit v7 on v6

--- a/solution.py
+++ b/solution.py
@@ -53,6 +53,7 @@
         for xl in range(X_LO):
             middle = device(1 - xl, z, y, xh, 1 - xl)
             over.append((device(xl, z, y, xh, 1 - xl), middle))
+            over.append((device(xl, z, y, xh, xl), device(xl, z, y, xh, 1 - xl)))
             home.append((middle, device(1 - xl, z, y, xh, xl)))
     return lax.ppermute(lax.ppermute(array, AXES, over), AXES, home)
 
@@ -86,19 +87,26 @@
     return pltpu.CompilerParams(vmem_limit_bytes=mib * 1024 * 1024)
 
 
-def pack_kernel(keys, values, out, held, sems):
+def pack_kernel(keys, values, out, held, packed, sems):
     xl, _, _ = position()
-    copies = [
-        pltpu.make_async_copy(source, held.at[kind], sems.at[kind])
-        for kind, source in enumerate((keys, values))
-    ]
-    for copy in copies:
-        copy.start()
-    for kind, copy in enumerate(copies):
-        copy.wait()
+    half = keys.shape[0] // 2
+    pieces = [(kind, pl.ds(i * half, half)) for kind in range(2) for i in range(2)]
+    loads, stores = [], []
+    for at, (kind, rows) in enumerate(pieces):
+        source = (keys, values)[kind].at[rows]
+        loads.append(pltpu.make_async_copy(source, held.at[kind, rows], sems.at[0, at]))
+        stores.append(
+            pltpu.make_async_copy(packed.at[:, kind, rows], out.at[:, kind, rows], sems.at[1, at])
+        )
+        loads[at].start()
+    for at, (kind, rows) in enumerate(pieces):
+        loads[at].wait()
         for chip in range(Y * X_HI):
             start = pl.multiple_of((chip * 2 + xl) * HEAD_DIM, HEAD_DIM)
-            out[chip, kind] = held[kind, :, pl.ds(start, HEAD_DIM)]
+            packed[chip, kind, rows] = held[kind, rows, pl.ds(start, HEAD_DIM)]
+        stores[at].start()
+    for store in stores:
+        store.wait()
 
 
 def pack(keys, values):
@@ -107,10 +115,11 @@
         pack_kernel,
         out_shape=jax.ShapeDtypeStruct(shape, keys.dtype),
         in_specs=[ANY, ANY],
-        out_specs=VMEM,
+        out_specs=ANY,
         scratch_shapes=[
             pltpu.VMEM((2,) + keys.shape, keys.dtype),
-            pltpu.SemaphoreType.DMA((2,)),
+            pltpu.VMEM(shape, keys.dtype),
+            pltpu.SemaphoreType.DMA((2, 4)),
         ],
         compiler_params=params(56),
         name="pack",

time: 83 us -> 81.3 us (0.980)
  starting transfers between devices: 33.1 us -> 29.8 us
  waiting for transfers between devices: 34 us -> 36 us
    ppermute x4, starting transfers between devices: 8.63 us -> 4.77 us  [trade_in_two(): return lax.ppermute(lax.ppermute(array, AXES, over), AXES, home)]
    ppermute x4, waiting for transfers between devices: 5.39 us -> 7.38 us  [trade_in_two(): return lax.ppermute(lax.ppermute(array, AXES, over), AXES, home)]
  transfers between devices with their start and end apart: 14 -> 14, of which waited for: 7 -> 6; matrix products, arithmetic and copies ran while one was open for 0% -> 0% of each run, Pallas kernels for 10% -> 10%
where the time goes in v7:
time: 81.3 us; the launch traced here: 81 us
  waiting for transfers between devices  36 us (44%)
  starting transfers between devices  29.8 us (37%)
  Pallas kernels  14.4 us (18%)
    all_to_all x2, waiting for transfers between devices, exchange(): lax.all_to_all(array, AXES, split_axis=0, concat_axis=0, axis_index_group...  14.3 us
    ppermute x7, waiting for transfers between devices, permute(): return lax.ppermute(array, AXES, pairs)  14.3 us
    all_to_all x2, starting transfers between devices, exchange(): lax.all_to_all(array, AXES, split_axis=0, concat_axis=0, axis_index_group...  12.1 us
    ppermute x7, starting transfers between devices, permute(): return lax.ppermute(array, AXES, pairs)  12 us
    ppermute x4, waiting for transfers between devices, trade_in_two(): return lax.ppermute(lax.ppermute(array, AXES, over), AXES, home)  7.38 us
    pallas_call x1, Pallas kernels, both_halves(): pl.pallas_call(both_halves_kernel, out_shape=(jax.ShapeDtypeStruct((rows,...  5.47 us
    ppermute x4, starting transfers between devices, trade_in_two(): return lax.ppermute(lax.ppermute(array, AXES, over), AXES, home)  4.77 us
    pallas_call x1, Pallas kernels, pack(): pl.pallas_call(pack_kernel, out_shape=jax.ShapeDtypeStruct(shape, keys.dt...  2.32 us
  transfers between devices with their start and end apart: 14, of which 6 were waited for; matrix products, arithmetic and copies ran while one was open for 0% of the time, Pallas kernels for 10%

profile of v7, /device:TPU:32, one launch (start us, length us, event | category | flops | bytes accessed | tf_op | source)
XLA Modules:
  0.0 81.0 jit_solution(5580063964446108981)
XLA Ops:
  0.7 0.1 collective-permute-start
  0.8 1.0 %collective-permute-start.2 = (bf16[1024,256]{1,0:T(8,128)(2,1)}, bf16[1024,256]{1,0:T(8,128)(2,1)}, u32[]{:S(2)}, u32[]{:S(2)}) collective-permute-start(bf16[1024,256]{1,0:T(8,128)(2,1)} %cotangents.1), channel_id=1, source_target_pairs={{1,129},{0,1},{128,0},{129,128},{3,131},{2,3},{130,2},{131,130},{5... | collective-permute-start | bytes 1572872 | tf_op jit(solution)/shard_map/ppermute | solution.py:58
  1.8 2.3 %pack.1 = bf16[8,2,128,256]{3,2,1,0:T(8,128)(2,1)} custom-call(bf16[128,4096]{1,0:T(8,128)(2,1)} %keys.1, bf16[128,4096]{1,0:T(8,128)(2,1)} %values.1), custom_call_target="tpu_custom_call" | custom-call | tf_op jit(solution)/shard_map/pack/pallas_call | solution.py:114
  4.1 6.6 %all-to-all-start = ((bf16[8,2,128,256]{3,2,1,0:T(8,128)(2,1)}), bf16[8,2,128,256]{3,2,1,0:T(8,128)(2,1)S(1)}, u32[]{:S(2)}, u32[]{:S(2)}) async-start(bf16[8,2,128,256]{3,2,1,0:T(8,128)(2,1)} %pack.1), calls=%async_computation | async-start | bytes 2097152 | tf_op jit(solution)/shard_map/all_to_all | solution.py:37
  10.8 0.0 collective-permute-done
  10.8 2.3 %collective-permute-start.1 = (bf16[1024,256]{1,0:T(8,128)(2,1)}, bf16[1024,256]{1,0:T(8,128)(2,1)S(1)}, u32[]{:S(2)}, u32[]{:S(2)}) collective-permute-start(bf16[1024,256]{1,0:T(8,128)(2,1)} %collective-permute-done), channel_id=1, source_target_pairs={{129,128},{0,1},{131,130},{2,3},{133,132},{4,5},{135,134},{6,7},{1... | collective-permute-start | bytes 1572872 | tf_op jit(solution)/shard_map/ppermute | solution.py:58
  13.1 5.7 %collective-permute-done.2 = bf16[1024,256]{1,0:T(8,128)(2,1)} collective-permute-done((bf16[1024,256]{1,0:T(8,128)(2,1)}, bf16[1024,256]{1,0:T(8,128)(2,1)}, u32[]{:S(2)}, u32[]{:S(2)}) %collective-permute-start.2) | collective-permute-done | bytes 524320 | tf_op jit(solution)/shard_map/ppermute | solution.py:58
  18.8 1.3 %collective-permute-start.3 = (bf16[1024,256]{1,0:T(8,128)(2,1)}, bf16[1024,256]{1,0:T(8,128)(2,1)S(1)}, u32[]{:S(2)}, u32[]{:S(2)}) collective-permute-start(bf16[1024,256]{1,0:T(8,128)(2,1)} %collective-permute-done.2), channel_id=1, source_target_pairs={{129,128},{0,1},{131,130},{2,3},{133,132},{4,5},{135,134},{6,7},{1... | collective-permute-start | bytes 1572872 | tf_op jit(solution)/shard_map/ppermute | solution.py:58
  20.1 1.7 %collective-permute-done.3.do_came = bf16[1024,256]{1,0:T(8,128)(2,1)S(1)} collective-permute-done((bf16[1024,256]{1,0:T(8,128)(2,1)}, bf16[1024,256]{1,0:T(8,128)(2,1)S(1)}, u32[]{:S(2)}, u32[]{:S(2)}) %collective-permute-start.3) | collective-permute-done | bytes 524320 | tf_op jit(solution)/shard_map/ppermute | solution.py:58
  21.8 0.2 select.1
  22.0 7.4 %all-to-all-done.own = bf16[8,2,128,256]{3,2,1,0:T(8,128)(2,1)S(1)} async-done(((bf16[8,2,128,256]{3,2,1,0:T(8,128)(2,1)}), bf16[8,2,128,256]{3,2,1,0:T(8,128)(2,1)S(1)}, u32[]{:S(2)}, u32[]{:S(2)}) %all-to-all-start) | async-done | bytes 1048608 | tf_op jit(solution)/shard_map/all_to_all | solution.py:37
  29.4 0.9 %collective-permute-start.4 = (bf16[8,2,128,256]{3,2,1,0:T(8,128)(2,1)S(1)}, bf16[8,2,128,256]{3,2,1,0:T(8,128)(2,1)S(1)}, u32[]{:S(2)}, u32[]{:S(2)}) collective-permute-start(bf16[8,2,128,256]{3,2,1,0:T(8,128)(2,1)S(1)} %all-to-all-done.own), channel_id=1, source_target_pairs={{0,1},{1,0},{2,3},{3,2},{4,5},{5,4},{6,7},{7,6},{8,9},{9,8},{10,11... | collective-permute-start | bytes 3145736 | tf_op jit(solution)/shard_map/ppermute | solution.py:33
  30.3 2.3 %own_half.1 = (bf16[1024,1024]{1,0:T(8,128)(2,1)S(1)}, f32[256,1024]{1,0:T(8,128)S(1)}, f32[16,1024]{1,0:T(8,128)S(1)}) custom-call(bf16[1024,256]{1,0:T(8,128)(2,1)S(1)} %get-tuple-element.31.queries, bf16[8,2,128,256]{3,2,1,0:T(8,128)(2,1)S(1)} %all-to-all-done.own), custom_call_target="tpu_custom_call" | custom-call | flops 1073741824 | bytes 2097152 | tf_op jit(solution)/shard_map/own_half/pallas_call | solution.py:351
  32.6 5.5 %both_halves.1 = (bf16[1024,256]{1,0:T(8,128)(2,1)S(1)}, bf16[2048,1024]{1,0:T(8,128)(2,1)S(1)}, bf16[8,2,128,256]{3,2,1,0:T(8,128)(2,1)S(1)}, bf16[8,2,128,256]{3,2,1,0:T(8,128)(2,1)S(1)}) custom-call(bf16[1024,256]{1,0:T(8,128)(2,1)S(1)} %get-tuple-element.31.queries, bf16[1024,256]{1,0:T(8,128)(2,1)S(1)} %get-tuple-element.32.cotangents, ...), custom_call_target="tpu_custom_call" | custom-call | flops 3221225472 | bytes 4194304 | tf_op jit(solution)/shard_map/both_halves/pallas_call | solution.py:407
  38.1 0.4 collective-permute-start.6
  38.5 1.4 %queries_step.1.mine = bf16[2,1024,256]{2,1,0:T(8,128)(2,1)S(1)} custom-call(bf16[8,2,128,256]{3,2,1,0:T(8,128)(2,1)S(1)} %all-to-all-done.own, bf16[8,2,128,256]{3,2,1,0:T(8,128)(2,1)S(1)} %collective-permute-done.4.other, bf16[2048,1024]{1,0:T(8,128)(2,1)S(1)} %get-tuple-element.36.ds_ref, bf16[1024,256]{1,0:T(8,128)(2,1)S(1)} %get-tuple-element.37.att_ref), custom_call_target="tpu_custom_call" | custom-call | flops 1073741824 | bytes 2097152 | tf_op jit(solution)/shard_map/queries_step/pallas_call | solution.py:441
  39.9 0.9 %collective-permute-start.5 = (bf16[2,1024,256]{2,1,0:T(8,128)(2,1)S(1)}, bf16[2,1024,256]{2,1,0:T(8,128)(2,1)S(1)}, u32[]{:S(2)}, u32[]{:S(2)}) collective-permute-start(bf16[2,1024,256]{2,1,0:T(8,128)(2,1)S(1)} %queries_step.1.mine), channel_id=1, source_target_pairs={{1,128},{128,1},{3,130},{130,3},{5,132},{132,5},{7,134},{134,7},{9... | collective-permute-start | bytes 3145736 | tf_op jit(solution)/shard_map/ppermute | solution.py:47
  40.8 0.0 collective-permute-done.6.came
  40.8 0.2 core_sum.1
  41.1 2.0 %collective-permute-start.7 = (bf16[2,2,128,256]{3,2,1,0:T(8,128)(2,1)S(1)}, bf16[2,2,128,256]{3,2,1,0:T(8,128)(2,1)S(1)}, u32[]{:S(2)}, u32[]{:S(2)}) collective-permute-start(bf16[2,2,128,256]{3,2,1,0:T(8,128)(2,1)S(1)} %get-tuple-element.43), channel_id=1, source_target_pairs={{0,16},{1,17},{2,18},{3,19},{4,20},{5,21},{6,22},{7,23},{8,24},{9,... | collective-permute-start | bytes 786440 | tf_op jit(solution)/shard_map/ppermute | solution.py:33
  43.1 0.1 collective-permute-start.8
  43.2 4.4 %collective-permute-start.9 = (bf16[2,128,256]{2,1,0:T(8,128)(2,1)S(1)}, bf16[2,128,256]{2,1,0:T(8,128)(2,1)S(1)}, u32[]{:S(2)}, u32[]{:S(2)}) collective-permute-start(bf16[2,128,256]{2,1,0:T(8,128)(2,1)S(1)} %get-tuple-element.47), channel_id=1, source_target_pairs={{0,32},{1,97},{2,34},{3,99},{4,36},{5,101},{6,38},{7,103},{8,40},{... | collective-permute-start | bytes 393224 | tf_op jit(solution)/shard_map/ppermute | solution.py:33
  47.6 7.2 %collective-permute-done.9.across = bf16[2,128,256]{2,1,0:T(8,128)(2,1)S(1)} collective-permute-done((bf16[2,128,256]{2,1,0:T(8,128)(2,1)S(1)}, bf16[2,128,256]{2,1,0:T(8,128)(2,1)S(1)}, u32[]{:S(2)}, u32[]{:S(2)}) %collective-permute-start.9) | collective-permute-done | bytes 131104 | tf_op jit(solution)/shard_map/ppermute | solution.py:33
  54.8 0.1 middle_sum.1
  54.9 1.5 %collective-permute-start.10 = (bf16[2,128,256]{2,1,0:T(8,128)(2,1)S(1)}, bf16[2,128,256]{2,1,0:T(8,128)(2,1)S(1)}, u32[]{:S(2)}, u32[]{:S(2)}) collective-permute-start(bf16[2,128,256]{2,1,0:T(8,128)(2,1)S(1)} %get-tuple-element.48), channel_id=1, source_target_pairs={{0,32},{1,33},{2,34},{3,35},{4,36},{5,37},{6,38},{7,39},{8,40},{9,... | collective-permute-start | bytes 393224 | tf_op jit(solution)/shard_map/ppermute | solution.py:33
  56.4 2.7 %collective-permute-start.11 = (bf16[2,128,256]{2,1,0:T(8,128)(2,1)S(1)}, bf16[2,128,256]{2,1,0:T(8,128)(2,1)S(1)}, u32[]{:S(2)}, u32[]{:S(2)}) collective-permute-start(bf16[2,128,256]{2,1,0:T(8,128)(2,1)S(1)} %get-tuple-element.49), channel_id=1, source_target_pairs={{0,96},{1,97},{2,98},{3,99},{4,100},{5,101},{6,102},{7,103},{8,104... | collective-permute-start | bytes 393224 | tf_op jit(solution)/shard_map/ppermute | solution.py:33
  59.1 7.0 %collective-permute-done.10.low = bf16[2,128,256]{2,1,0:T(8,128)(2,1)S(1)} collective-permute-done((bf16[2,128,256]{2,1,0:T(8,128)(2,1)S(1)}, bf16[2,128,256]{2,1,0:T(8,128)(2,1)S(1)}, u32[]{:S(2)}, u32[]{:S(2)}) %collective-permute-start.10) | collective-permute-done | bytes 131104 | tf_op jit(solution)/shard_map/ppermute | solution.py:33
  66.1 0.7 last_sum.1
  66.8 5.5 %all-to-all-start.1 = ((bf16[16,16,256]{2,1,0:T(8,128)(2,1)}), bf16[16,16,256]{2,1,0:T(8,128)(2,1)S(1)}, u32[]{:S(2)}, u32[]{:S(2)}) async-start(bf16[16,16,256]{2,1,0:T(8,128)(2,1)} %last_sum.1), calls=%async_computation.1 | async-start | bytes 262144 | tf_op jit(solution)/shard_map/all_to_all | solution.py:37
  72.3 1.1 %unpack.1 = (bf16[1024,256]{1,0:T(8,128)(2,1)}, bf16[1024,256]{1,0:T(8,128)(2,1)}) custom-call(bf16[2,1024,256]{2,1,0:T(8,128)(2,1)S(1)} %queries_step.1.mine, bf16[2,1024,256]{2,1,0:T(8,128)(2,1)S(1)} %collective-permute-done.5.came), custom_call_target="tpu_custom_call" | custom-call | tf_op jit(solution)/shard_map/unpack/pallas_call | solution.py:159
  73.4 6.9 %all-to-all-done.1.parts = bf16[16,16,256]{2,1,0:T(8,128)(2,1)S(1)} async-done(((bf16[16,16,256]{2,1,0:T(8,128)(2,1)}), bf16[16,16,256]{2,1,0:T(8,128)(2,1)S(1)}, u32[]{:S(2)}, u32[]{:S(2)}) %all-to-all-start.1) | async-done | bytes 131104 | tf_op jit(solution)/shard_map/all_to_all | solution.py:37
  80.3 0.7 columns.1
  (10 shorter events, 0.0 us)
Async XLA Ops:
  0.6 21.2 %copy-start = (bf16[1024,256]{1,0:T(8,128)(2,1)S(1)}, bf16[1024,256]{1,0:T(8,128)(2,1)}, u32[]{:S(2)}) copy-start(bf16[1024,256]{1,0:T(8,128)(2,1)} %queries.1) | copy-start | bytes 1572868
  0.6 21.2 %copy-start.1 = (bf16[1024,256]{1,0:T(8,128)(2,1)S(1)}, bf16[1024,256]{1,0:T(8,128)(2,1)}, u32[]{:S(2)}) copy-start(bf16[1024,256]{1,0:T(8,128)(2,1)} %cotangents.1) | copy-start | bytes 1572868
  0.7 10.1 %collective-permute-start = (bf16[1024,256]{1,0:T(8,128)(2,1)}, bf16[1024,256]{1,0:T(8,128)(2,1)}, u32[]{:S(2)}, u32[]{:S(2)}) collective-permute-start(bf16[1024,256]{1,0:T(8,128)(2,1)} %queries.1), channel_id=1, source_target_pairs={{1,129},{0,1},{128,0},{129,128},{3,131},{2,3},{130,2},{131,130},{5... | collective-permute-start | bytes 1572872 | tf_op jit(solution)/shard_map/ppermute | solution.py:58
  0.8 18.0 %collective-permute-start.2 = (bf16[1024,256]{1,0:T(8,128)(2,1)}, bf16[1024,256]{1,0:T(8,128)(2,1)}, u32[]{:S(2)}, u32[]{:S(2)}) collective-permute-start(bf16[1024,256]{1,0:T(8,128)(2,1)} %cotangents.1), channel_id=1, source_target_pairs={{1,129},{0,1},{128,0},{129,128},{3,131},{2,3},{130,2},{131,130},{5... | collective-permute-start | bytes 1572872 | tf_op jit(solution)/shard_map/ppermute | solution.py:58
  4.1 25.3 %all-to-all-start = ((bf16[8,2,128,256]{3,2,1,0:T(8,128)(2,1)}), bf16[8,2,128,256]{3,2,1,0:T(8,128)(2,1)S(1)}, u32[]{:S(2)}, u32[]{:S(2)}) async-start(bf16[8,2,128,256]{3,2,1,0:T(8,128)(2,1)} %pack.1), calls=%async_computation | async-start | bytes 2097152 | tf_op jit(solution)/shard_map/all_to_all | solution.py:37
  10.8 9.3 %collective-permute-start.1 = (bf16[1024,256]{1,0:T(8,128)(2,1)}, bf16[1024,256]{1,0:T(8,128)(2,1)S(1)}, u32[]{:S(2)}, u32[]{:S(2)}) collective-permute-start(bf16[1024,256]{1,0:T(8,128)(2,1)} %collective-permute-done), channel_id=1, source_target_pairs={{129,128},{0,1},{131,130},{2,3},{133,132},{4,5},{135,134},{6,7},{1... | collective-permute-start | bytes 1572872 | tf_op jit(solution)/shard_map/ppermute | solution.py:58
  18.8 3.0 %collective-permute-start.3 = (bf16[1024,256]{1,0:T(8,128)(2,1)}, bf16[1024,256]{1,0:T(8,128)(2,1)S(1)}, u32[]{:S(2)}, u32[]{:S(2)}) collective-permute-start(bf16[1024,256]{1,0:T(8,128)(2,1)} %collective-permute-done.2), channel_id=1, source_target_pairs={{129,128},{0,1},{131,130},{2,3},{133,132},{4,5},{135,134},{6,7},{1... | collective-permute-start | bytes 1572872 | tf_op jit(solution)/shard_map/ppermute | solution.py:58
  29.4 3.2 %collective-permute-start.4 = (bf16[8,2,128,256]{3,2,1,0:T(8,128)(2,1)S(1)}, bf16[8,2,128,256]{3,2,1,0:T(8,128)(2,1)S(1)}, u32[]{:S(2)}, u32[]{:S(2)}) collective-permute-start(bf16[8,2,128,256]{3,2,1,0:T(8,128)(2,1)S(1)} %all-to-all-done.own), channel_id=1, source_target_pairs={{0,1},{1,0},{2,3},{3,2},{4,5},{5,4},{6,7},{7,6},{8,9},{9,8},{10,11... | collective-permute-start | bytes 3145736 | tf_op jit(solution)/shard_map/ppermute | solution.py:33
  38.1 2.7 %collective-permute-start.6 = (bf16[8,2,128,256]{3,2,1,0:T(8,128)(2,1)S(1)}, bf16[8,2,128,256]{3,2,1,0:T(8,128)(2,1)S(1)}, u32[]{:S(2)}, u32[]{:S(2)}) collective-permute-start(bf16[8,2,128,256]{3,2,1,0:T(8,128)(2,1)S(1)} %get-tuple-element.41), channel_id=1, source_target_pairs={{0,1},{1,0},{2,3},{3,2},{4,5},{5,4},{6,7},{7,6},{8,9},{9,8},{10,11... | collective-permute-start | bytes 3145736 | tf_op jit(solution)/shard_map/ppermute | solution.py:33
  39.9 32.4 %collective-permute-start.5 = (bf16[2,1024,256]{2,1,0:T(8,128)(2,1)S(1)}, bf16[2,1024,256]{2,1,0:T(8,128)(2,1)S(1)}, u32[]{:S(2)}, u32[]{:S(2)}) collective-permute-start(bf16[2,1024,256]{2,1,0:T(8,128)(2,1)S(1)} %queries_step.1.mine), channel_id=1, source_target_pairs={{1,128},{128,1},{3,130},{130,3},{5,132},{132,5},{7,134},{134,7},{9... | collective-permute-start | bytes 3145736 | tf_op jit(solution)/shard_map/ppermute | solution.py:47
  41.1 13.7 %collective-permute-start.7 = (bf16[2,2,128,256]{3,2,1,0:T(8,128)(2,1)S(1)}, bf16[2,2,128,256]{3,2,1,0:T(8,128)(2,1)S(1)}, u32[]{:S(2)}, u32[]{:S(2)}) collective-permute-start(bf16[2,2,128,256]{3,2,1,0:T(8,128)(2,1)S(1)} %get-tuple-element.43), channel_id=1, source_target_pairs={{0,16},{1,17},{2,18},{3,19},{4,20},{5,21},{6,22},{7,23},{8,24},{9,... | collective-permute-start | bytes 786440 | tf_op jit(solution)/shard_map/ppermute | solution.py:33
  43.1 11.7 %collective-permute-start.8 = (bf16[2,2,128,256]{3,2,1,0:T(8,128)(2,1)S(1)}, bf16[2,2,128,256]{3,2,1,0:T(8,128)(2,1)S(1)}, u32[]{:S(2)}, u32[]{:S(2)}) collective-permute-start(bf16[2,2,128,256]{3,2,1,0:T(8,128)(2,1)S(1)} %get-tuple-element.44), channel_id=1, source_target_pairs={{0,112},{1,113},{2,114},{3,115},{4,116},{5,117},{6,118},{7,119},{8... | collective-permute-start | bytes 786440 | tf_op jit(solution)/shard_map/ppermute | solution.py:33
  43.2 11.6 %collective-permute-start.9 = (bf16[2,128,256]{2,1,0:T(8,128)(2,1)S(1)}, bf16[2,128,256]{2,1,0:T(8,128)(2,1)S(1)}, u32[]{:S(2)}, u32[]{:S(2)}) collective-permute-start(bf16[2,128,256]{2,1,0:T(8,128)(2,1)S(1)} %get-tuple-element.47), channel_id=1, source_target_pairs={{0,32},{1,97},{2,34},{3,99},{4,36},{5,101},{6,38},{7,103},{8,40},{... | collective-permute-start | bytes 393224 | tf_op jit(solution)/shard_map/ppermute | solution.py:33
  54.9 11.2 %collective-permute-start.10 = (bf16[2,128,256]{2,1,0:T(8,128)(2,1)S(1)}, bf16[2,128,256]{2,1,0:T(8,128)(2,1)S(1)}, u32[]{:S(2)}, u32[]{:S(2)}) collective-permute-start(bf16[2,128,256]{2,1,0:T(8,128)(2,1)S(1)} %get-tuple-element.48), channel_id=1, source_target_pairs={{0,32},{1,33},{2,34},{3,35},{4,36},{5,37},{6,38},{7,39},{8,40},{9,... | collective-permute-start | bytes 393224 | tf_op jit(solution)/shard_map/ppermute | solution.py:33
  56.4 9.7 %collective-permute-start.11 = (bf16[2,128,256]{2,1,0:T(8,128)(2,1)S(1)}, bf16[2,128,256]{2,1,0:T(8,128)(2,1)S(1)}, u32[]{:S(2)}, u32[]{:S(2)}) collective-permute-start(bf16[2,128,256]{2,1,0:T(8,128)(2,1)S(1)} %get-tuple-element.49), channel_id=1, source_target_pairs={{0,96},{1,97},{2,98},{3,99},{4,100},{5,101},{6,102},{7,103},{8,104... | collective-permute-start | bytes 393224 | tf_op jit(solution)/shard_map/ppermute | solution.py:33
  66.8 13.5 %all-to-all-start.1 = ((bf16[16,16,256]{2,1,0:T(8,128)(2,1)}), bf16[16,16,256]{2,1,0:T(8,128)(2,1)S(1)}, u32[]{:S(2)}, u32[]{:S(2)}) async-start(bf16[16,16,256]{2,1,0:T(8,128)(2,1)} %last_sum.1), calls=%async_computation.1 | async-start | bytes 262144 | tf_op jit(solution)/shard_map/all_to_all | solution.py:37

commit v8 on v7

--- a/solution.py
+++ b/solution.py
@@ -39,23 +39,20 @@
     )
 
 
-def trade(array):
-    pairs = []
-    for z, y, xh in itertools.product(range(Z), range(Y), range(X_HI)):
-        one, two = device(0, z, y, xh, 1), device(1, z, y, xh, 0)
-        pairs += [(one, two), (two, one)]
-    return lax.ppermute(array, AXES, pairs)
-
-
-def trade_in_two(array):
-    over, home = [], []
-    for z, y, xh in itertools.product(range(Z), range(Y), range(X_HI)):
-        for xl in range(X_LO):
-            middle = device(1 - xl, z, y, xh, 1 - xl)
-            over.append((device(xl, z, y, xh, 1 - xl), middle))
-            over.append((device(xl, z, y, xh, xl), device(xl, z, y, xh, 1 - xl)))
-            home.append((middle, device(1 - xl, z, y, xh, xl)))
-    return lax.ppermute(lax.ppermute(array, AXES, over), AXES, home)
+def cross_from_other(xl, z, y, xh, c):
+    return (xl, z, y, xh, 1 - c) if c == xl else (1 - xl, z, y, xh, c)
+
+
+def cross_from_same(xl, z, y, xh, c):
+    return (1 - xl, z, y, xh, c) if c == xl else (xl, z, y, xh, 1 - c)
+
+
+def trade_in(array):
+    return permute(permute(array, cross_from_other), other_core)
+
+
+def trade_out(array):
+    return permute(permute(array, other_core), cross_from_same)
 
 
 def other_core(xl, z, y, xh, c):
@@ -452,14 +449,14 @@
 
 
 def per_device(queries, mem_keys, mem_values, grad_out):
-    q, do = select(queries, grad_out, trade_in_two(queries), trade_in_two(grad_out))
+    q, do = select(queries, grad_out, trade_in(queries), trade_in(grad_out))
     own = exchange(pack(mem_keys, mem_values), head_groups())
     own, q, do = lax.optimization_barrier((own, q, do))
     other = permute(own, other_core)
     att, ds, keep, send = both_halves(q, do, own, other, *own_half(q, own))
     came = permute(send, other_core)
     rows = queries_step(own, other, ds, att)
-    traded = trade(rows)
+    traded = trade_out(rows)
     sums = sum_over_z(keep, came)
     attended, query_gradients = unpack(rows, traded)
     grad_keys, grad_values = columns(exchange(sums, column_groups()))

time: 81.3 us -> 84.4 us (1.038)
  blocking collectives: 0 us -> 11.6 us
  starting transfers between devices: 29.8 us -> 22.6 us
    ppermute x7 -> x13, waiting for transfers between devices: 14.3 us -> 27.1 us  [permute(): return lax.ppermute(array, AXES, pairs)]
    all_to_all x0 -> x1, blocking collectives: none -> 11.6 us  [exchange(): lax.all_to_all(array, AXES, split_axis=0, concat_axis=0, axis_index_group...]
    ppermute x5 -> x0, waiting for transfers between devices: 7.38 us -> none  [the longest x4 7.38 us: trade_in_two(): return lax.ppermute(lax.ppermute(array, AXES, over), AXES, home)]
    all_to_all x2 -> x1, waiting for transfers between devices: 14.3 us -> 8.33 us  [exchange(): lax.all_to_all(array, AXES, split_axis=0, concat_axis=0, axis_index_group...]
    ppermute x5 -> x0, starting transfers between devices: 5.68 us -> none  [the longest x4 4.77 us: trade_in_two(): return lax.ppermute(lax.ppermute(array, AXES, over), AXES, home)]
    all_to_all x2 -> x1, starting transfers between devices: 12.1 us -> 6.65 us  [exchange(): lax.all_to_all(array, AXES, split_axis=0, concat_axis=0, axis_index_group...]
    ppermute x7 -> x13, starting transfers between devices: 12 us -> 16 us  [permute(): return lax.ppermute(array, AXES, pairs)]
  transfers between devices with their start and end apart: 14 -> 14, of which waited for: 6 -> 7; matrix products, arithmetic and copies ran while one was open for 0% -> 0% of each run, Pallas kernels for 10% -> 7%
where the time goes in v8:
time: 84.4 us; the launch traced here: 84.2 us
  waiting for transfers between devices  35.5 us (42%)
  starting transfers between devices  22.6 us (27%)
  Pallas kernels  13.7 us (16%)
  blocking collectives  11.6 us (14%)
    ppermute x13, waiting for transfers between devices, permute(): return lax.ppermute(array, AXES, pairs)  27.1 us
    ppermute x13, starting transfers between devices, permute(): return lax.ppermute(array, AXES, pairs)  16 us
    all_to_all x1, blocking collectives, exchange(): lax.all_to_all(array, AXES, split_axis=0, concat_axis=0, axis_index_group...  11.6 us
    all_to_all x1, waiting for transfers between devices, exchange(): lax.all_to_all(array, AXES, split_axis=0, concat_axis=0, axis_index_group...  8.33 us
    all_to_all x1, starting transfers between devices, exchange(): lax.all_to_all(array, AXES, split_axis=0, concat_axis=0, axis_index_group...  6.65 us
    pallas_call x1, Pallas kernels, both_halves(): pl.pallas_call(both_halves_kernel, out_shape=(jax.ShapeDtypeStruct((rows,...  5.47 us
    pallas_call x1, Pallas kernels, pack(): pl.pallas_call(pack_kernel, out_shape=jax.ShapeDtypeStruct(shape, keys.dt...  2.32 us
    pallas_call x1, Pallas kernels, own_half(): pl.pallas_call(own_half_kernel, out_shape=(jax.ShapeDtypeStruct((memory,...  2.28 us
  transfers between devices with their start and end apart: 14, of which 7 were waited for; matrix products, arithmetic and copies ran while one was open for 0% of the time, Pallas kernels for 7%

profile of v8, /device:TPU:32, one launch (start us, length us, event | category | flops | bytes accessed | tf_op | source)
XLA Modules:
  0.0 84.2 jit_solution(14321497409280917795)
XLA Ops:
  0.7 0.1 collective-permute-start
  0.8 1.0 %collective-permute-start.2 = (bf16[1024,256]{1,0:T(8,128)(2,1)}, bf16[1024,256]{1,0:T(8,128)(2,1)}, u32[]{:S(2)}, u32[]{:S(2)}) collective-permute-start(bf16[1024,256]{1,0:T(8,128)(2,1)} %cotangents.1), channel_id=1, source_target_pairs={{0,1},{1,129},{2,3},{3,131},{4,5},{5,133},{6,7},{7,135},{8,9},{9,1... | collective-permute-start | bytes 1572872 | tf_op jit(solution)/shard_map/ppermute | solution.py:33
  1.8 2.3 %pack.1 = bf16[8,2,128,256]{3,2,1,0:T(8,128)(2,1)} custom-call(bf16[128,4096]{1,0:T(8,128)(2,1)} %keys.1, bf16[128,4096]{1,0:T(8,128)(2,1)} %values.1), custom_call_target="tpu_custom_call" | custom-call | tf_op jit(solution)/shard_map/pack/pallas_call | solution.py:111
  4.1 6.6 %all-to-all-start = ((bf16[8,2,128,256]{3,2,1,0:T(8,128)(2,1)}), bf16[8,2,128,256]{3,2,1,0:T(8,128)(2,1)S(1)}, u32[]{:S(2)}, u32[]{:S(2)}) async-start(bf16[8,2,128,256]{3,2,1,0:T(8,128)(2,1)} %pack.1), calls=%async_computation | async-start | bytes 2097152 | tf_op jit(solution)/shard_map/all_to_all | solution.py:37
  10.8 0.5 collective-permute-start.1
  11.2 7.6 %collective-permute-done.2 = bf16[1024,256]{1,0:T(8,128)(2,1)} collective-permute-done((bf16[1024,256]{1,0:T(8,128)(2,1)}, bf16[1024,256]{1,0:T(8,128)(2,1)}, u32[]{:S(2)}, u32[]{:S(2)}) %collective-permute-start.2) | collective-permute-done | bytes 524320 | tf_op jit(solution)/shard_map/ppermute | solution.py:33
  18.8 0.0 collective-permute-start.3
  18.8 0.0 collective-permute-done.1.q_came
  18.8 2.1 %collective-permute-done.3.do_came = bf16[1024,256]{1,0:T(8,128)(2,1)S(1)} collective-permute-done((bf16[1024,256]{1,0:T(8,128)(2,1)}, bf16[1024,256]{1,0:T(8,128)(2,1)S(1)}, u32[]{:S(2)}, u32[]{:S(2)}) %collective-permute-start.3) | collective-permute-done | bytes 524320 | tf_op jit(solution)/shard_map/ppermute | solution.py:33
  20.9 0.2 select.1
  21.1 8.3 %all-to-all-done.own = bf16[8,2,128,256]{3,2,1,0:T(8,128)(2,1)S(1)} async-done(((bf16[8,2,128,256]{3,2,1,0:T(8,128)(2,1)}), bf16[8,2,128,256]{3,2,1,0:T(8,128)(2,1)S(1)}, u32[]{:S(2)}, u32[]{:S(2)}) %all-to-all-start) | async-done | bytes 1048608 | tf_op jit(solution)/shard_map/all_to_all | solution.py:37
  29.4 0.9 %collective-permute-start.4 = (bf16[8,2,128,256]{3,2,1,0:T(8,128)(2,1)S(1)}, bf16[8,2,128,256]{3,2,1,0:T(8,128)(2,1)S(1)}, u32[]{:S(2)}, u32[]{:S(2)}) collective-permute-start(bf16[8,2,128,256]{3,2,1,0:T(8,128)(2,1)S(1)} %all-to-all-done.own), channel_id=1, source_target_pairs={{0,1},{1,0},{2,3},{3,2},{4,5},{5,4},{6,7},{7,6},{8,9},{9,8},{10,11... | collective-permute-start | bytes 3145736 | tf_op jit(solution)/shard_map/ppermute | solution.py:33
  30.3 2.3 %own_half.1 = (bf16[1024,1024]{1,0:T(8,128)(2,1)S(1)}, f32[256,1024]{1,0:T(8,128)S(1)}, f32[16,1024]{1,0:T(8,128)S(1)}) custom-call(bf16[1024,256]{1,0:T(8,128)(2,1)S(1)} %get-tuple-element.31.queries, bf16[8,2,128,256]{3,2,1,0:T(8,128)(2,1)S(1)} %all-to-all-done.own), custom_call_target="tpu_custom_call" | custom-call | flops 1073741824 | bytes 2097152 | tf_op jit(solution)/shard_map/own_half/pallas_call | solution.py:348
  32.6 5.5 %both_halves.1 = (bf16[1024,256]{1,0:T(8,128)(2,1)S(1)}, bf16[2048,1024]{1,0:T(8,128)(2,1)S(1)}, bf16[8,2,128,256]{3,2,1,0:T(8,128)(2,1)S(1)}, bf16[8,2,128,256]{3,2,1,0:T(8,128)(2,1)S(1)}) custom-call(bf16[1024,256]{1,0:T(8,128)(2,1)S(1)} %get-tuple-element.31.queries, bf16[1024,256]{1,0:T(8,128)(2,1)S(1)} %get-tuple-element.32.cotangents, ...), custom_call_target="tpu_custom_call" | custom-call | flops 3221225472 | bytes 4194304 | tf_op jit(solution)/shard_map/both_halves/pallas_call | solution.py:404
  38.1 1.4 %queries_step.1.mine = bf16[2,1024,256]{2,1,0:T(8,128)(2,1)S(1)} custom-call(bf16[8,2,128,256]{3,2,1,0:T(8,128)(2,1)S(1)} %all-to-all-done.own, bf16[8,2,128,256]{3,2,1,0:T(8,128)(2,1)S(1)} %collective-permute-done.4.other, bf16[2048,1024]{1,0:T(8,128)(2,1)S(1)} %get-tuple-element.36.ds_ref, bf16[1024,256]{1,0:T(8,128)(2,1)S(1)} %get-tuple-element.37.att_ref), custom_call_target="tpu_custom_call" | custom-call | flops 1073741824 | bytes 2097152 | tf_op jit(solution)/shard_map/queries_step/pallas_call | solution.py:438
  39.5 0.4 collective-permute-start.5
  39.9 0.2 collective-permute-start.7
  40.1 2.1 %collective-permute-done.5 = bf16[2,1024,256]{2,1,0:T(8,128)(2,1)S(1)} collective-permute-done((bf16[2,1024,256]{2,1,0:T(8,128)(2,1)S(1)}, bf16[2,1024,256]{2,1,0:T(8,128)(2,1)S(1)}, u32[]{:S(2)}, u32[]{:S(2)}) %collective-permute-start.5) | collective-permute-done | bytes 1048608 | tf_op jit(solution)/shard_map/ppermute | solution.py:33
  42.2 1.9 %collective-permute-start.6 = (bf16[2,1024,256]{2,1,0:T(8,128)(2,1)S(1)}, bf16[2,1024,256]{2,1,0:T(8,128)(2,1)S(1)}, u32[]{:S(2)}, u32[]{:S(2)}) collective-permute-start(bf16[2,1024,256]{2,1,0:T(8,128)(2,1)S(1)} %collective-permute-done.5), channel_id=1, source_target_pairs={{0,128},{1,0},{2,130},{3,2},{4,132},{5,4},{6,134},{7,6},{8,136},{9... | collective-permute-start | bytes 3145736 | tf_op jit(solution)/shard_map/ppermute | solution.py:33
  44.1 0.2 core_sum.1
  44.3 2.0 %collective-permute-start.8 = (bf16[2,2,128,256]{3,2,1,0:T(8,128)(2,1)S(1)}, bf16[2,2,128,256]{3,2,1,0:T(8,128)(2,1)S(1)}, u32[]{:S(2)}, u32[]{:S(2)}) collective-permute-start(bf16[2,2,128,256]{3,2,1,0:T(8,128)(2,1)S(1)} %get-tuple-element.43), channel_id=1, source_target_pairs={{0,16},{1,17},{2,18},{3,19},{4,20},{5,21},{6,22},{7,23},{8,24},{9,... | collective-permute-start | bytes 786440 | tf_op jit(solution)/shard_map/ppermute | solution.py:33
  46.3 0.1 collective-permute-start.9
  46.4 4.4 %collective-permute-start.10 = (bf16[2,128,256]{2,1,0:T(8,128)(2,1)S(1)}, bf16[2,128,256]{2,1,0:T(8,128)(2,1)S(1)}, u32[]{:S(2)}, u32[]{:S(2)}) collective-permute-start(bf16[2,128,256]{2,1,0:T(8,128)(2,1)S(1)} %get-tuple-element.47), channel_id=1, source_target_pairs={{0,32},{1,97},{2,34},{3,99},{4,36},{5,101},{6,38},{7,103},{8,40},{... | collective-permute-start | bytes 393224 | tf_op jit(solution)/shard_map/ppermute | solution.py:33
  50.8 7.4 %collective-permute-done.10.across = bf16[2,128,256]{2,1,0:T(8,128)(2,1)S(1)} collective-permute-done((bf16[2,128,256]{2,1,0:T(8,128)(2,1)S(1)}, bf16[2,128,256]{2,1,0:T(8,128)(2,1)S(1)}, u32[]{:S(2)}, u32[]{:S(2)}) %collective-permute-start.10) | collective-permute-done | bytes 131104 | tf_op jit(solution)/shard_map/ppermute | solution.py:33
  58.2 0.1 middle_sum.1
  58.3 4.5 %collective-permute-start.11 = (bf16[2,128,256]{2,1,0:T(8,128)(2,1)S(1)}, bf16[2,128,256]{2,1,0:T(8,128)(2,1)S(1)}, u32[]{:S(2)}, u32[]{:S(2)}) collective-permute-start(bf16[2,128,256]{2,1,0:T(8,128)(2,1)S(1)} %get-tuple-element.48), channel_id=1, source_target_pairs={{0,32},{1,33},{2,34},{3,35},{4,36},{5,37},{6,38},{7,39},{8,40},{9,... | collective-permute-start | bytes 393224 | tf_op jit(solution)/shard_map/ppermute | solution.py:33
  62.8 6.0 %collective-permute-done.11.low = bf16[2,128,256]{2,1,0:T(8,128)(2,1)S(1)} collective-permute-done((bf16[2,128,256]{2,1,0:T(8,128)(2,1)S(1)}, bf16[2,128,256]{2,1,0:T(8,128)(2,1)S(1)}, u32[]{:S(2)}, u32[]{:S(2)}) %collective-permute-start.11) | collective-permute-done | bytes 131104 | tf_op jit(solution)/shard_map/ppermute | solution.py:33
  68.8 1.9 %collective-permute-done.12.high = bf16[2,128,256]{2,1,0:T(8,128)(2,1)S(1)} collective-permute-done((bf16[2,128,256]{2,1,0:T(8,128)(2,1)S(1)}, bf16[2,128,256]{2,1,0:T(8,128)(2,1)S(1)}, u32[]{:S(2)}, u32[]{:S(2)}) %collective-permute-start.12) | collective-permute-done | bytes 131104 | tf_op jit(solution)/shard_map/ppermute | solution.py:33
  70.7 0.1 last_sum.1
  70.8 11.6 %all_to_all.10.parts = bf16[16,16,256]{2,1,0:T(8,128)(2,1)S(1)} all-to-all(bf16[16,16,256]{2,1,0:T(8,128)(2,1)S(1)} %last_sum.1), channel_id=1, replica_groups={{0,128,2,130,4,132,6,134,8,136,10,138,12,140,14,142},{1,129,3,131,5,133..., dimensions={0} | all-to-all | bytes 262144 | tf_op jit(solution)/shard_map/all_to_all | solution.py:37
  82.4 0.7 columns.1
  83.1 1.1 %unpack.1 = (bf16[1024,256]{1,0:T(8,128)(2,1)}, bf16[1024,256]{1,0:T(8,128)(2,1)}) custom-call(bf16[2,1024,256]{2,1,0:T(8,128)(2,1)S(1)} %queries_step.1.mine, bf16[2,1024,256]{2,1,0:T(8,128)(2,1)S(1)} %collective-permute-done.6.came), custom_call_target="tpu_custom_call" | custom-call | tf_op jit(solution)/shard_map/unpack/pallas_call | solution.py:156
  (11 shorter events, 0.0 us)
Async XLA Ops:
  0.6 20.3 %copy-start = (bf16[1024,256]{1,0:T(8,128)(2,1)S(1)}, bf16[1024,256]{1,0:T(8,128)(2,1)}, u32[]{:S(2)}) copy-start(bf16[1024,256]{1,0:T(8,128)(2,1)} %queries.1) | copy-start | bytes 1572868
  0.6 20.3 %copy-start.1 = (bf16[1024,256]{1,0:T(8,128)(2,1)S(1)}, bf16[1024,256]{1,0:T(8,128)(2,1)}, u32[]{:S(2)}) copy-start(bf16[1024,256]{1,0:T(8,128)(2,1)} %cotangents.1) | copy-start | bytes 1572868
  0.7 10.1 %collective-permute-start = (bf16[1024,256]{1,0:T(8,128)(2,1)}, bf16[1024,256]{1,0:T(8,128)(2,1)}, u32[]{:S(2)}, u32[]{:S(2)}) collective-permute-start(bf16[1024,256]{1,0:T(8,128)(2,1)} %queries.1), channel_id=1, source_target_pairs={{0,1},{1,129},{2,3},{3,131},{4,5},{5,133},{6,7},{7,135},{8,9},{9,1... | collective-permute-start | bytes 1572872 | tf_op jit(solution)/shard_map/ppermute | solution.py:33
  0.8 18.0 %collective-permute-start.2 = (bf16[1024,256]{1,0:T(8,128)(2,1)}, bf16[1024,256]{1,0:T(8,128)(2,1)}, u32[]{:S(2)}, u32[]{:S(2)}) collective-permute-start(bf16[1024,256]{1,0:T(8,128)(2,1)} %cotangents.1), channel_id=1, source_target_pairs={{0,1},{1,129},{2,3},{3,131},{4,5},{5,133},{6,7},{7,135},{8,9},{9,1... | collective-permute-start | bytes 1572872 | tf_op jit(solution)/shard_map/ppermute | solution.py:33
  4.1 25.3 %all-to-all-start = ((bf16[8,2,128,256]{3,2,1,0:T(8,128)(2,1)}), bf16[8,2,128,256]{3,2,1,0:T(8,128)(2,1)S(1)}, u32[]{:S(2)}, u32[]{:S(2)}) async-start(bf16[8,2,128,256]{3,2,1,0:T(8,128)(2,1)} %pack.1), calls=%async_computation | async-start | bytes 2097152 | tf_op jit(solution)/shard_map/all_to_all | solution.py:37
  10.8 8.0 %collective-permute-start.1 = (bf16[1024,256]{1,0:T(8,128)(2,1)}, bf16[1024,256]{1,0:T(8,128)(2,1)S(1)}, u32[]{:S(2)}, u32[]{:S(2)}) collective-permute-start(bf16[1024,256]{1,0:T(8,128)(2,1)} %collective-permute-done), channel_id=1, source_target_pairs={{0,1},{1,0},{2,3},{3,2},{4,5},{5,4},{6,7},{7,6},{8,9},{9,8},{10,11... | collective-permute-start | bytes 1572872 | tf_op jit(solution)/shard_map/ppermute | solution.py:33
  18.8 2.1 %collective-permute-start.3 = (bf16[1024,256]{1,0:T(8,128)(2,1)}, bf16[1024,256]{1,0:T(8,128)(2,1)S(1)}, u32[]{:S(2)}, u32[]{:S(2)}) collective-permute-start(bf16[1024,256]{1,0:T(8,128)(2,1)} %collective-permute-done.2), channel_id=1, source_target_pairs={{0,1},{1,0},{2,3},{3,2},{4,5},{5,4},{6,7},{7,6},{8,9},{9,8},{10,11... | collective-permute-start | bytes 1572872 | tf_op jit(solution)/shard_map/ppermute | solution.py:33
  29.4 3.2 %collective-permute-start.4 = (bf16[8,2,128,256]{3,2,1,0:T(8,128)(2,1)S(1)}, bf16[8,2,128,256]{3,2,1,0:T(8,128)(2,1)S(1)}, u32[]{:S(2)}, u32[]{:S(2)}) collective-permute-start(bf16[8,2,128,256]{3,2,1,0:T(8,128)(2,1)S(1)} %all-to-all-done.own), channel_id=1, source_target_pairs={{0,1},{1,0},{2,3},{3,2},{4,5},{5,4},{6,7},{7,6},{8,9},{9,8},{10,11... | collective-permute-start | bytes 3145736 | tf_op jit(solution)/shard_map/ppermute | solution.py:33
  39.5 2.7 %collective-permute-start.5 = (bf16[2,1024,256]{2,1,0:T(8,128)(2,1)S(1)}, bf16[2,1024,256]{2,1,0:T(8,128)(2,1)S(1)}, u32[]{:S(2)}, u32[]{:S(2)}) collective-permute-start(bf16[2,1024,256]{2,1,0:T(8,128)(2,1)S(1)} %queries_step.1.mine), channel_id=1, source_target_pairs={{0,1},{1,0},{2,3},{3,2},{4,5},{5,4},{6,7},{7,6},{8,9},{9,8},{10,11... | collective-permute-start | bytes 3145736 | tf_op jit(solution)/shard_map/ppermute | solution.py:33
  39.9 4.2 %collective-permute-start.7 = (bf16[8,2,128,256]{3,2,1,0:T(8,128)(2,1)S(1)}, bf16[8,2,128,256]{3,2,1,0:T(8,128)(2,1)S(1)}, u32[]{:S(2)}, u32[]{:S(2)}) collective-permute-start(bf16[8,2,128,256]{3,2,1,0:T(8,128)(2,1)S(1)} %get-tuple-element.41), channel_id=1, source_target_pairs={{0,1},{1,0},{2,3},{3,2},{4,5},{5,4},{6,7},{7,6},{8,9},{9,8},{10,11... | collective-permute-start | bytes 3145736 | tf_op jit(solution)/shard_map/ppermute | solution.py:33
  42.2 40.9 %collective-permute-start.6 = (bf16[2,1024,256]{2,1,0:T(8,128)(2,1)S(1)}, bf16[2,1024,256]{2,1,0:T(8,128)(2,1)S(1)}, u32[]{:S(2)}, u32[]{:S(2)}) collective-permute-start(bf16[2,1024,256]{2,1,0:T(8,128)(2,1)S(1)} %collective-permute-done.5), channel_id=1, source_target_pairs={{0,128},{1,0},{2,130},{3,2},{4,132},{5,4},{6,134},{7,6},{8,136},{9... | collective-permute-start | bytes 3145736 | tf_op jit(solution)/shard_map/ppermute | solution.py:33
  44.3 13.9 %collective-permute-start.8 = (bf16[2,2,128,256]{3,2,1,0:T(8,128)(2,1)S(1)}, bf16[2,2,128,256]{3,2,1,0:T(8,128)(2,1)S(1)}, u32[]{:S(2)}, u32[]{:S(2)}) collective-permute-start(bf16[2,2,128,256]{3,2,1,0:T(8,128)(2,1)S(1)} %get-tuple-element.43), channel_id=1, source_target_pairs={{0,16},{1,17},{2,18},{3,19},{4,20},{5,21},{6,22},{7,23},{8,24},{9,... | collective-permute-start | bytes 786440 | tf_op jit(solution)/shard_map/ppermute | solution.py:33
  46.3 11.9 %collective-permute-start.9 = (bf16[2,2,128,256]{3,2,1,0:T(8,128)(2,1)S(1)}, bf16[2,2,128,256]{3,2,1,0:T(8,128)(2,1)S(1)}, u32[]{:S(2)}, u32[]{:S(2)}) collective-permute-start(bf16[2,2,128,256]{3,2,1,0:T(8,128)(2,1)S(1)} %get-tuple-element.44), channel_id=1, source_target_pairs={{0,112},{1,113},{2,114},{3,115},{4,116},{5,117},{6,118},{7,119},{8... | collective-permute-start | bytes 786440 | tf_op jit(solution)/shard_map/ppermute | solution.py:33
  46.4 11.8 %collective-permute-start.10 = (bf16[2,128,256]{2,1,0:T(8,128)(2,1)S(1)}, bf16[2,128,256]{2,1,0:T(8,128)(2,1)S(1)}, u32[]{:S(2)}, u32[]{:S(2)}) collective-permute-start(bf16[2,128,256]{2,1,0:T(8,128)(2,1)S(1)} %get-tuple-element.47), channel_id=1, source_target_pairs={{0,32},{1,97},{2,34},{3,99},{4,36},{5,101},{6,38},{7,103},{8,40},{... | collective-permute-start | bytes 393224 | tf_op jit(solution)/shard_map/ppermute | solution.py:33
  58.3 10.5 %collective-permute-start.11 = (bf16[2,128,256]{2,1,0:T(8,128)(2,1)S(1)}, bf16[2,128,256]{2,1,0:T(8,128)(2,1)S(1)}, u32[]{:S(2)}, u32[]{:S(2)}) collective-permute-start(bf16[2,128,256]{2,1,0:T(8,128)(2,1)S(1)} %get-tuple-element.48), channel_id=1, source_target_pairs={{0,32},{1,33},{2,34},{3,35},{4,36},{5,37},{6,38},{7,39},{8,40},{9,... | collective-permute-start | bytes 393224 | tf_op jit(solution)/shard_map/ppermute | solution.py:33
  62.8 7.9 %collective-permute-start.12 = (bf16[2,128,256]{2,1,0:T(8,128)(2,1)S(1)}, bf16[2,128,256]{2,1,0:T(8,128)(2,1)S(1)}, u32[]{:S(2)}, u32[]{:S(2)}) collective-permute-start(bf16[2,128,256]{2,1,0:T(8,128)(2,1)S(1)} %get-tuple-element.49), channel_id=1, source_target_pairs={{0,96},{1,97},{2,98},{3,99},{4,100},{5,101},{6,102},{7,103},{8,104... | collective-permute-start | bytes 393224 | tf_op jit(solution)/shard_map/ppermute | solution.py:33
